TPU v7x, 32 devices: a whole 2x2x4 slice. The times are simulated.
32 devices in a mesh: conv: 2 (over x), seq: 8 (over z, y), head: 2 (over core).
Axes of the slice: x: 2, y: 2, z: 4, core: 2. Of those that a mesh axis runs over, the one named last changes fastest.
Arguments:
- queries: bfloat16 [3072, 2048], P(('conv', 'seq'), 'head'), parts along dimension 0, may hold values from -10 to 10, as said below
- key_states: bfloat16 [3072, 512], P(('conv', 'seq'), 'head'), parts along dimension 0, may hold values from -5 to 5, as said below
- value_states: bfloat16 [3072, 512], P(('conv', 'seq'), 'head'), parts along dimension 0, may hold values from -16 to 16
- out_weight: bfloat16 [2048, 4096], P('head'), may hold values from -0.125 to 0.125
- turn_lengths: int32 [32], P('conv'), parts along dimension 0, may hold values from 1 to 959, as said below
- block_flags: int32 [16, 8], P(('conv', 'seq')), parts along dimension 0, may hold values 0 or 1
Outputs:
- pooled: float32 [32, 4096], P(('conv', 'seq'), 'head'), parts along dimension 0
There are 2 independent parts, one for each index of `conv`. A program takes and returns all parts, laid end to end along the dimension named above; an argument that names none is the same for every part. Nothing has to cross between parts.
Inputs may be any that keep to these rules, and one draw needn't show every extreme that they name: `queries`: every entry lies within the stated bounds. `key_states`: every entry lies within the stated bounds. `turn_lengths`: the lengths sum to 1536; turn 0 has one token and turn 1, the longest, has exactly 959 tokens.
All inputs are finite; a program needn't handle non-finite values. No bound on the sum of `block_flags` on one device may be relied on, other than what follows from the above.
Results may differ from a plain program's by a relative error of at most 0.0035.
Values may be sent and summed in bfloat16 or wider, within the bound.
No kernel may reach another device: no remote copies, remote signals or barrier semaphores. Data moves between devices by JAX's collectives and lax.ppermute only.
A program may use at most 128 MiB of HBM per device.

v0:
```python
import functools
import math

import jax
import jax.numpy as jnp
from jax import lax
from jax.experimental import pallas as pl
from jax.experimental.pallas import tpu as pltpu
from jax.sharding import PartitionSpec as P

HD = 128

big_negative = -1e30
log_two_e = 1.4426950408889634

big_limit = 45 * 1024 * 1024
small_cost = pl.CostEstimate(flops=1024, bytes_accessed=1024, transcendentals=0)

in_vmem = pl.BlockSpec(memory_space=pltpu.VMEM)
in_smem = pl.BlockSpec(memory_space=pltpu.SMEM)
anywhere = pl.BlockSpec(memory_space=pl.ANY)


def place(across):
    index = lax.axis_index("seq")
    return index // across, lax.rem(index, across)


def block_at(z, y, e, across):
    return z * across + lax.rem(y - e + across, across)


def call(kernel, out_shape, **settings):
    limit = settings.pop("limit", 16 * 1024 * 1024)
    return pl.pallas_call(
        kernel,
        out_shape=out_shape,
        out_specs=jax.tree.map(lambda _: in_vmem, out_shape),
        compiler_params=pltpu.CompilerParams(vmem_limit_bytes=limit),
        cost_estimate=small_cost,
        **settings,
    )


def pick(rows, number, parts):
    width = rows.shape[1] // parts
    picked = rows[:, :width]
    for part in range(1, parts):
        picked = jnp.where(number == part, rows[:, part * width : (part + 1) * width], picked)
    return picked


def pair(keys, values):
    which = lax.broadcasted_iota(jnp.int32, (2,) + keys.shape, 0)
    return jnp.where(which == 0, keys[None], values[None])


def join_kernel(*refs):
    *parts, _, out_ref = refs
    for e, part in enumerate(parts):
        out_ref[e] = part[...]


def join(parts, after):
    shape = jax.ShapeDtypeStruct((len(parts),) + parts[0].shape, parts[0].dtype)
    return call(join_kernel, shape, in_specs=[in_vmem] * len(parts) + [anywhere])(*parts, after)


def rows_update(turned_ref, rows_refs, switches, state, first):
    top, total_sum, totals = state
    across, _, columns = turned_ref.shape
    rows = rows_refs[0].shape[2]
    count = across * len(rows_refs)
    factor = log_two_e / math.sqrt(HD)
    keys = [kv_ref[:, 0].reshape(across * rows, HD) for kv_ref in rows_refs]
    values = [kv_ref[:, 1].reshape(across * rows, HD).T for kv_ref in rows_refs]
    logits = [
        [jnp.dot(part, turned_ref[e], preferred_element_type=jnp.float32) for part in keys]
        for e in range(across)
    ]
    if first:
        key_pos = lax.broadcasted_iota(jnp.int32, (rows, 1), 0)
        column = lax.broadcasted_iota(jnp.int32, (1, columns), 1)
        causal = key_pos <= lax.rem(column, rows)
    for e in range(across):
        blocks = [
            logits[e][b // across][b % across * rows : (b % across + 1) * rows] for b in range(count)
        ]
        if first:
            blocks[e] = jnp.where(causal, blocks[e], big_negative)
        new_top = None if first else top[e]
        for b in range(count):
            block_top = jnp.ceil(jnp.max(blocks[b], axis=0, keepdims=True) * factor)
            if switches[e][b] is not None:
                block_top = jnp.where(switches[e][b], block_top, big_negative)
            new_top = block_top if new_top is None else jnp.maximum(new_top, block_top)
        weights, block_sum = [], None
        for b in range(count):
            against = new_top
            if switches[e][b] is not None:
                against = jnp.where(switches[e][b], new_top, -big_negative)
            weights.append(jnp.exp2(blocks[b] * factor - against))
            part = jnp.sum(weights[b], axis=0, keepdims=True)
            block_sum = part if block_sum is None else block_sum + part
        update = None
        for i, part in enumerate(values):
            mine = weights[i * across : (i + 1) * across]
            mine = jnp.concatenate([w.astype(jnp.bfloat16) for w in mine], axis=0)
            part = jnp.dot(part, mine, preferred_element_type=jnp.float32)
            update = part if update is None else update + part
        if not first:
            rescale = jnp.exp2(top[e] - new_top)
            block_sum = total_sum[e] * rescale + block_sum
            update = totals[e] * rescale + update
        top[e] = new_top
        total_sum[e] = block_sum
        totals[e] = update


def switch_of(flags_ref, e, owner, columns, allowed=None):
    flag = flags_ref[e, pl.ds(jnp.maximum(owner, 0), 1), :]
    if allowed is not None:
        flag = flag * jnp.where(allowed, 1.0, 0.0)
    return jnp.concatenate([flag] * (columns // HD), axis=1) > 0.5


def weight_piece(weight_ref, out_ref, start, sem):
    return pltpu.make_async_copy(weight_ref.at[start : start + out_ref.shape[0]], out_ref, sem)


def first_kernel(across, turns, meta_ref, own_flags_ref, *refs):
    queries, refs = refs[:across], refs[across:]
    kv_ref, weight_ref, turned_ref, flags_ref, member_ref, inverse_ref, weight_out = refs[:7]
    state, rows_ref, copied = refs[7:10], refs[10], refs[11]
    weight_copy = weight_piece(weight_ref, weight_out, 0, copied)
    weight_copy.start()
    z, y = place(across)
    q_rows = kv_ref.shape[2]
    repeat = queries[0].shape[1] // HD
    columns = repeat * q_rows
    for e in range(across):
        for r in range(repeat):
            turned_ref[e, :, r * q_rows : (r + 1) * q_rows] = queries[e][
                0:q_rows, r * HD : (r + 1) * HD
            ].T
    flags_ref[0] = own_flags_ref[...]
    for e in range(1, across):
        flags_ref[e] = queries[e][q_rows:, 0:HD].astype(jnp.float32)
    owners = [block_at(z, y, e, across) for e in range(across)]
    switches = [
        [
            None if e == b else switch_of(flags_ref, e, owners[b], columns, owners[b] < owners[e])
            for b in range(across)
        ]
        for e in range(across)
    ]
    rows_update(turned_ref, [kv_ref], switches, state, True)

    column = lax.broadcasted_iota(jnp.int32, (1, columns), 1)
    for e in range(across):
        position = lax.rem(column, q_rows) + owners[e] * q_rows
        start = jnp.int32(0)
        for t in range(turns):
            length = meta_ref[t]
            inside = (position >= start) & (position < start + length)
            rows_ref[t : t + 1, :] = jnp.where(inside, 1.0, 0.0)
            if e == 0:
                count = jnp.full((1, HD), length, jnp.int32).astype(jnp.float32)
                inverse_ref[t : t + 1, :] = 1.0 / count
            start = start + length
        for r in range(repeat):
            mine = (column >= r * q_rows) & (column < (r + 1) * q_rows)
            member_ref[e, r * turns : (r + 1) * turns, :] = jnp.where(
                mine, rows_ref[...], 0.0
            ).astype(jnp.bfloat16)
    weight_copy.wait()


def attend_first(across, turns, meta, flags, queries, rows, weight, piece):
    q_rows = rows.shape[2]
    repeat = queries[0].shape[1] // HD
    columns = repeat * q_rows
    f32, b16 = jnp.float32, jnp.bfloat16
    return call(
        functools.partial(first_kernel, across, turns),
        [
            jax.ShapeDtypeStruct((across, HD, columns), b16),
            jax.ShapeDtypeStruct((across,) + flags.shape, f32),
            jax.ShapeDtypeStruct((across, repeat * turns, columns), b16),
            jax.ShapeDtypeStruct((turns, HD), f32),
            jax.ShapeDtypeStruct((piece, weight.shape[1]), weight.dtype),
            jax.ShapeDtypeStruct((across, 1, columns), f32),
            jax.ShapeDtypeStruct((across, 1, columns), f32),
            jax.ShapeDtypeStruct((across, HD, columns), f32),
        ],
        in_specs=[in_smem] + [in_vmem] * (across + 2) + [anywhere],
        scratch_shapes=[pltpu.VMEM((turns, columns), f32), pltpu.SemaphoreType.DMA(())],
        limit=big_limit,
    )(meta, flags, *queries, rows, weight)


def next_kernel(across, distances, turns, last, weight_at, flags_ref, turned_ref, *refs):
    below_count = len(distances)
    below, state, refs = refs[:below_count], refs[below_count : below_count + 3], refs[below_count + 3 :]
    if weight_at is not None:
        weight_ref, weight_out, copied = refs[0], refs[-2], refs[-1]
        refs = refs[1:-2]
        weight_copy = weight_piece(weight_ref, weight_out, weight_at, copied)
        weight_copy.start()
    z, y = place(across)
    columns = turned_ref.shape[2]

    def update(rows, from_distances):
        switches = [
            [
                switch_of(flags_ref, e, block_at(z - distance, y, b, across), columns)
                for distance in from_distances
                for b in range(across)
            ]
            for e in range(across)
        ]
        rows_update(turned_ref, rows, switches, state, False)

    for number, distance in enumerate(distances, 1):
        here = (z >= distance) if number == len(distances) else (z == distance)
        pl.when(here)(functools.partial(update, below[:number], distances[:number]))

    if weight_at is not None:
        weight_copy.wait()
    if last:
        member_ref, inverse_ref, out_ref = refs
        rows = out_ref.shape[1]
        pooled = None
        for e in range(across):
            attended = (state[2][e] / state[1][e]).astype(jnp.bfloat16)
            part = lax.dot_general(
                member_ref[e],
                attended,
                (((1,), (1,)), ((), ())),
                preferred_element_type=jnp.float32,
            )
            pooled = part if pooled is None else pooled + part
        for r in range(pooled.shape[0] // turns):
            mean = pooled[r * turns : (r + 1) * turns] * inverse_ref[...]
            for s in range(out_ref.shape[0]):
                out_ref[s, :, r * HD : (r + 1) * HD] = mean[s * rows : (s + 1) * rows]


def attend_next(across, distances, turns, turned, flags, below, state, pool, out_piece, weight, at, piece):
    last = pool is not None
    args = [flags, turned, *below, *state]
    in_specs = [in_vmem] * len(args)
    aliases, scratch = {}, []
    if at is not None:
        args.append(weight)
        in_specs.append(anywhere)
        scratch = [pltpu.SemaphoreType.DMA(())]
    if last:
        args += list(pool)
        in_specs += [in_vmem] * len(pool)
        out_shape = [jax.ShapeDtypeStruct(out_piece, jnp.float32)]
    else:
        out_shape = [jax.ShapeDtypeStruct(part.shape, part.dtype) for part in state]
        aliases = {2 + len(below) + i: i for i in range(len(state))}
    if at is not None:
        out_shape.append(jax.ShapeDtypeStruct((piece, weight.shape[1]), weight.dtype))
    return call(
        functools.partial(next_kernel, across, distances, turns, last, at),
        out_shape,
        in_specs=in_specs,
        scratch_shapes=scratch,
        input_output_aliases=aliases,
        limit=big_limit if at is not None else 16 * 1024 * 1024,
    )(*args)


def project_kernel(across, other, parts_ref, *refs):
    weights, out_ref = refs[:-1], refs[-1]
    side = lax.axis_index("head")
    if other:
        side = 1 - side
    groups = []
    for y in range(across):
        total = parts_ref[y]
        for s in range(y + across, parts_ref.shape[0], across):
            total = total + parts_ref[s]
        groups.append(total)
    total = jnp.concatenate(groups, axis=1)
    rows = total.shape[0]
    high = total.astype(jnp.bfloat16)
    low = (total - high.astype(jnp.float32)).astype(jnp.bfloat16)
    both = jnp.concatenate([high, low], axis=0)
    half = out_ref.shape[1]
    step = math.gcd(half, 512)
    for c in range(half // step):
        start = pl.multiple_of(side * half + c * step, step)
        product, at = None, 0
        for weight_ref in weights:
            depth = weight_ref.shape[0]
            part = jnp.dot(
                both[:, at : at + depth],
                weight_ref[:, pl.ds(start, step)],
                preferred_element_type=jnp.float32,
            )
            product = part if product is None else product + part
            at += depth
        out_ref[:, c * step : (c + 1) * step] = product[:rows] + product[rows:]


def project(across, other, parts, weights):
    return call(
        functools.partial(project_kernel, across, other),
        jax.ShapeDtypeStruct((parts.shape[1], weights[0].shape[1] // 2), jnp.float32),
        in_specs=[in_vmem] * (1 + len(weights)),
    )(parts, *weights)


def on_device(count, queries, key_states, value_states, out_weight, turn_lengths, block_flags):
    across = key_states.shape[1] // HD
    down = count // across
    turns = turn_lengths.shape[0]

    def over(rows, shift):
        pairs = [(i, i - i % across + (i + shift) % across) for i in range(count)]
        return lax.ppermute(rows, "seq", pairs)

    def up(rows, distance, lowest=0):
        step = distance * across
        pairs = [(i, i + step) for i in range(lowest * across, count - step)]
        return lax.ppermute(rows, "seq", pairs)

    _, y = place(across)
    heads = []
    for shift in range(across):
        at = lax.rem(y + shift, across)
        heads.append(pair(pick(key_states, at, across), pick(value_states, at, across)))
    meta = lax.optimization_barrier(jnp.concatenate([turn_lengths, block_flags[0]]))
    padded = -(-count // 16) * 16
    flags = jnp.pad(meta[turns:], (0, padded - count))[:, None]
    groups = [pick(queries, lax.rem(y + shift, across), across) for shift in range(across)]
    sent = []
    for group in groups[1:]:
        under = jnp.broadcast_to(flags, (padded, group.shape[1])).astype(group.dtype)
        sent.append(jnp.concatenate([group, under], axis=0))
    flags = jnp.broadcast_to(flags, (padded, HD)).astype(jnp.float32)
    others = [over(group, shift) for shift, group in enumerate(sent, 1)]
    rows = join([heads[0]] + [over(heads[shift], shift) for shift in range(1, across)], sent[0])
    below = [rows, up(rows, 1)] + [None] * (down - 2)
    for distance in range(3, down):
        below[distance] = up(rows, distance)
    below[1], *others = lax.optimization_barrier((below[1], *others))
    if down > 2:
        below[2] = up(below[1], 1, 1)
    depth = out_weight.shape[0]
    pieces = [4 * depth // 8, 2 * depth // 8, 2 * depth // 8]
    turned, flags, member, inverse, weight, *state = attend_first(
        across, turns, meta, flags, [groups[0], *others], rows, out_weight, pieces[0]
    )
    weights = [weight]
    out_piece = (count, turns // count, queries.shape[1] // across)
    stages = [[1]] + [list(range(d, min(d + 2, down))) for d in range(2, down, 2)]
    for number, distances in enumerate(stages):
        last = number == len(stages) - 1
        with_weight = last or number == 0
        state = attend_next(
            across,
            distances,
            turns,
            turned,
            flags,
            [below[distance] for distance in distances],
            state,
            (member, inverse) if last else None,
            out_piece,
            out_weight,
            sum(pieces[: len(weights)]) if with_weight else None,
            pieces[len(weights)] if with_weight else None,
        )
        if with_weight:
            *state, weight = state
            weights.append(weight)
    parts = lax.all_to_all(state[0], "seq", split_axis=0, concat_axis=0, tiled=True)
    theirs = project(across, True, parts, weights)
    theirs = lax.ppermute(theirs, "head", [(0, 1), (1, 0)])
    return project(across, False, parts, weights) + theirs


def solution(mesh):
    in_specs = (
        P(("conv", "seq"), "head"),
        P(("conv", "seq"), "head"),
        P(("conv", "seq"), "head"),
        P("head", None),
        P("conv"),
        P(("conv", "seq"), None),
    )
    out_specs = P(("conv", "seq"), "head")
    return jax.shard_map(
        functools.partial(on_device, mesh.shape["seq"]),
        mesh=mesh,
        in_specs=in_specs,
        out_specs=out_specs,
        check_vma=False,
    )
```

profile of v0, /device:TPU:0, one launch (start us, length us, event | category | flops | bytes accessed | tf_op | source)
XLA Modules:
  0.0 43.2 jit_solution(5469759144594223397)
XLA Ops:
  0.0 0.9 %broadcast_select_fusion.4 = (bf16[192,128]{1,0:T(8,128)(2,1)S(1)}, bf16[192,128]{1,0:T(8,128)(2,1)S(1)}, bf16[192,128]{1,0:T(8,128)(2,1)S(1)}, bf16[192,128]{1,0:T(8,128)(2,1)S(1)}) fusion(pred[]{:T(512)S(6)} %eq.19, bf16[192,256]{1,0:T(8,128)(2,1)} %param.8, pred[]{:T(512)S(6)} %eq.17, bf16[192,256]{1,0:T(8,128)(2,1)} %param.7), kind=kLoop, calls=%fused_computation.5 | loop fusion | flops 98304 | bytes 393218 | tf_op jit(solution)/shard_map/jit(_where)/select_n | solution.py:49
  0.9 0.1 broadcast_select_fusion.2
  1.0 3.0 %collective-permute-start = (bf16[2,192,128]{2,1,0:T(8,128)(2,1)S(1)}, bf16[2,192,128]{2,1,0:T(8,128)(2,1)S(1)}, u32[]{:S(2)}, u32[]{:S(2)}) collective-permute-start(bf16[2,192,128]{2,1,0:T(8,128)(2,1)S(1)} %get-tuple-element.45), channel_id=1, source_target_pairs={{0,2},{2,0},{4,6},{6,4},{8,10},{10,8},{12,14},{14,12},{1,3},{3,1},... | collective-permute-start | bytes 294920 | tf_op jit(solution)/shard_map/ppermute | solution.py:325
  4.0 0.7 %pad_add_fusion.meta_ref = s32[24]{0:T(128)S(1)} fusion(s32[8]{0:T(128)} %bitcast.1, s32[16]{0:T(128)} %param.10), kind=kLoop, calls=%fused_computation.9 | loop fusion | flops 24 | bytes 192 | tf_op jit(solution)/shard_map/concatenate | solution.py:337
  4.8 0.1 slice.27
  4.8 1.1 %broadcast_select_fusion = (bf16[192,512]{1,0:T(8,128)(2,1)S(1)}, bf16[192,512]{1,0:T(8,128)(2,1)S(1)}) fusion(pred[]{:T(512)S(6)} %eq.19, bf16[192,1024]{1,0:T(8,128)(2,1)} %param.6, pred[]{:T(512)S(6)} %eq.17), kind=kLoop, calls=%fused_computation.1 | loop fusion | flops 196608 | bytes 786434 | tf_op jit(solution)/shard_map/jit(_where)/select_n | solution.py:49
  5.9 0.1 pad.6.clone
  6.0 0.1 pad_maximum_fusion.refs_2_
  6.1 0.1 collective-permute-start.2
  6.2 0.6 %collective-permute-done.refs_1_ = bf16[2,192,128]{2,1,0:T(8,128)(2,1)S(1)} collective-permute-done((bf16[2,192,128]{2,1,0:T(8,128)(2,1)S(1)}, bf16[2,192,128]{2,1,0:T(8,128)(2,1)S(1)}, u32[]{:S(2)}, u32[]{:S(2)}) %collective-permute-start) | collective-permute-done | bytes 98336 | tf_op jit(solution)/shard_map/ppermute | solution.py:325
  6.8 3.8 %collective-permute-start.1 = (bf16[2,2,192,128]{3,2,1,0:T(8,128)(2,1)S(1)}, bf16[2,2,192,128]{3,2,1,0:T(8,128)(2,1)S(1)}, u32[]{:S(2)}, u32[]{:S(2)}) collective-permute-start(bf16[2,2,192,128]{3,2,1,0:T(8,128)(2,1)S(1)} %shard_map.64.refs_2_), channel_id=1, source_target_pairs={{0,4},{2,6},{4,8},{6,10},{8,12},{10,14},{1,5},{3,7},{5,9},{7,11},{... | collective-permute-start | bytes 589832 | tf_op jit(solution)/shard_map/ppermute | solution.py:330
  10.6 3.3 %collective-permute-start.4 = (bf16[2,2,192,128]{3,2,1,0:T(8,128)(2,1)S(1)}, bf16[2,2,192,128]{3,2,1,0:T(8,128)(2,1)S(1)}, u32[]{:S(2)}, u32[]{:S(2)}) collective-permute-start(bf16[2,2,192,128]{3,2,1,0:T(8,128)(2,1)S(1)} %shard_map.64.refs_2_), channel_id=1, source_target_pairs={{0,12},{2,14},{1,13},{3,15},{16,28},{18,30},{17,29},{19,31}} | collective-permute-start | bytes 589832 | tf_op jit(solution)/shard_map/ppermute | solution.py:330
  14.0 0.0 collective-permute-done.2.refs_1_
  14.0 0.7 %collective-permute-done.1.refs_0_ = bf16[2,2,192,128]{3,2,1,0:T(8,128)(2,1)S(1)} collective-permute-done((bf16[2,2,192,128]{3,2,1,0:T(8,128)(2,1)S(1)}, bf16[2,2,192,128]{3,2,1,0:T(8,128)(2,1)S(1)}, u32[]{:S(2)}, u32[]{:S(2)}) %collective-permute-start.1) | collective-permute-done | bytes 196640 | tf_op jit(solution)/shard_map/ppermute | solution.py:330
  14.7 0.7 %collective-permute-start.3 = (bf16[2,2,192,128]{3,2,1,0:T(8,128)(2,1)S(1)}, bf16[2,2,192,128]{3,2,1,0:T(8,128)(2,1)S(1)}, u32[]{:S(2)}, u32[]{:S(2)}) collective-permute-start(bf16[2,2,192,128]{3,2,1,0:T(8,128)(2,1)S(1)} %collective-permute-done.1.refs_0_), channel_id=1, source_target_pairs={{4,8},{6,10},{8,12},{10,14},{5,9},{7,11},{9,13},{11,15},{20,24},{2... | collective-permute-start | bytes 589832 | tf_op jit(solution)/shard_map/ppermute | solution.py:330
  15.4 0.1 broadcast_in_dim.41.own_flags_ref
  15.4 3.4 %shard_map.65 = (bf16[2,128,768]{2,1,0:T(8,128)(2,1)S(1)}, f32[2,16,128]{2,1,0:T(8,128)S(1)}, bf16[2,64,768]{2,1,0:T(8,128)(2,1)S(1)}, f32[16,128]{1,0:T(8,128)S...) custom-call(s32[24]{0:T(128)S(1)} %pad_add_fusion.meta_ref, ...), custom_call_target="tpu_custom_call" | custom-call | flops 1024 | bytes 1024 | tf_op jit(solution)/shard_map/pallas_call | solution.py:184
  18.8 1.6 %shard_map.66 = (f32[2,1,768]{2,1,0:T(1,128)S(1)}, f32[2,1,768]{2,1,0:T(1,128)S(1)}, f32[2,128,768]{2,1,0:T(8,128)S(1)}, bf16[256,4096]{1,0:T(8,128)(2,1)S(1)}) custom-call(f32[2,16,128]{2,1,0:T(8,128)S(1)} %get-tuple-element.22.flags_ref, ...), custom_call_target="tpu_custom_call", output_to_operand_aliasing={{0}: (3, {}), {1}: (4, {}), {2}: (5, {})} | custom-call | flops 1024 | bytes 1024 | tf_op jit(solution)/shard_map/pallas_call | solution.py:267
  20.5 0.0 collective-permute-done.4.refs_1_
  20.5 0.0 collective-permute-done.3.refs_0_
  20.5 1.9 %shard_map.67 = (f32[8,2,512]{2,1,0:T(2,128)S(1)}, bf16[256,4096]{1,0:T(8,128)(2,1)S(1)}) custom-call(f32[2,16,128]{2,1,0:T(8,128)S(1)} %get-tuple-element.22.flags_ref, bf16[2,128,768]{2,1,0:T(8,128)(2,1)S(1)} %get-tuple-element.23.turned_ref, bf16[2,2,192,128]{3,2,1,0:T(8,128)(2,1)S(1)} %collective-permute-done.3.refs_0_, ...), custom_call_target="tpu_custom_call" | custom-call | flops 1024 | bytes 1024 | tf_op jit(solution)/shard_map/pallas_call | solution.py:267
  22.4 18.4 %all_to_all.5.parts_ref = f32[8,2,512]{2,1,0:T(2,128)S(1)} all-to-all(f32[8,2,512]{2,1,0:T(2,128)S(1)} %get-tuple-element.33), channel_id=1, replica_groups=mesh['conv'=2,'seq'=8,'head'=2] {'seq'}, dimensions={0} | all-to-all | bytes 65536 | tf_op jit(solution)/shard_map/all_to_all | solution.py:382
  40.7 0.7 %shard_map.69 = f32[2,2048]{1,0:T(2,128)S(1)} custom-call(f32[8,2,512]{2,1,0:T(2,128)S(1)} %all_to_all.5.parts_ref, bf16[512,4096]{1,0:T(8,128)(2,1)S(1)} %get-tuple-element.34.refs_0_, bf16[256,4096]{1,0:T(8,128)(2,1)S(1)} %get-tuple-element.35.refs_1_, bf16[256,4096]{1,0:T(8,128)(2,1)S(1)} %get-tuple-element.36.refs_2_), custom_call_target="tpu_custom_call" | custom-call | flops 1024 | bytes 1024 | tf_op jit(solution)/shard_map/pallas_call | solution.py:311
  41.4 0.0 collective-permute-start.5
  41.4 0.7 %shard_map.68 = f32[2,2048]{1,0:T(2,128)S(1)} custom-call(f32[8,2,512]{2,1,0:T(2,128)S(1)} %all_to_all.5.parts_ref, bf16[512,4096]{1,0:T(8,128)(2,1)S(1)} %get-tuple-element.34.refs_0_, bf16[256,4096]{1,0:T(8,128)(2,1)S(1)} %get-tuple-element.35.refs_1_, bf16[256,4096]{1,0:T(8,128)(2,1)S(1)} %get-tuple-element.36.refs_2_), custom_call_target="tpu_custom_call" | custom-call | flops 1024 | bytes 1024 | tf_op jit(solution)/shard_map/pallas_call | solution.py:311
  42.1 0.5 %collective-permute-done.5 = f32[2,2048]{1,0:T(2,128)S(1)} collective-permute-done((f32[2,2048]{1,0:T(2,128)S(1)}, f32[2,2048]{1,0:T(2,128)S(1)}, u32[]{:S(2)}, u32[]{:S(2)}) %collective-permute-start.5) | collective-permute-done | bytes 16416 | tf_op jit(solution)/shard_map/ppermute | solution.py:384
  42.6 0.6 %add.10 = f32[2,2048]{1,0:T(2,128)} add(f32[2,2048]{1,0:T(2,128)S(1)} %shard_map.68, f32[2,2048]{1,0:T(2,128)S(1)} %collective-permute-done.5) | non-fusion elementwise | flops 4096 | bytes 49152 | tf_op jit(solution)/shard_map/add | solution.py:385
  (3 shorter events, 0.0 us)
Async XLA Ops:
  1.0 5.8 %collective-permute-start = (bf16[2,192,128]{2,1,0:T(8,128)(2,1)S(1)}, bf16[2,192,128]{2,1,0:T(8,128)(2,1)S(1)}, u32[]{:S(2)}, u32[]{:S(2)}) collective-permute-start(bf16[2,192,128]{2,1,0:T(8,128)(2,1)S(1)} %get-tuple-element.45), channel_id=1, source_target_pairs={{0,2},{2,0},{4,6},{6,4},{8,10},{10,8},{12,14},{14,12},{1,3},{3,1},... | collective-permute-start | bytes 294920 | tf_op jit(solution)/shard_map/ppermute | solution.py:325
  6.1 7.9 %collective-permute-start.2 = (bf16[208,512]{1,0:T(8,128)(2,1)S(1)}, bf16[208,512]{1,0:T(8,128)(2,1)S(1)}, u32[]{:S(2)}, u32[]{:S(2)}) collective-permute-start(bf16[208,512]{1,0:T(8,128)(2,1)S(1)} %pad_maximum_fusion.refs_2_), channel_id=1, source_target_pairs={{0,2},{2,0},{4,6},{6,4},{8,10},{10,8},{12,14},{14,12},{1,3},{3,1},... | collective-permute-start | bytes 638984 | tf_op jit(solution)/shard_map/ppermute | solution.py:325
  6.8 7.9 %collective-permute-start.1 = (bf16[2,2,192,128]{3,2,1,0:T(8,128)(2,1)S(1)}, bf16[2,2,192,128]{3,2,1,0:T(8,128)(2,1)S(1)}, u32[]{:S(2)}, u32[]{:S(2)}) collective-permute-start(bf16[2,2,192,128]{3,2,1,0:T(8,128)(2,1)S(1)} %shard_map.64.refs_2_), channel_id=1, source_target_pairs={{0,4},{2,6},{4,8},{6,10},{8,12},{10,14},{1,5},{3,7},{5,9},{7,11},{... | collective-permute-start | bytes 589832 | tf_op jit(solution)/shard_map/ppermute | solution.py:330
  10.6 9.8 %collective-permute-start.4 = (bf16[2,2,192,128]{3,2,1,0:T(8,128)(2,1)S(1)}, bf16[2,2,192,128]{3,2,1,0:T(8,128)(2,1)S(1)}, u32[]{:S(2)}, u32[]{:S(2)}) collective-permute-start(bf16[2,2,192,128]{3,2,1,0:T(8,128)(2,1)S(1)} %shard_map.64.refs_2_), channel_id=1, source_target_pairs={{0,12},{2,14},{1,13},{3,15},{16,28},{18,30},{17,29},{19,31}} | collective-permute-start | bytes 589832 | tf_op jit(solution)/shard_map/ppermute | solution.py:330
  14.7 5.8 %collective-permute-start.3 = (bf16[2,2,192,128]{3,2,1,0:T(8,128)(2,1)S(1)}, bf16[2,2,192,128]{3,2,1,0:T(8,128)(2,1)S(1)}, u32[]{:S(2)}, u32[]{:S(2)}) collective-permute-start(bf16[2,2,192,128]{3,2,1,0:T(8,128)(2,1)S(1)} %collective-permute-done.1.refs_0_), channel_id=1, source_target_pairs={{4,8},{6,10},{8,12},{10,14},{5,9},{7,11},{9,13},{11,15},{20,24},{2... | collective-permute-start | bytes 589832 | tf_op jit(solution)/shard_map/ppermute | solution.py:330
  41.4 1.2 %collective-permute-start.5 = (f32[2,2048]{1,0:T(2,128)S(1)}, f32[2,2048]{1,0:T(2,128)S(1)}, u32[]{:S(2)}, u32[]{:S(2)}) collective-permute-start(f32[2,2048]{1,0:T(2,128)S(1)} %shard_map.69), channel_id=1, source_target_pairs={{0,1},{1,0},{2,3},{3,2},{4,5},{5,4},{6,7},{7,6},{8,9},{9,8},{10,11... | collective-permute-start | bytes 49160 | tf_op jit(solution)/shard_map/ppermute | solution.py:384
where the time goes:
time: 43.6 us; the launch traced here: 43.2 us
  blocking collectives  18.4 us (42%)
  starting transfers between devices  10.9 us (25%)
  Pallas kernels  8.24 us (19%)
  other arithmetic  3.5 us (8%)
  waiting for transfers between devices  1.9 us (4%)
    all_to_all x1, blocking collectives, on_device(): lax.all_to_all(state[0], 'seq', split_axis=0, concat_axis=0, tiled=True)  18.4 us
    ppermute x3, starting transfers between devices, up(): return lax.ppermute(rows, 'seq', pairs)  7.77 us
    pallas_call x2, Pallas kernels, attend_next(): call(functools.partial(next_kernel, across, distances, turns, last, at),...  3.49 us
    pallas_call x1, Pallas kernels, attend_first(): call(functools.partial(first_kernel, across, turns), [jax.ShapeDtypeStruc...  3.4 us
    ppermute x2, starting transfers between devices, over(): return lax.ppermute(rows, 'seq', pairs)  3.11 us
    select_n x2, other arithmetic, pick(): jnp.where(number == part, rows[:, part * width:(part + 1) * width], picked)  1.94 us
    pallas_call x2, Pallas kernels, project(): call(functools.partial(project_kernel, across, other), jax.ShapeDtypeStru...  1.34 us
  transfers between devices with their start and end apart: 6, of which 3 were waited for; matrix products, arithmetic and copies ran while one was open for 5% of the time, Pallas kernels for 13%

commit v1 on v0

--- a/solution.py
+++ b/solution.py
@@ -348,7 +348,6 @@
     below = [rows, up(rows, 1)] + [None] * (down - 2)
     for distance in range(3, down):
         below[distance] = up(rows, distance)
-    below[1], *others = lax.optimization_barrier((below[1], *others))
     if down > 2:
         below[2] = up(below[1], 1, 1)
     depth = out_weight.shape[0]

time: 43.6 us -> 43.6 us (level)
  starting transfers between devices: 10.9 us -> 12.4 us
  blocking collectives: 18.4 us -> 17.2 us
    ppermute x2, starting transfers between devices: 3.11 us -> 4.62 us  [over(): return lax.ppermute(rows, 'seq', pairs)]
    all_to_all x1, blocking collectives: 18.4 us -> 17.2 us  [on_device(): lax.all_to_all(state[0], 'seq', split_axis=0, concat_axis=0, tiled=True)]
    ppermute x3, waiting for transfers between devices: 0.73 us -> 0.01 us  [up(): return lax.ppermute(rows, 'seq', pairs)]
where the time goes in v1:
time: 43.6 us; the launch traced here: 43.2 us
  blocking collectives  17.2 us (39%)
  starting transfers between devices  12.4 us (28%)
  Pallas kernels  8.24 us (19%)
  other arithmetic  3.5 us (8%)
  waiting for transfers between devices  1.58 us (4%)
    all_to_all x1, blocking collectives, on_device(): lax.all_to_all(state[0], 'seq', split_axis=0, concat_axis=0, tiled=True)  17.2 us
    ppermute x3, starting transfers between devices, up(): return lax.ppermute(rows, 'seq', pairs)  7.77 us
    ppermute x2, starting transfers between devices, over(): return lax.ppermute(rows, 'seq', pairs)  4.62 us
    pallas_call x2, Pallas kernels, attend_next(): call(functools.partial(next_kernel, across, distances, turns, last, at),...  3.49 us
    pallas_call x1, Pallas kernels, attend_first(): call(functools.partial(first_kernel, across, turns), [jax.ShapeDtypeStruc...  3.4 us
    select_n x2, other arithmetic, pick(): jnp.where(number == part, rows[:, part * width:(part + 1) * width], picked)  1.94 us
    pallas_call x2, Pallas kernels, project(): call(functools.partial(project_kernel, across, other), jax.ShapeDtypeStru...  1.34 us
    ppermute x2, waiting for transfers between devices, over(): return lax.ppermute(rows, 'seq', pairs)  1.05 us
  transfers between devices with their start and end apart: 6, of which 3 were waited for; matrix products, arithmetic and copies ran while one was open for 5% of the time, Pallas kernels for 13%

profile of v1, /device:TPU:0, one launch (start us, length us, event | category | flops | bytes accessed | tf_op | source)
XLA Modules:
  0.0 43.2 jit_solution(14882569913748695109)
XLA Ops:
  0.0 0.9 %broadcast_select_fusion.4 = (bf16[192,128]{1,0:T(8,128)(2,1)S(1)}, bf16[192,128]{1,0:T(8,128)(2,1)S(1)}, bf16[192,128]{1,0:T(8,128)(2,1)S(1)}, bf16[192,128]{1,0:T(8,128)(2,1)S(1)}) fusion(pred[]{:T(512)S(6)} %eq.18, bf16[192,256]{1,0:T(8,128)(2,1)} %param.8, pred[]{:T(512)S(6)} %eq.17, bf16[192,256]{1,0:T(8,128)(2,1)} %param.7), kind=kLoop, calls=%fused_computation.5 | loop fusion | flops 98304 | bytes 393218 | tf_op jit(solution)/shard_map/jit(_where)/select_n | solution.py:49
  0.9 0.1 broadcast_select_fusion.2
  1.0 3.0 %collective-permute-start.1 = (bf16[2,192,128]{2,1,0:T(8,128)(2,1)S(1)}, bf16[2,192,128]{2,1,0:T(8,128)(2,1)S(1)}, u32[]{:S(2)}, u32[]{:S(2)}) collective-permute-start(bf16[2,192,128]{2,1,0:T(8,128)(2,1)S(1)} %get-tuple-element.39), channel_id=1, source_target_pairs={{0,2},{2,0},{4,6},{6,4},{8,10},{10,8},{12,14},{14,12},{1,3},{3,1},... | collective-permute-start | bytes 294920 | tf_op jit(solution)/shard_map/ppermute | solution.py:325
  4.0 0.7 %pad_add_fusion.meta_ref = s32[24]{0:T(128)S(1)} fusion(s32[8]{0:T(128)} %bitcast.1, s32[16]{0:T(128)} %param.10), kind=kLoop, calls=%fused_computation.9 | loop fusion | flops 24 | bytes 192 | tf_op jit(solution)/shard_map/concatenate | solution.py:337
  4.8 0.1 slice.27
  4.8 1.1 %broadcast_select_fusion = (bf16[192,512]{1,0:T(8,128)(2,1)S(1)}, bf16[192,512]{1,0:T(8,128)(2,1)S(1)}) fusion(pred[]{:T(512)S(6)} %eq.18, bf16[192,1024]{1,0:T(8,128)(2,1)} %param.6, pred[]{:T(512)S(6)} %eq.17), kind=kLoop, calls=%fused_computation.1 | loop fusion | flops 196608 | bytes 786434 | tf_op jit(solution)/shard_map/jit(_where)/select_n | solution.py:49
  5.9 0.1 pad.6.clone
  6.0 0.1 pad_maximum_fusion.refs_2_
  6.1 0.7 %collective-permute-done.1.refs_1_ = bf16[2,192,128]{2,1,0:T(8,128)(2,1)S(1)} collective-permute-done((bf16[2,192,128]{2,1,0:T(8,128)(2,1)S(1)}, bf16[2,192,128]{2,1,0:T(8,128)(2,1)S(1)}, u32[]{:S(2)}, u32[]{:S(2)}) %collective-permute-start.1) | collective-permute-done | bytes 98336 | tf_op jit(solution)/shard_map/ppermute | solution.py:325
  6.8 3.8 %collective-permute-start.2 = (bf16[2,2,192,128]{3,2,1,0:T(8,128)(2,1)S(1)}, bf16[2,2,192,128]{3,2,1,0:T(8,128)(2,1)S(1)}, u32[]{:S(2)}, u32[]{:S(2)}) collective-permute-start(bf16[2,2,192,128]{3,2,1,0:T(8,128)(2,1)S(1)} %shard_map.64.refs_2_), channel_id=1, source_target_pairs={{0,4},{2,6},{4,8},{6,10},{8,12},{10,14},{1,5},{3,7},{5,9},{7,11},{... | collective-permute-start | bytes 589832 | tf_op jit(solution)/shard_map/ppermute | solution.py:330
  10.6 1.6 %collective-permute-start = (bf16[208,512]{1,0:T(8,128)(2,1)S(1)}, bf16[208,512]{1,0:T(8,128)(2,1)S(1)}, u32[]{:S(2)}, u32[]{:S(2)}) collective-permute-start(bf16[208,512]{1,0:T(8,128)(2,1)S(1)} %pad_maximum_fusion.refs_2_), channel_id=1, source_target_pairs={{0,2},{2,0},{4,6},{6,4},{8,10},{10,8},{12,14},{14,12},{1,3},{3,1},... | collective-permute-start | bytes 638984 | tf_op jit(solution)/shard_map/ppermute | solution.py:325
  12.2 3.3 %collective-permute-start.4 = (bf16[2,2,192,128]{3,2,1,0:T(8,128)(2,1)S(1)}, bf16[2,2,192,128]{3,2,1,0:T(8,128)(2,1)S(1)}, u32[]{:S(2)}, u32[]{:S(2)}) collective-permute-start(bf16[2,2,192,128]{3,2,1,0:T(8,128)(2,1)S(1)} %shard_map.64.refs_2_), channel_id=1, source_target_pairs={{0,12},{2,14},{1,13},{3,15},{16,28},{18,30},{17,29},{19,31}} | collective-permute-start | bytes 589832 | tf_op jit(solution)/shard_map/ppermute | solution.py:330
  15.5 0.0 collective-permute-done.2.refs_0_
  15.5 0.7 %collective-permute-start.3 = (bf16[2,2,192,128]{3,2,1,0:T(8,128)(2,1)S(1)}, bf16[2,2,192,128]{3,2,1,0:T(8,128)(2,1)S(1)}, u32[]{:S(2)}, u32[]{:S(2)}) collective-permute-start(bf16[2,2,192,128]{3,2,1,0:T(8,128)(2,1)S(1)} %collective-permute-done.2.refs_0_), channel_id=1, source_target_pairs={{4,8},{6,10},{8,12},{10,14},{5,9},{7,11},{9,13},{11,15},{20,24},{2... | collective-permute-start | bytes 589832 | tf_op jit(solution)/shard_map/ppermute | solution.py:330
  16.2 0.3 collective-permute-done.refs_1_
  16.5 0.1 broadcast_in_dim.41.own_flags_ref
  16.6 3.4 %shard_map.65 = (bf16[2,128,768]{2,1,0:T(8,128)(2,1)S(1)}, f32[2,16,128]{2,1,0:T(8,128)S(1)}, bf16[2,64,768]{2,1,0:T(8,128)(2,1)S(1)}, f32[16,128]{1,0:T(8,128)S...) custom-call(s32[24]{0:T(128)S(1)} %pad_add_fusion.meta_ref, ...), custom_call_target="tpu_custom_call" | custom-call | flops 1024 | bytes 1024 | tf_op jit(solution)/shard_map/pallas_call | solution.py:184
  20.0 1.6 %shard_map.66 = (f32[2,1,768]{2,1,0:T(1,128)S(1)}, f32[2,1,768]{2,1,0:T(1,128)S(1)}, f32[2,128,768]{2,1,0:T(8,128)S(1)}, bf16[256,4096]{1,0:T(8,128)(2,1)S(1)}) custom-call(f32[2,16,128]{2,1,0:T(8,128)S(1)} %get-tuple-element.19.flags_ref, ...), custom_call_target="tpu_custom_call", output_to_operand_aliasing={{0}: (3, {}), {1}: (4, {}), {2}: (5, {})} | custom-call | flops 1024 | bytes 1024 | tf_op jit(solution)/shard_map/pallas_call | solution.py:267
  21.6 0.0 collective-permute-done.4.refs_1_
  21.6 0.0 collective-permute-done.3.refs_0_
  21.7 1.9 %shard_map.67 = (f32[8,2,512]{2,1,0:T(2,128)S(1)}, bf16[256,4096]{1,0:T(8,128)(2,1)S(1)}) custom-call(f32[2,16,128]{2,1,0:T(8,128)S(1)} %get-tuple-element.19.flags_ref, bf16[2,128,768]{2,1,0:T(8,128)(2,1)S(1)} %get-tuple-element.20.turned_ref, bf16[2,2,192,128]{3,2,1,0:T(8,128)(2,1)S(1)} %collective-permute-done.3.refs_0_, ...), custom_call_target="tpu_custom_call" | custom-call | flops 1024 | bytes 1024 | tf_op jit(solution)/shard_map/pallas_call | solution.py:267
  23.6 17.2 %all_to_all.5.parts_ref = f32[8,2,512]{2,1,0:T(2,128)S(1)} all-to-all(f32[8,2,512]{2,1,0:T(2,128)S(1)} %get-tuple-element.29), channel_id=1, replica_groups=mesh['conv'=2,'seq'=8,'head'=2] {'seq'}, dimensions={0} | all-to-all | bytes 65536 | tf_op jit(solution)/shard_map/all_to_all | solution.py:381
  40.7 0.7 %shard_map.69 = f32[2,2048]{1,0:T(2,128)S(1)} custom-call(f32[8,2,512]{2,1,0:T(2,128)S(1)} %all_to_all.5.parts_ref, bf16[512,4096]{1,0:T(8,128)(2,1)S(1)} %get-tuple-element.30.refs_0_, bf16[256,4096]{1,0:T(8,128)(2,1)S(1)} %get-tuple-element.31.refs_1_, bf16[256,4096]{1,0:T(8,128)(2,1)S(1)} %get-tuple-element.32.refs_2_), custom_call_target="tpu_custom_call" | custom-call | flops 1024 | bytes 1024 | tf_op jit(solution)/shard_map/pallas_call | solution.py:311
  41.4 0.0 collective-permute-start.5
  41.4 0.7 %shard_map.68 = f32[2,2048]{1,0:T(2,128)S(1)} custom-call(f32[8,2,512]{2,1,0:T(2,128)S(1)} %all_to_all.5.parts_ref, bf16[512,4096]{1,0:T(8,128)(2,1)S(1)} %get-tuple-element.30.refs_0_, bf16[256,4096]{1,0:T(8,128)(2,1)S(1)} %get-tuple-element.31.refs_1_, bf16[256,4096]{1,0:T(8,128)(2,1)S(1)} %get-tuple-element.32.refs_2_), custom_call_target="tpu_custom_call" | custom-call | flops 1024 | bytes 1024 | tf_op jit(solution)/shard_map/pallas_call | solution.py:311
  42.1 0.5 %collective-permute-done.5 = f32[2,2048]{1,0:T(2,128)S(1)} collective-permute-done((f32[2,2048]{1,0:T(2,128)S(1)}, f32[2,2048]{1,0:T(2,128)S(1)}, u32[]{:S(2)}, u32[]{:S(2)}) %collective-permute-start.5) | collective-permute-done | bytes 16416 | tf_op jit(solution)/shard_map/ppermute | solution.py:383
  42.6 0.6 %add.10 = f32[2,2048]{1,0:T(2,128)} add(f32[2,2048]{1,0:T(2,128)S(1)} %shard_map.68, f32[2,2048]{1,0:T(2,128)S(1)} %collective-permute-done.5) | non-fusion elementwise | flops 4096 | bytes 49152 | tf_op jit(solution)/shard_map/add | solution.py:384
  (3 shorter events, 0.0 us)
Async XLA Ops:
  1.0 5.8 %collective-permute-start.1 = (bf16[2,192,128]{2,1,0:T(8,128)(2,1)S(1)}, bf16[2,192,128]{2,1,0:T(8,128)(2,1)S(1)}, u32[]{:S(2)}, u32[]{:S(2)}) collective-permute-start(bf16[2,192,128]{2,1,0:T(8,128)(2,1)S(1)} %get-tuple-element.39), channel_id=1, source_target_pairs={{0,2},{2,0},{4,6},{6,4},{8,10},{10,8},{12,14},{14,12},{1,3},{3,1},... | collective-permute-start | bytes 294920 | tf_op jit(solution)/shard_map/ppermute | solution.py:325
  6.8 8.7 %collective-permute-start.2 = (bf16[2,2,192,128]{3,2,1,0:T(8,128)(2,1)S(1)}, bf16[2,2,192,128]{3,2,1,0:T(8,128)(2,1)S(1)}, u32[]{:S(2)}, u32[]{:S(2)}) collective-permute-start(bf16[2,2,192,128]{3,2,1,0:T(8,128)(2,1)S(1)} %shard_map.64.refs_2_), channel_id=1, source_target_pairs={{0,4},{2,6},{4,8},{6,10},{8,12},{10,14},{1,5},{3,7},{5,9},{7,11},{... | collective-permute-start | bytes 589832 | tf_op jit(solution)/shard_map/ppermute | solution.py:330
  10.6 5.9 %collective-permute-start = (bf16[208,512]{1,0:T(8,128)(2,1)S(1)}, bf16[208,512]{1,0:T(8,128)(2,1)S(1)}, u32[]{:S(2)}, u32[]{:S(2)}) collective-permute-start(bf16[208,512]{1,0:T(8,128)(2,1)S(1)} %pad_maximum_fusion.refs_2_), channel_id=1, source_target_pairs={{0,2},{2,0},{4,6},{6,4},{8,10},{10,8},{12,14},{14,12},{1,3},{3,1},... | collective-permute-start | bytes 638984 | tf_op jit(solution)/shard_map/ppermute | solution.py:325
  12.2 9.4 %collective-permute-start.4 = (bf16[2,2,192,128]{3,2,1,0:T(8,128)(2,1)S(1)}, bf16[2,2,192,128]{3,2,1,0:T(8,128)(2,1)S(1)}, u32[]{:S(2)}, u32[]{:S(2)}) collective-permute-start(bf16[2,2,192,128]{3,2,1,0:T(8,128)(2,1)S(1)} %shard_map.64.refs_2_), channel_id=1, source_target_pairs={{0,12},{2,14},{1,13},{3,15},{16,28},{18,30},{17,29},{19,31}} | collective-permute-start | bytes 589832 | tf_op jit(solution)/shard_map/ppermute | solution.py:330
  15.5 6.1 %collective-permute-start.3 = (bf16[2,2,192,128]{3,2,1,0:T(8,128)(2,1)S(1)}, bf16[2,2,192,128]{3,2,1,0:T(8,128)(2,1)S(1)}, u32[]{:S(2)}, u32[]{:S(2)}) collective-permute-start(bf16[2,2,192,128]{3,2,1,0:T(8,128)(2,1)S(1)} %collective-permute-done.2.refs_0_), channel_id=1, source_target_pairs={{4,8},{6,10},{8,12},{10,14},{5,9},{7,11},{9,13},{11,15},{20,24},{2... | collective-permute-start | bytes 589832 | tf_op jit(solution)/shard_map/ppermute | solution.py:330
  41.4 1.2 %collective-permute-start.5 = (f32[2,2048]{1,0:T(2,128)S(1)}, f32[2,2048]{1,0:T(2,128)S(1)}, u32[]{:S(2)}, u32[]{:S(2)}) collective-permute-start(f32[2,2048]{1,0:T(2,128)S(1)} %shard_map.69), channel_id=1, source_target_pairs={{0,1},{1,0},{2,3},{3,2},{4,5},{5,4},{6,7},{7,6},{8,9},{9,8},{10,11... | collective-permute-start | bytes 49160 | tf_op jit(solution)/shard_map/ppermute | solution.py:383

commit v2 on v1

--- a/solution.py
+++ b/solution.py
@@ -56,14 +56,14 @@
 
 
 def join_kernel(*refs):
-    *parts, _, out_ref = refs
+    *parts, out_ref = refs
     for e, part in enumerate(parts):
         out_ref[e] = part[...]
 
 
-def join(parts, after):
+def join(parts):
     shape = jax.ShapeDtypeStruct((len(parts),) + parts[0].shape, parts[0].dtype)
-    return call(join_kernel, shape, in_specs=[in_vmem] * len(parts) + [anywhere])(*parts, after)
+    return call(join_kernel, shape, in_specs=[in_vmem] * len(parts))(*parts)
 
 
 def rows_update(turned_ref, rows_refs, switches, state, first):
@@ -124,14 +124,55 @@
     return jnp.concatenate([flag] * (columns // HD), axis=1) > 0.5
 
 
+def member_kernel(across, turns, meta_ref, after_ref, member_ref, inverse_ref, rows_ref):
+    del after_ref
+    z, y = place(across)
+    columns = rows_ref.shape[1]
+    repeat = member_ref.shape[1] // turns
+    q_rows = columns // repeat
+    owners = [block_at(z, y, e, across) for e in range(across)]
+    column = lax.broadcasted_iota(jnp.int32, (1, columns), 1)
+    for e in range(across):
+        position = lax.rem(column, q_rows) + owners[e] * q_rows
+        start = jnp.int32(0)
+        for t in range(turns):
+            length = meta_ref[t]
+            inside = (position >= start) & (position < start + length)
+            rows_ref[t : t + 1, :] = jnp.where(inside, 1.0, 0.0)
+            if e == 0:
+                count = jnp.full((1, HD), length, jnp.int32).astype(jnp.float32)
+                inverse_ref[t : t + 1, :] = 1.0 / count
+            start = start + length
+        for r in range(repeat):
+            mine = (column >= r * q_rows) & (column < (r + 1) * q_rows)
+            member_ref[e, r * turns : (r + 1) * turns, :] = jnp.where(
+                mine, rows_ref[...], 0.0
+            ).astype(jnp.bfloat16)
+
+
+def members(across, turns, meta, group):
+    q_rows, width = group.shape
+    repeat = width // HD
+    columns = repeat * q_rows
+    return call(
+        functools.partial(member_kernel, across, turns),
+        [
+            jax.ShapeDtypeStruct((across, repeat * turns, columns), jnp.bfloat16),
+            jax.ShapeDtypeStruct((turns, HD), jnp.float32),
+        ],
+        in_specs=[in_smem, anywhere],
+        scratch_shapes=[pltpu.VMEM((turns, columns), jnp.float32)],
+    )(meta, group)
+
+
 def weight_piece(weight_ref, out_ref, start, sem):
     return pltpu.make_async_copy(weight_ref.at[start : start + out_ref.shape[0]], out_ref, sem)
 
 
-def first_kernel(across, turns, meta_ref, own_flags_ref, *refs):
+def first_kernel(across, own_flags_ref, *refs):
     queries, refs = refs[:across], refs[across:]
-    kv_ref, weight_ref, turned_ref, flags_ref, member_ref, inverse_ref, weight_out = refs[:7]
-    state, rows_ref, copied = refs[7:10], refs[10], refs[11]
+    kv_ref, weight_ref, turned_ref, flags_ref, weight_out = refs[:5]
+    state, copied = refs[5:8], refs[8]
     weight_copy = weight_piece(weight_ref, weight_out, 0, copied)
     weight_copy.start()
     z, y = place(across)
@@ -156,47 +197,28 @@
     ]
     rows_update(turned_ref, [kv_ref], switches, state, True)
 
-    column = lax.broadcasted_iota(jnp.int32, (1, columns), 1)
-    for e in range(across):
-        position = lax.rem(column, q_rows) + owners[e] * q_rows
-        start = jnp.int32(0)
-        for t in range(turns):
-            length = meta_ref[t]
-            inside = (position >= start) & (position < start + length)
-            rows_ref[t : t + 1, :] = jnp.where(inside, 1.0, 0.0)
-            if e == 0:
-                count = jnp.full((1, HD), length, jnp.int32).astype(jnp.float32)
-                inverse_ref[t : t + 1, :] = 1.0 / count
-            start = start + length
-        for r in range(repeat):
-            mine = (column >= r * q_rows) & (column < (r + 1) * q_rows)
-            member_ref[e, r * turns : (r + 1) * turns, :] = jnp.where(
-                mine, rows_ref[...], 0.0
-            ).astype(jnp.bfloat16)
     weight_copy.wait()
 
 
-def attend_first(across, turns, meta, flags, queries, rows, weight, piece):
+def attend_first(across, flags, queries, rows, weight, piece):
     q_rows = rows.shape[2]
     repeat = queries[0].shape[1] // HD
     columns = repeat * q_rows
     f32, b16 = jnp.float32, jnp.bfloat16
     return call(
-        functools.partial(first_kernel, across, turns),
+        functools.partial(first_kernel, across),
         [
             jax.ShapeDtypeStruct((across, HD, columns), b16),
             jax.ShapeDtypeStruct((across,) + flags.shape, f32),
-            jax.ShapeDtypeStruct((across, repeat * turns, columns), b16),
-            jax.ShapeDtypeStruct((turns, HD), f32),
             jax.ShapeDtypeStruct((piece, weight.shape[1]), weight.dtype),
             jax.ShapeDtypeStruct((across, 1, columns), f32),
             jax.ShapeDtypeStruct((across, 1, columns), f32),
             jax.ShapeDtypeStruct((across, HD, columns), f32),
         ],
-        in_specs=[in_smem] + [in_vmem] * (across + 2) + [anywhere],
-        scratch_shapes=[pltpu.VMEM((turns, columns), f32), pltpu.SemaphoreType.DMA(())],
+        in_specs=[in_vmem] * (across + 2) + [anywhere],
+        scratch_shapes=[pltpu.SemaphoreType.DMA(())],
         limit=big_limit,
-    )(meta, flags, *queries, rows, weight)
+    )(flags, *queries, rows, weight)
 
 
 def next_kernel(across, distances, turns, last, weight_at, flags_ref, turned_ref, *refs):
@@ -334,6 +356,8 @@
     for shift in range(across):
         at = lax.rem(y + shift, across)
         heads.append(pair(pick(key_states, at, across), pick(value_states, at, across)))
+    rows = join([heads[0]] + [over(heads[shift], shift) for shift in range(1, across)])
+    rows, queries = lax.optimization_barrier((rows, queries))
     meta = lax.optimization_barrier(jnp.concatenate([turn_lengths, block_flags[0]]))
     padded = -(-count // 16) * 16
     flags = jnp.pad(meta[turns:], (0, padded - count))[:, None]
@@ -343,17 +367,18 @@
         under = jnp.broadcast_to(flags, (padded, group.shape[1])).astype(group.dtype)
         sent.append(jnp.concatenate([group, under], axis=0))
     flags = jnp.broadcast_to(flags, (padded, HD)).astype(jnp.float32)
+    below = [rows, up(rows, 1)] + [None] * (down - 2)
+    member, inverse = members(across, turns, meta, groups[0])
+    far, inverse, *sent = lax.optimization_barrier((rows, inverse, *sent))
     others = [over(group, shift) for shift, group in enumerate(sent, 1)]
-    rows = join([heads[0]] + [over(heads[shift], shift) for shift in range(1, across)], sent[0])
-    below = [rows, up(rows, 1)] + [None] * (down - 2)
     for distance in range(3, down):
-        below[distance] = up(rows, distance)
+        below[distance] = up(far, distance)
     if down > 2:
         below[2] = up(below[1], 1, 1)
     depth = out_weight.shape[0]
     pieces = [4 * depth // 8, 2 * depth // 8, 2 * depth // 8]
-    turned, flags, member, inverse, weight, *state = attend_first(
-        across, turns, meta, flags, [groups[0], *others], rows, out_weight, pieces[0]
+    turned, flags, weight, *state = attend_first(
+        across, flags, [groups[0], *others], rows, out_weight, pieces[0]
     )
     weights = [weight]
     out_piece = (count, turns // count, queries.shape[1] // across)

time: 43.6 us -> 41.2 us (0.945)
  blocking collectives: 17.2 us -> 13.7 us
  waiting for transfers between devices: 1.58 us -> 2.73 us
    all_to_all x1, blocking collectives: 17.2 us -> 13.7 us  [on_device(): lax.all_to_all(state[0], 'seq', split_axis=0, concat_axis=0, tiled=True)]
    ppermute x2, waiting for transfers between devices: 1.05 us -> 2.21 us  [over(): return lax.ppermute(rows, 'seq', pairs)]
    pallas_call x2 -> x3, Pallas kernels: 3.41 us -> 3.35 us  [the longest x1 2.61 us: attend_first(): call(functools.partial(first_kernel, across), [jax.ShapeDtypeStruct((acro...]
  transfers between devices with their start and end apart: 6 -> 6, of which waited for: 3 -> 3; matrix products, arithmetic and copies ran while one was open for 5% -> 5% of each run, Pallas kernels for 13% -> 14%
where the time goes in v2:
time: 41.2 us; the launch traced here: 40.8 us
  blocking collectives  13.7 us (33%)
  starting transfers between devices  12.4 us (30%)
  Pallas kernels  8.18 us (20%)
  other arithmetic  3.5 us (8%)
  waiting for transfers between devices  2.73 us (7%)
    all_to_all x1, blocking collectives, on_device(): lax.all_to_all(state[0], 'seq', split_axis=0, concat_axis=0, tiled=True)  13.7 us
    ppermute x3, starting transfers between devices, up(): return lax.ppermute(rows, 'seq', pairs)  7.77 us
    ppermute x2, starting transfers between devices, over(): return lax.ppermute(rows, 'seq', pairs)  4.62 us
    pallas_call x2, Pallas kernels, attend_next(): call(functools.partial(next_kernel, across, distances, turns, last, at),...  3.49 us
    pallas_call x1, Pallas kernels, attend_first(): call(functools.partial(first_kernel, across), [jax.ShapeDtypeStruct((acro...  2.61 us
    ppermute x2, waiting for transfers between devices, over(): return lax.ppermute(rows, 'seq', pairs)  2.21 us
    select_n x2, other arithmetic, pick(): jnp.where(number == part, rows[:, part * width:(part + 1) * width], picked)  1.94 us
    pallas_call x2, Pallas kernels, project(): call(functools.partial(project_kernel, across, other), jax.ShapeDtypeStru...  1.34 us
  transfers between devices with their start and end apart: 6, of which 3 were waited for; matrix products, arithmetic and copies ran while one was open for 5% of the time, Pallas kernels for 14%

profile of v2, /device:TPU:0, one launch (start us, length us, event | category | flops | bytes accessed | tf_op | source)
XLA Modules:
  0.0 40.8 jit_solution(9562512709152751074)
XLA Ops:
  0.0 0.9 %broadcast_select_fusion.4 = (bf16[192,128]{1,0:T(8,128)(2,1)S(1)}, bf16[192,128]{1,0:T(8,128)(2,1)S(1)}, bf16[192,128]{1,0:T(8,128)(2,1)S(1)}, bf16[192,128]{1,0:T(8,128)(2,1)S(1)}) fusion(pred[]{:T(512)S(6)} %eq.19, bf16[192,256]{1,0:T(8,128)(2,1)} %param.8, pred[]{:T(512)S(6)} %eq.17, bf16[192,256]{1,0:T(8,128)(2,1)} %param.7), kind=kLoop, calls=%fused_computation.5 | loop fusion | flops 98304 | bytes 393218 | tf_op jit(solution)/shard_map/jit(_where)/select_n | solution.py:49
  0.9 0.1 broadcast_select_fusion.2
  1.0 3.0 %collective-permute-start = (bf16[2,192,128]{2,1,0:T(8,128)(2,1)S(1)}, bf16[2,192,128]{2,1,0:T(8,128)(2,1)S(1)}, u32[]{:S(2)}, u32[]{:S(2)}) collective-permute-start(bf16[2,192,128]{2,1,0:T(8,128)(2,1)S(1)} %get-tuple-element.51), channel_id=1, source_target_pairs={{0,2},{2,0},{4,6},{6,4},{8,10},{10,8},{12,14},{14,12},{1,3},{3,1},... | collective-permute-start | bytes 294920 | tf_op jit(solution)/shard_map/ppermute | solution.py:347
  4.0 0.7 %pad_add_fusion.meta_ref = s32[24]{0:T(128)S(1)} fusion(s32[8]{0:T(128)} %bitcast.1, s32[16]{0:T(128)} %param.10), kind=kLoop, calls=%fused_computation.9 | loop fusion | flops 24 | bytes 192 | tf_op jit(solution)/shard_map/concatenate | solution.py:361
  4.8 0.1 slice.27
  4.8 0.1 pad.6.clone
  4.9 1.9 %collective-permute-done.refs_1_ = bf16[2,192,128]{2,1,0:T(8,128)(2,1)S(1)} collective-permute-done((bf16[2,192,128]{2,1,0:T(8,128)(2,1)S(1)}, bf16[2,192,128]{2,1,0:T(8,128)(2,1)S(1)}, u32[]{:S(2)}, u32[]{:S(2)}) %collective-permute-start) | collective-permute-done | bytes 98336 | tf_op jit(solution)/shard_map/ppermute | solution.py:347
  6.8 3.8 %collective-permute-start.2 = (bf16[2,2,192,128]{3,2,1,0:T(8,128)(2,1)S(1)}, bf16[2,2,192,128]{3,2,1,0:T(8,128)(2,1)S(1)}, u32[]{:S(2)}, u32[]{:S(2)}) collective-permute-start(bf16[2,2,192,128]{3,2,1,0:T(8,128)(2,1)S(1)} %shard_map.64.refs_2_), channel_id=1, source_target_pairs={{0,4},{2,6},{4,8},{6,10},{8,12},{10,14},{1,5},{3,7},{5,9},{7,11},{... | collective-permute-start | bytes 589832 | tf_op jit(solution)/shard_map/ppermute | solution.py:352
  10.6 1.1 %broadcast_select_fusion = (bf16[192,512]{1,0:T(8,128)(2,1)S(1)}, bf16[192,512]{1,0:T(8,128)(2,1)S(1)}) fusion(pred[]{:T(512)S(6)} %eq.19, bf16[192,1024]{1,0:T(8,128)(2,1)} %param.6, pred[]{:T(512)S(6)} %eq.17), kind=kLoop, calls=%fused_computation.1 | loop fusion | flops 196608 | bytes 786434 | tf_op jit(solution)/shard_map/jit(_where)/select_n | solution.py:49
  11.7 0.7 %shard_map.65 = (bf16[2,64,768]{2,1,0:T(8,128)(2,1)S(1)}, f32[16,128]{1,0:T(8,128)S(1)}) custom-call(s32[24]{0:T(128)S(1)} %pad_add_fusion.meta_ref, bf16[192,512]{1,0:T(8,128)(2,1)S(1)} %get-tuple-element.44.after_ref.refs_0_), custom_call_target="tpu_custom_call" | custom-call | flops 1024 | bytes 1024 | tf_op jit(solution)/shard_map/pallas_call | solution.py:157
  12.4 0.1 pad_maximum_fusion
  12.5 1.6 %collective-permute-start.1 = (bf16[208,512]{1,0:T(8,128)(2,1)S(1)}, bf16[208,512]{1,0:T(8,128)(2,1)S(1)}, u32[]{:S(2)}, u32[]{:S(2)}) collective-permute-start(bf16[208,512]{1,0:T(8,128)(2,1)S(1)} %pad_maximum_fusion), channel_id=1, source_target_pairs={{0,2},{2,0},{4,6},{6,4},{8,10},{10,8},{12,14},{14,12},{1,3},{3,1},... | collective-permute-start | bytes 638984 | tf_op jit(solution)/shard_map/ppermute | solution.py:347
  14.1 3.3 %collective-permute-start.4 = (bf16[2,2,192,128]{3,2,1,0:T(8,128)(2,1)S(1)}, bf16[2,2,192,128]{3,2,1,0:T(8,128)(2,1)S(1)}, u32[]{:S(2)}, u32[]{:S(2)}) collective-permute-start(bf16[2,2,192,128]{3,2,1,0:T(8,128)(2,1)S(1)} %shard_map.64.refs_2_), channel_id=1, source_target_pairs={{0,12},{2,14},{1,13},{3,15},{16,28},{18,30},{17,29},{19,31}} | collective-permute-start | bytes 589832 | tf_op jit(solution)/shard_map/ppermute | solution.py:352
  17.4 0.0 collective-permute-done.2.refs_0_
  17.4 0.7 %collective-permute-start.3 = (bf16[2,2,192,128]{3,2,1,0:T(8,128)(2,1)S(1)}, bf16[2,2,192,128]{3,2,1,0:T(8,128)(2,1)S(1)}, u32[]{:S(2)}, u32[]{:S(2)}) collective-permute-start(bf16[2,2,192,128]{3,2,1,0:T(8,128)(2,1)S(1)} %collective-permute-done.2.refs_0_), channel_id=1, source_target_pairs={{4,8},{6,10},{8,12},{10,14},{5,9},{7,11},{9,13},{11,15},{20,24},{2... | collective-permute-start | bytes 589832 | tf_op jit(solution)/shard_map/ppermute | solution.py:352
  18.1 0.3 collective-permute-done.1.refs_1_
  18.4 0.1 broadcast_in_dim.41.own_flags_ref
  18.5 2.6 %shard_map.66 = (bf16[2,128,768]{2,1,0:T(8,128)(2,1)S(1)}, f32[2,16,128]{2,1,0:T(8,128)S(1)}, bf16[512,4096]{1,0:T(8,128)(2,1)S(1)}, f32[2,1,768]{2,1,0:T(1,128)...) custom-call(f32[16,128]{1,0:T(8,128)S(1)} %broadcast_in_dim.41.own_flags_ref, ...), custom_call_target="tpu_custom_call" | custom-call | flops 1024 | bytes 1024 | tf_op jit(solution)/shard_map/pallas_call | solution.py:208
  21.1 1.6 %shard_map.67 = (f32[2,1,768]{2,1,0:T(1,128)S(1)}, f32[2,1,768]{2,1,0:T(1,128)S(1)}, f32[2,128,768]{2,1,0:T(8,128)S(1)}, bf16[256,4096]{1,0:T(8,128)(2,1)S(1)}) custom-call(f32[2,16,128]{2,1,0:T(8,128)S(1)} %get-tuple-element.28.flags_ref, ...), custom_call_target="tpu_custom_call", output_to_operand_aliasing={{0}: (3, {}), {1}: (4, {}), {2}: (5, {})} | custom-call | flops 1024 | bytes 1024 | tf_op jit(solution)/shard_map/pallas_call | solution.py:289
  22.7 0.0 collective-permute-done.4.refs_1_
  22.7 0.0 collective-permute-done.3.refs_0_
  22.8 1.9 %shard_map.68 = (f32[8,2,512]{2,1,0:T(2,128)S(1)}, bf16[256,4096]{1,0:T(8,128)(2,1)S(1)}) custom-call(f32[2,16,128]{2,1,0:T(8,128)S(1)} %get-tuple-element.28.flags_ref, bf16[2,128,768]{2,1,0:T(8,128)(2,1)S(1)} %get-tuple-element.29.turned_ref, bf16[2,2,192,128]{3,2,1,0:T(8,128)(2,1)S(1)} %collective-permute-done.3.refs_0_, ...), custom_call_target="tpu_custom_call" | custom-call | flops 1024 | bytes 1024 | tf_op jit(solution)/shard_map/pallas_call | solution.py:289
  24.7 13.7 %all_to_all.5.parts_ref = f32[8,2,512]{2,1,0:T(2,128)S(1)} all-to-all(f32[8,2,512]{2,1,0:T(2,128)S(1)} %get-tuple-element.39), channel_id=1, replica_groups=mesh['conv'=2,'seq'=8,'head'=2] {'seq'}, dimensions={0} | all-to-all | bytes 65536 | tf_op jit(solution)/shard_map/all_to_all | solution.py:406
  38.3 0.7 %shard_map.70 = f32[2,2048]{1,0:T(2,128)S(1)} custom-call(f32[8,2,512]{2,1,0:T(2,128)S(1)} %all_to_all.5.parts_ref, bf16[512,4096]{1,0:T(8,128)(2,1)S(1)} %get-tuple-element.40.refs_0_, bf16[256,4096]{1,0:T(8,128)(2,1)S(1)} %get-tuple-element.41.refs_1_, bf16[256,4096]{1,0:T(8,128)(2,1)S(1)} %get-tuple-element.42.refs_2_), custom_call_target="tpu_custom_call" | custom-call | flops 1024 | bytes 1024 | tf_op jit(solution)/shard_map/pallas_call | solution.py:333
  39.0 0.0 collective-permute-start.5
  39.0 0.7 %shard_map.69 = f32[2,2048]{1,0:T(2,128)S(1)} custom-call(f32[8,2,512]{2,1,0:T(2,128)S(1)} %all_to_all.5.parts_ref, bf16[512,4096]{1,0:T(8,128)(2,1)S(1)} %get-tuple-element.40.refs_0_, bf16[256,4096]{1,0:T(8,128)(2,1)S(1)} %get-tuple-element.41.refs_1_, bf16[256,4096]{1,0:T(8,128)(2,1)S(1)} %get-tuple-element.42.refs_2_), custom_call_target="tpu_custom_call" | custom-call | flops 1024 | bytes 1024 | tf_op jit(solution)/shard_map/pallas_call | solution.py:333
  39.7 0.5 %collective-permute-done.5 = f32[2,2048]{1,0:T(2,128)S(1)} collective-permute-done((f32[2,2048]{1,0:T(2,128)S(1)}, f32[2,2048]{1,0:T(2,128)S(1)}, u32[]{:S(2)}, u32[]{:S(2)}) %collective-permute-start.5) | collective-permute-done | bytes 16416 | tf_op jit(solution)/shard_map/ppermute | solution.py:408
  40.2 0.6 %add.10 = f32[2,2048]{1,0:T(2,128)} add(f32[2,2048]{1,0:T(2,128)S(1)} %shard_map.69, f32[2,2048]{1,0:T(2,128)S(1)} %collective-permute-done.5) | non-fusion elementwise | flops 4096 | bytes 49152 | tf_op jit(solution)/shard_map/add | solution.py:409
  (3 shorter events, 0.0 us)
Async XLA Ops:
  1.0 5.8 %collective-permute-start = (bf16[2,192,128]{2,1,0:T(8,128)(2,1)S(1)}, bf16[2,192,128]{2,1,0:T(8,128)(2,1)S(1)}, u32[]{:S(2)}, u32[]{:S(2)}) collective-permute-start(bf16[2,192,128]{2,1,0:T(8,128)(2,1)S(1)} %get-tuple-element.51), channel_id=1, source_target_pairs={{0,2},{2,0},{4,6},{6,4},{8,10},{10,8},{12,14},{14,12},{1,3},{3,1},... | collective-permute-start | bytes 294920 | tf_op jit(solution)/shard_map/ppermute | solution.py:347
  6.8 10.6 %collective-permute-start.2 = (bf16[2,2,192,128]{3,2,1,0:T(8,128)(2,1)S(1)}, bf16[2,2,192,128]{3,2,1,0:T(8,128)(2,1)S(1)}, u32[]{:S(2)}, u32[]{:S(2)}) collective-permute-start(bf16[2,2,192,128]{3,2,1,0:T(8,128)(2,1)S(1)} %shard_map.64.refs_2_), channel_id=1, source_target_pairs={{0,4},{2,6},{4,8},{6,10},{8,12},{10,14},{1,5},{3,7},{5,9},{7,11},{... | collective-permute-start | bytes 589832 | tf_op jit(solution)/shard_map/ppermute | solution.py:352
  12.5 5.9 %collective-permute-start.1 = (bf16[208,512]{1,0:T(8,128)(2,1)S(1)}, bf16[208,512]{1,0:T(8,128)(2,1)S(1)}, u32[]{:S(2)}, u32[]{:S(2)}) collective-permute-start(bf16[208,512]{1,0:T(8,128)(2,1)S(1)} %pad_maximum_fusion), channel_id=1, source_target_pairs={{0,2},{2,0},{4,6},{6,4},{8,10},{10,8},{12,14},{14,12},{1,3},{3,1},... | collective-permute-start | bytes 638984 | tf_op jit(solution)/shard_map/ppermute | solution.py:347
  14.1 8.6 %collective-permute-start.4 = (bf16[2,2,192,128]{3,2,1,0:T(8,128)(2,1)S(1)}, bf16[2,2,192,128]{3,2,1,0:T(8,128)(2,1)S(1)}, u32[]{:S(2)}, u32[]{:S(2)}) collective-permute-start(bf16[2,2,192,128]{3,2,1,0:T(8,128)(2,1)S(1)} %shard_map.64.refs_2_), channel_id=1, source_target_pairs={{0,12},{2,14},{1,13},{3,15},{16,28},{18,30},{17,29},{19,31}} | collective-permute-start | bytes 589832 | tf_op jit(solution)/shard_map/ppermute | solution.py:352
  17.4 5.3 %collective-permute-start.3 = (bf16[2,2,192,128]{3,2,1,0:T(8,128)(2,1)S(1)}, bf16[2,2,192,128]{3,2,1,0:T(8,128)(2,1)S(1)}, u32[]{:S(2)}, u32[]{:S(2)}) collective-permute-start(bf16[2,2,192,128]{3,2,1,0:T(8,128)(2,1)S(1)} %collective-permute-done.2.refs_0_), channel_id=1, source_target_pairs={{4,8},{6,10},{8,12},{10,14},{5,9},{7,11},{9,13},{11,15},{20,24},{2... | collective-permute-start | bytes 589832 | tf_op jit(solution)/shard_map/ppermute | solution.py:352
  39.0 1.2 %collective-permute-start.5 = (f32[2,2048]{1,0:T(2,128)S(1)}, f32[2,2048]{1,0:T(2,128)S(1)}, u32[]{:S(2)}, u32[]{:S(2)}) collective-permute-start(f32[2,2048]{1,0:T(2,128)S(1)} %shard_map.70), channel_id=1, source_target_pairs={{0,1},{1,0},{2,3},{3,2},{4,5},{5,4},{6,7},{7,6},{8,9},{9,8},{10,11... | collective-permute-start | bytes 49160 | tf_op jit(solution)/shard_map/ppermute | solution.py:408

commit v3 on v2

--- a/solution.py
+++ b/solution.py
@@ -382,10 +382,10 @@
     )
     weights = [weight]
     out_piece = (count, turns // count, queries.shape[1] // across)
-    stages = [[1]] + [list(range(d, min(d + 2, down))) for d in range(2, down, 2)]
+    stages = [[1]] + [list(range(d, min(d + 2, down))) for d in range(3, down, 2)] + [[2]]
     for number, distances in enumerate(stages):
         last = number == len(stages) - 1
-        with_weight = last or number == 0
+        with_weight = number < 2
         state = attend_next(
             across,
             distances,

time: 41.2 us -> 40.5 us (0.983)
  blocking collectives: 13.7 us -> 13 us
    all_to_all x1, blocking collectives: 13.7 us -> 13 us  [on_device(): lax.all_to_all(state[0], 'seq', split_axis=0, concat_axis=0, tiled=True)]
    pallas_call x2 -> x3, Pallas kernels: 3.49 us -> 3.51 us  [attend_next(): call(functools.partial(next_kernel, across, distances, turns, last, at),...]
  transfers between devices with their start and end apart: 6 -> 6, of which waited for: 3 -> 3; matrix products, arithmetic and copies ran while one was open for 5% -> 5% of each run, Pallas kernels for 14% -> 18%
where the time goes in v3:
time: 40.5 us; the launch traced here: 40.2 us
  blocking collectives  13 us (32%)
  starting transfers between devices  12.4 us (31%)
  Pallas kernels  8.2 us (20%)
  other arithmetic  3.5 us (9%)
  waiting for transfers between devices  2.73 us (7%)
    all_to_all x1, blocking collectives, on_device(): lax.all_to_all(state[0], 'seq', split_axis=0, concat_axis=0, tiled=True)  13 us
    ppermute x3, starting transfers between devices, up(): return lax.ppermute(rows, 'seq', pairs)  7.77 us
    ppermute x2, starting transfers between devices, over(): return lax.ppermute(rows, 'seq', pairs)  4.62 us
    pallas_call x3, Pallas kernels, attend_next(): call(functools.partial(next_kernel, across, distances, turns, last, at),...  3.51 us
    pallas_call x1, Pallas kernels, attend_first(): call(functools.partial(first_kernel, across), [jax.ShapeDtypeStruct((acro...  2.61 us
    ppermute x2, waiting for transfers between devices, over(): return lax.ppermute(rows, 'seq', pairs)  2.21 us
    select_n x2, other arithmetic, pick(): jnp.where(number == part, rows[:, part * width:(part + 1) * width], picked)  1.94 us
    pallas_call x2, Pallas kernels, project(): call(functools.partial(project_kernel, across, other), jax.ShapeDtypeStru...  1.34 us
  transfers between devices with their start and end apart: 6, of which 3 were waited for; matrix products, arithmetic and copies ran while one was open for 5% of the time, Pallas kernels for 18%

profile of v3, /device:TPU:0, one launch (start us, length us, event | category | flops | bytes accessed | tf_op | source)
XLA Modules:
  0.0 40.2 jit_solution(4455306907060383872)
XLA Ops:
  0.0 0.9 %broadcast_select_fusion.4 = (bf16[192,128]{1,0:T(8,128)(2,1)S(1)}, bf16[192,128]{1,0:T(8,128)(2,1)S(1)}, bf16[192,128]{1,0:T(8,128)(2,1)S(1)}, bf16[192,128]{1,0:T(8,128)(2,1)S(1)}) fusion(pred[]{:T(512)S(6)} %eq.19, bf16[192,256]{1,0:T(8,128)(2,1)} %param.8, pred[]{:T(512)S(6)} %eq.17, bf16[192,256]{1,0:T(8,128)(2,1)} %param.7), kind=kLoop, calls=%fused_computation.5 | loop fusion | flops 98304 | bytes 393218 | tf_op jit(solution)/shard_map/jit(_where)/select_n | solution.py:49
  0.9 0.1 broadcast_select_fusion.2
  1.0 3.0 %collective-permute-start = (bf16[2,192,128]{2,1,0:T(8,128)(2,1)S(1)}, bf16[2,192,128]{2,1,0:T(8,128)(2,1)S(1)}, u32[]{:S(2)}, u32[]{:S(2)}) collective-permute-start(bf16[2,192,128]{2,1,0:T(8,128)(2,1)S(1)} %get-tuple-element.55), channel_id=1, source_target_pairs={{0,2},{2,0},{4,6},{6,4},{8,10},{10,8},{12,14},{14,12},{1,3},{3,1},... | collective-permute-start | bytes 294920 | tf_op jit(solution)/shard_map/ppermute | solution.py:347
  4.0 0.7 %pad_add_fusion.meta_ref = s32[24]{0:T(128)S(1)} fusion(s32[8]{0:T(128)} %bitcast.1, s32[16]{0:T(128)} %param.10), kind=kLoop, calls=%fused_computation.9 | loop fusion | flops 24 | bytes 192 | tf_op jit(solution)/shard_map/concatenate | solution.py:361
  4.8 0.1 slice.27
  4.8 0.1 pad.6.clone
  4.9 1.9 %collective-permute-done.refs_1_ = bf16[2,192,128]{2,1,0:T(8,128)(2,1)S(1)} collective-permute-done((bf16[2,192,128]{2,1,0:T(8,128)(2,1)S(1)}, bf16[2,192,128]{2,1,0:T(8,128)(2,1)S(1)}, u32[]{:S(2)}, u32[]{:S(2)}) %collective-permute-start) | collective-permute-done | bytes 98336 | tf_op jit(solution)/shard_map/ppermute | solution.py:347
  6.8 3.8 %collective-permute-start.2 = (bf16[2,2,192,128]{3,2,1,0:T(8,128)(2,1)S(1)}, bf16[2,2,192,128]{3,2,1,0:T(8,128)(2,1)S(1)}, u32[]{:S(2)}, u32[]{:S(2)}) collective-permute-start(bf16[2,2,192,128]{3,2,1,0:T(8,128)(2,1)S(1)} %shard_map.64.refs_2_), channel_id=1, source_target_pairs={{0,4},{2,6},{4,8},{6,10},{8,12},{10,14},{1,5},{3,7},{5,9},{7,11},{... | collective-permute-start | bytes 589832 | tf_op jit(solution)/shard_map/ppermute | solution.py:352
  10.6 1.1 %broadcast_select_fusion = (bf16[192,512]{1,0:T(8,128)(2,1)S(1)}, bf16[192,512]{1,0:T(8,128)(2,1)S(1)}) fusion(pred[]{:T(512)S(6)} %eq.19, bf16[192,1024]{1,0:T(8,128)(2,1)} %param.6, pred[]{:T(512)S(6)} %eq.17), kind=kLoop, calls=%fused_computation.1 | loop fusion | flops 196608 | bytes 786434 | tf_op jit(solution)/shard_map/jit(_where)/select_n | solution.py:49
  11.7 0.7 %shard_map.65 = (bf16[2,64,768]{2,1,0:T(8,128)(2,1)S(1)}, f32[16,128]{1,0:T(8,128)S(1)}) custom-call(s32[24]{0:T(128)S(1)} %pad_add_fusion.meta_ref, bf16[192,512]{1,0:T(8,128)(2,1)S(1)} %get-tuple-element.48.after_ref.refs_0_), custom_call_target="tpu_custom_call" | custom-call | flops 1024 | bytes 1024 | tf_op jit(solution)/shard_map/pallas_call | solution.py:157
  12.4 0.1 pad_maximum_fusion
  12.5 1.6 %collective-permute-start.1 = (bf16[208,512]{1,0:T(8,128)(2,1)S(1)}, bf16[208,512]{1,0:T(8,128)(2,1)S(1)}, u32[]{:S(2)}, u32[]{:S(2)}) collective-permute-start(bf16[208,512]{1,0:T(8,128)(2,1)S(1)} %pad_maximum_fusion), channel_id=1, source_target_pairs={{0,2},{2,0},{4,6},{6,4},{8,10},{10,8},{12,14},{14,12},{1,3},{3,1},... | collective-permute-start | bytes 638984 | tf_op jit(solution)/shard_map/ppermute | solution.py:347
  14.1 3.3 %collective-permute-start.4 = (bf16[2,2,192,128]{3,2,1,0:T(8,128)(2,1)S(1)}, bf16[2,2,192,128]{3,2,1,0:T(8,128)(2,1)S(1)}, u32[]{:S(2)}, u32[]{:S(2)}) collective-permute-start(bf16[2,2,192,128]{3,2,1,0:T(8,128)(2,1)S(1)} %shard_map.64.refs_2_), channel_id=1, source_target_pairs={{0,12},{2,14},{1,13},{3,15},{16,28},{18,30},{17,29},{19,31}} | collective-permute-start | bytes 589832 | tf_op jit(solution)/shard_map/ppermute | solution.py:352
  17.4 0.0 collective-permute-done.2.refs_0_
  17.4 0.7 %collective-permute-start.3 = (bf16[2,2,192,128]{3,2,1,0:T(8,128)(2,1)S(1)}, bf16[2,2,192,128]{3,2,1,0:T(8,128)(2,1)S(1)}, u32[]{:S(2)}, u32[]{:S(2)}) collective-permute-start(bf16[2,2,192,128]{3,2,1,0:T(8,128)(2,1)S(1)} %collective-permute-done.2.refs_0_), channel_id=1, source_target_pairs={{4,8},{6,10},{8,12},{10,14},{5,9},{7,11},{9,13},{11,15},{20,24},{2... | collective-permute-start | bytes 589832 | tf_op jit(solution)/shard_map/ppermute | solution.py:352
  18.1 0.3 collective-permute-done.1.refs_1_
  18.4 0.1 broadcast_in_dim.41.own_flags_ref
  18.5 2.6 %shard_map.66 = (bf16[2,128,768]{2,1,0:T(8,128)(2,1)S(1)}, f32[2,16,128]{2,1,0:T(8,128)S(1)}, bf16[512,4096]{1,0:T(8,128)(2,1)S(1)}, f32[2,1,768]{2,1,0:T(1,128)...) custom-call(f32[16,128]{1,0:T(8,128)S(1)} %broadcast_in_dim.41.own_flags_ref, ...), custom_call_target="tpu_custom_call" | custom-call | flops 1024 | bytes 1024 | tf_op jit(solution)/shard_map/pallas_call | solution.py:208
  21.1 1.6 %shard_map.67 = (f32[2,1,768]{2,1,0:T(1,128)S(1)}, f32[2,1,768]{2,1,0:T(1,128)S(1)}, f32[2,128,768]{2,1,0:T(8,128)S(1)}, bf16[256,4096]{1,0:T(8,128)(2,1)S(1)}) custom-call(f32[2,16,128]{2,1,0:T(8,128)S(1)} %get-tuple-element.30.flags_ref, ...), custom_call_target="tpu_custom_call", output_to_operand_aliasing={{0}: (3, {}), {1}: (4, {}), {2}: (5, {})} | custom-call | flops 1024 | bytes 1024 | tf_op jit(solution)/shard_map/pallas_call | solution.py:289
  22.7 0.0 collective-permute-done.4.refs_0_
  22.7 1.6 %shard_map.68 = (f32[2,1,768]{2,1,0:T(1,128)S(1)}, f32[2,1,768]{2,1,0:T(1,128)S(1)}, f32[2,128,768]{2,1,0:T(8,128)S(1)}, bf16[256,4096]{1,0:T(8,128)(2,1)S(1)}) custom-call(f32[2,16,128]{2,1,0:T(8,128)S(1)} %get-tuple-element.30.flags_ref, ...), custom_call_target="tpu_custom_call", output_to_operand_aliasing={{0}: (3, {}), {1}: (4, {}), {2}: (5, {})} | custom-call | flops 1024 | bytes 1024 | tf_op jit(solution)/shard_map/pallas_call | solution.py:289
  24.4 0.0 collective-permute-done.3.refs_0_
  24.4 0.3 shard_map.69
  24.7 13.0 %all_to_all.5.parts_ref = f32[8,2,512]{2,1,0:T(2,128)S(1)} all-to-all(f32[8,2,512]{2,1,0:T(2,128)S(1)} %shard_map.69), channel_id=1, replica_groups=mesh['conv'=2,'seq'=8,'head'=2] {'seq'}, dimensions={0} | all-to-all | bytes 65536 | tf_op jit(solution)/shard_map/all_to_all | solution.py:406
  37.7 0.7 %shard_map.71 = f32[2,2048]{1,0:T(2,128)S(1)} custom-call(f32[8,2,512]{2,1,0:T(2,128)S(1)} %all_to_all.5.parts_ref, bf16[512,4096]{1,0:T(8,128)(2,1)S(1)} %get-tuple-element.44.refs_0_, bf16[256,4096]{1,0:T(8,128)(2,1)S(1)} %get-tuple-element.45.refs_1_, bf16[256,4096]{1,0:T(8,128)(2,1)S(1)} %get-tuple-element.46.refs_2_), custom_call_target="tpu_custom_call" | custom-call | flops 1024 | bytes 1024 | tf_op jit(solution)/shard_map/pallas_call | solution.py:333
  38.3 0.0 collective-permute-start.5
  38.4 0.7 %shard_map.70 = f32[2,2048]{1,0:T(2,128)S(1)} custom-call(f32[8,2,512]{2,1,0:T(2,128)S(1)} %all_to_all.5.parts_ref, bf16[512,4096]{1,0:T(8,128)(2,1)S(1)} %get-tuple-element.44.refs_0_, bf16[256,4096]{1,0:T(8,128)(2,1)S(1)} %get-tuple-element.45.refs_1_, bf16[256,4096]{1,0:T(8,128)(2,1)S(1)} %get-tuple-element.46.refs_2_), custom_call_target="tpu_custom_call" | custom-call | flops 1024 | bytes 1024 | tf_op jit(solution)/shard_map/pallas_call | solution.py:333
  39.0 0.5 %collective-permute-done.5 = f32[2,2048]{1,0:T(2,128)S(1)} collective-permute-done((f32[2,2048]{1,0:T(2,128)S(1)}, f32[2,2048]{1,0:T(2,128)S(1)}, u32[]{:S(2)}, u32[]{:S(2)}) %collective-permute-start.5) | collective-permute-done | bytes 16416 | tf_op jit(solution)/shard_map/ppermute | solution.py:408
  39.5 0.6 %add.10 = f32[2,2048]{1,0:T(2,128)} add(f32[2,2048]{1,0:T(2,128)S(1)} %shard_map.70, f32[2,2048]{1,0:T(2,128)S(1)} %collective-permute-done.5) | non-fusion elementwise | flops 4096 | bytes 49152 | tf_op jit(solution)/shard_map/add | solution.py:409
  (3 shorter events, 0.0 us)
Async XLA Ops:
  1.0 5.8 %collective-permute-start = (bf16[2,192,128]{2,1,0:T(8,128)(2,1)S(1)}, bf16[2,192,128]{2,1,0:T(8,128)(2,1)S(1)}, u32[]{:S(2)}, u32[]{:S(2)}) collective-permute-start(bf16[2,192,128]{2,1,0:T(8,128)(2,1)S(1)} %get-tuple-element.55), channel_id=1, source_target_pairs={{0,2},{2,0},{4,6},{6,4},{8,10},{10,8},{12,14},{14,12},{1,3},{3,1},... | collective-permute-start | bytes 294920 | tf_op jit(solution)/shard_map/ppermute | solution.py:347
  6.8 10.6 %collective-permute-start.2 = (bf16[2,2,192,128]{3,2,1,0:T(8,128)(2,1)S(1)}, bf16[2,2,192,128]{3,2,1,0:T(8,128)(2,1)S(1)}, u32[]{:S(2)}, u32[]{:S(2)}) collective-permute-start(bf16[2,2,192,128]{3,2,1,0:T(8,128)(2,1)S(1)} %shard_map.64.refs_2_), channel_id=1, source_target_pairs={{0,4},{2,6},{4,8},{6,10},{8,12},{10,14},{1,5},{3,7},{5,9},{7,11},{... | collective-permute-start | bytes 589832 | tf_op jit(solution)/shard_map/ppermute | solution.py:352
  12.5 5.9 %collective-permute-start.1 = (bf16[208,512]{1,0:T(8,128)(2,1)S(1)}, bf16[208,512]{1,0:T(8,128)(2,1)S(1)}, u32[]{:S(2)}, u32[]{:S(2)}) collective-permute-start(bf16[208,512]{1,0:T(8,128)(2,1)S(1)} %pad_maximum_fusion), channel_id=1, source_target_pairs={{0,2},{2,0},{4,6},{6,4},{8,10},{10,8},{12,14},{14,12},{1,3},{3,1},... | collective-permute-start | bytes 638984 | tf_op jit(solution)/shard_map/ppermute | solution.py:347
  14.1 8.6 %collective-permute-start.4 = (bf16[2,2,192,128]{3,2,1,0:T(8,128)(2,1)S(1)}, bf16[2,2,192,128]{3,2,1,0:T(8,128)(2,1)S(1)}, u32[]{:S(2)}, u32[]{:S(2)}) collective-permute-start(bf16[2,2,192,128]{3,2,1,0:T(8,128)(2,1)S(1)} %shard_map.64.refs_2_), channel_id=1, source_target_pairs={{0,12},{2,14},{1,13},{3,15},{16,28},{18,30},{17,29},{19,31}} | collective-permute-start | bytes 589832 | tf_op jit(solution)/shard_map/ppermute | solution.py:352
  17.4 6.9 %collective-permute-start.3 = (bf16[2,2,192,128]{3,2,1,0:T(8,128)(2,1)S(1)}, bf16[2,2,192,128]{3,2,1,0:T(8,128)(2,1)S(1)}, u32[]{:S(2)}, u32[]{:S(2)}) collective-permute-start(bf16[2,2,192,128]{3,2,1,0:T(8,128)(2,1)S(1)} %collective-permute-done.2.refs_0_), channel_id=1, source_target_pairs={{4,8},{6,10},{8,12},{10,14},{5,9},{7,11},{9,13},{11,15},{20,24},{2... | collective-permute-start | bytes 589832 | tf_op jit(solution)/shard_map/ppermute | solution.py:352
  38.3 1.2 %collective-permute-start.5 = (f32[2,2048]{1,0:T(2,128)S(1)}, f32[2,2048]{1,0:T(2,128)S(1)}, u32[]{:S(2)}, u32[]{:S(2)}) collective-permute-start(f32[2,2048]{1,0:T(2,128)S(1)} %shard_map.71), channel_id=1, source_target_pairs={{0,1},{1,0},{2,3},{3,2},{4,5},{5,4},{6,7},{7,6},{8,9},{9,8},{10,11... | collective-permute-start | bytes 49160 | tf_op jit(solution)/shard_map/ppermute | solution.py:408

commit v4 on v3

--- a/solution.py
+++ b/solution.py
@@ -14,7 +14,7 @@
 log_two_e = 1.4426950408889634
 
 big_limit = 45 * 1024 * 1024
-small_cost = pl.CostEstimate(flops=1024, bytes_accessed=1024, transcendentals=0)
+short_flops, long_flops = 2e9, 4e9
 
 in_vmem = pl.BlockSpec(memory_space=pltpu.VMEM)
 in_smem = pl.BlockSpec(memory_space=pltpu.SMEM)
@@ -30,14 +30,19 @@
     return z * across + lax.rem(y - e + across, across)
 
 
+def cost_of(flops):
+    return pl.CostEstimate(flops=int(flops), bytes_accessed=1024, transcendentals=0)
+
+
 def call(kernel, out_shape, **settings):
     limit = settings.pop("limit", 16 * 1024 * 1024)
+    cost = cost_of(settings.pop("cost", 0))
     return pl.pallas_call(
         kernel,
         out_shape=out_shape,
         out_specs=jax.tree.map(lambda _: in_vmem, out_shape),
         compiler_params=pltpu.CompilerParams(vmem_limit_bytes=limit),
-        cost_estimate=small_cost,
+        cost_estimate=cost,
         **settings,
     )
 
@@ -69,11 +74,11 @@
 def rows_update(turned_ref, rows_refs, switches, state, first):
     top, total_sum, totals = state
     across, _, columns = turned_ref.shape
-    rows = rows_refs[0].shape[2]
+    rows = rows_refs[0][0].shape[1]
     count = across * len(rows_refs)
     factor = log_two_e / math.sqrt(HD)
-    keys = [kv_ref[:, 0].reshape(across * rows, HD) for kv_ref in rows_refs]
-    values = [kv_ref[:, 1].reshape(across * rows, HD).T for kv_ref in rows_refs]
+    keys = [jnp.concatenate([part[0] for part in parts], axis=0) for parts in rows_refs]
+    values = [jnp.concatenate([part[1] for part in parts], axis=0).T for parts in rows_refs]
     logits = [
         [jnp.dot(part, turned_ref[e], preferred_element_type=jnp.float32) for part in keys]
         for e in range(across)
@@ -124,8 +129,13 @@
     return jnp.concatenate([flag] * (columns // HD), axis=1) > 0.5
 
 
-def member_kernel(across, turns, meta_ref, after_ref, member_ref, inverse_ref, rows_ref):
-    del after_ref
+def weight_piece(weight_ref, out_ref, start, sem):
+    return pltpu.make_async_copy(weight_ref.at[start : start + out_ref.shape[0]], out_ref, sem)
+
+
+def member_kernel(across, turns, meta_ref, _, weight_ref, member_ref, inverse_ref, weight_out, rows_ref, copied):
+    weight_copy = weight_piece(weight_ref, weight_out, 0, copied)
+    weight_copy.start()
     z, y = place(across)
     columns = rows_ref.shape[1]
     repeat = member_ref.shape[1] // turns
@@ -148,9 +158,10 @@
             member_ref[e, r * turns : (r + 1) * turns, :] = jnp.where(
                 mine, rows_ref[...], 0.0
             ).astype(jnp.bfloat16)
-
-
-def members(across, turns, meta, group):
+    weight_copy.wait()
+
+
+def members(across, turns, meta, group, weight, piece):
     q_rows, width = group.shape
     repeat = width // HD
     columns = repeat * q_rows
@@ -159,21 +170,20 @@
         [
             jax.ShapeDtypeStruct((across, repeat * turns, columns), jnp.bfloat16),
             jax.ShapeDtypeStruct((turns, HD), jnp.float32),
+            jax.ShapeDtypeStruct((piece, weight.shape[1]), weight.dtype),
         ],
-        in_specs=[in_smem, anywhere],
-        scratch_shapes=[pltpu.VMEM((turns, columns), jnp.float32)],
-    )(meta, group)
-
-
-def weight_piece(weight_ref, out_ref, start, sem):
-    return pltpu.make_async_copy(weight_ref.at[start : start + out_ref.shape[0]], out_ref, sem)
-
-
-def first_kernel(across, own_flags_ref, *refs):
+        in_specs=[in_smem, anywhere, anywhere],
+        scratch_shapes=[pltpu.VMEM((turns, columns), jnp.float32), pltpu.SemaphoreType.DMA(())],
+        limit=big_limit,
+        cost=long_flops,
+    )(meta, group, weight)
+
+
+def first_kernel(across, weight_at, own_flags_ref, *refs):
     queries, refs = refs[:across], refs[across:]
     kv_ref, weight_ref, turned_ref, flags_ref, weight_out = refs[:5]
     state, copied = refs[5:8], refs[8]
-    weight_copy = weight_piece(weight_ref, weight_out, 0, copied)
+    weight_copy = weight_piece(weight_ref, weight_out, weight_at, copied)
     weight_copy.start()
     z, y = place(across)
     q_rows = kv_ref.shape[2]
@@ -195,18 +205,18 @@
         ]
         for e in range(across)
     ]
-    rows_update(turned_ref, [kv_ref], switches, state, True)
+    rows_update(turned_ref, [[kv_ref.at[e] for e in range(across)]], switches, state, True)
 
     weight_copy.wait()
 
 
-def attend_first(across, flags, queries, rows, weight, piece):
+def attend_first(across, flags, queries, rows, weight, at, piece):
     q_rows = rows.shape[2]
     repeat = queries[0].shape[1] // HD
     columns = repeat * q_rows
     f32, b16 = jnp.float32, jnp.bfloat16
     return call(
-        functools.partial(first_kernel, across),
+        functools.partial(first_kernel, across, at),
         [
             jax.ShapeDtypeStruct((across, HD, columns), b16),
             jax.ShapeDtypeStruct((across,) + flags.shape, f32),
@@ -222,8 +232,15 @@
 
 
 def next_kernel(across, distances, turns, last, weight_at, flags_ref, turned_ref, *refs):
-    below_count = len(distances)
-    below, state, refs = refs[:below_count], refs[below_count : below_count + 3], refs[below_count + 3 :]
+    below = []
+    for distance in distances:
+        if distance < 3:
+            below.append([refs[0].at[e] for e in range(across)])
+            refs = refs[1:]
+        else:
+            below.append(refs[:across])
+            refs = refs[across:]
+    state, refs = refs[:3], refs[3:]
     if weight_at is not None:
         weight_ref, weight_out, copied = refs[0], refs[-2], refs[-1]
         refs = refs[1:-2]
@@ -292,6 +309,7 @@
         in_specs=in_specs,
         scratch_shapes=scratch,
         input_output_aliases=aliases,
+        cost=short_flops,
         limit=big_limit if at is not None else 16 * 1024 * 1024,
     )(*args)
 
@@ -351,12 +369,15 @@
         pairs = [(i, i + step) for i in range(lowest * across, count - step)]
         return lax.ppermute(rows, "seq", pairs)
 
+    depth = out_weight.shape[0]
+    pieces = [depth // 8, 4 * depth // 8, 2 * depth // 8, depth // 8]
     _, y = place(across)
     heads = []
     for shift in range(across):
         at = lax.rem(y + shift, across)
         heads.append(pair(pick(key_states, at, across), pick(value_states, at, across)))
-    rows = join([heads[0]] + [over(heads[shift], shift) for shift in range(1, across)])
+    swapped = [over(heads[shift], shift) for shift in range(1, across)]
+    rows = join([heads[0]] + swapped)
     rows, queries = lax.optimization_barrier((rows, queries))
     meta = lax.optimization_barrier(jnp.concatenate([turn_lengths, block_flags[0]]))
     padded = -(-count // 16) * 16
@@ -367,32 +388,35 @@
         under = jnp.broadcast_to(flags, (padded, group.shape[1])).astype(group.dtype)
         sent.append(jnp.concatenate([group, under], axis=0))
     flags = jnp.broadcast_to(flags, (padded, HD)).astype(jnp.float32)
-    below = [rows, up(rows, 1)] + [None] * (down - 2)
-    member, inverse = members(across, turns, meta, groups[0])
-    far, inverse, *sent = lax.optimization_barrier((rows, inverse, *sent))
+    below = [[rows], up(rows, 1)] + [None] * (down - 2)
+    early = [up(heads[0], distance) for distance in range(3, down)]
+    member, inverse, weight = members(across, turns, meta, groups[0], out_weight, pieces[0])
+    inverse, *swapped = lax.optimization_barrier((inverse, *swapped))
     others = [over(group, shift) for shift, group in enumerate(sent, 1)]
+    below[1], *early = lax.optimization_barrier((below[1], *early))
     for distance in range(3, down):
-        below[distance] = up(far, distance)
+        late = [up(part, distance) for part in swapped]
+        below[distance] = [early[distance - 3]] + late
     if down > 2:
-        below[2] = up(below[1], 1, 1)
-    depth = out_weight.shape[0]
-    pieces = [4 * depth // 8, 2 * depth // 8, 2 * depth // 8]
+        below[2] = [up(below[1], 1, 1)]
+    below[1] = [below[1]]
+    weights = [weight]
     turned, flags, weight, *state = attend_first(
-        across, flags, [groups[0], *others], rows, out_weight, pieces[0]
+        across, flags, [groups[0], *others], rows, out_weight, pieces[0], pieces[1]
     )
-    weights = [weight]
+    weights.append(weight)
     out_piece = (count, turns // count, queries.shape[1] // across)
-    stages = [[1]] + [list(range(d, min(d + 2, down))) for d in range(3, down, 2)] + [[2]]
+    stages = [list(range(d, min(d + 2, down))) for d in range(3, down, 2)] + [[1], [2]]
     for number, distances in enumerate(stages):
         last = number == len(stages) - 1
-        with_weight = number < 2
+        with_weight = last or distances == [1]
         state = attend_next(
             across,
             distances,
             turns,
             turned,
             flags,
-            [below[distance] for distance in distances],
+            [part for distance in distances for part in below[distance]],
             state,
             (member, inverse) if last else None,
             out_piece,

time: 40.5 us -> 41.1 us (1.015)
  waiting for transfers between devices: 2.73 us -> 0.78 us
  starting transfers between devices: 12.4 us -> 14.3 us
  Pallas kernels: 8.2 us -> 8.87 us
    ppermute x3 -> x4, starting transfers between devices: 7.77 us -> 10.7 us  [up(): return lax.ppermute(rows, 'seq', pairs)]
    ppermute x2, waiting for transfers between devices: 2.21 us -> 0.25 us  [over(): return lax.ppermute(rows, 'seq', pairs)]
    pallas_call x1, Pallas kernels: 0.73 us -> 1.77 us  [members(): call(functools.partial(member_kernel, across, turns), [jax.ShapeDtypeStru...]
    ppermute x2, starting transfers between devices: 4.62 us -> 3.6 us  [over(): return lax.ppermute(rows, 'seq', pairs)]
  transfers between devices with their start and end apart: 6 -> 7, of which waited for: 3 -> 2; matrix products, arithmetic and copies ran while one was open for 5% -> 5% of each run, Pallas kernels for 18% -> 16%
where the time goes in v4:
time: 41.1 us; the launch traced here: 40.7 us
  starting transfers between devices  14.3 us (35%)
  blocking collectives  12.9 us (31%)
  Pallas kernels  8.87 us (22%)
  other arithmetic  3.5 us (9%)
  waiting for transfers between devices  0.78 us (2%)
    all_to_all x1, blocking collectives, on_device(): lax.all_to_all(state[0], 'seq', split_axis=0, concat_axis=0, tiled=True)  12.9 us
    ppermute x4, starting transfers between devices, up(): return lax.ppermute(rows, 'seq', pairs)  10.7 us
    ppermute x2, starting transfers between devices, over(): return lax.ppermute(rows, 'seq', pairs)  3.6 us
    pallas_call x3, Pallas kernels, attend_next(): call(functools.partial(next_kernel, across, distances, turns, last, at),...  3.14 us
    pallas_call x1, Pallas kernels, attend_first(): call(functools.partial(first_kernel, across, at), [jax.ShapeDtypeStruct((...  2.61 us
    select_n x2, other arithmetic, pick(): jnp.where(number == part, rows[:, part * width:(part + 1) * width], picked)  1.94 us
    pallas_call x1, Pallas kernels, members(): call(functools.partial(member_kernel, across, turns), [jax.ShapeDtypeStru...  1.77 us
    pallas_call x2, Pallas kernels, project(): call(functools.partial(project_kernel, across, other), jax.ShapeDtypeStru...  1.34 us
  transfers between devices with their start and end apart: 7, of which 2 were waited for; matrix products, arithmetic and copies ran while one was open for 5% of the time, Pallas kernels for 16%

profile of v4, /device:TPU:0, one launch (start us, length us, event | category | flops | bytes accessed | tf_op | source)
XLA Modules:
  0.0 40.7 jit_solution(4498362422598324834)
XLA Ops:
  0.0 0.9 %broadcast_select_fusion.4 = (bf16[192,128]{1,0:T(8,128)(2,1)S(1)}, bf16[192,128]{1,0:T(8,128)(2,1)S(1)}, bf16[192,128]{1,0:T(8,128)(2,1)S(1)}, bf16[192,128]{1,0:T(8,128)(2,1)S(1)}) fusion(pred[]{:T(512)S(6)} %eq.19, bf16[192,256]{1,0:T(8,128)(2,1)} %param.8, pred[]{:T(512)S(6)} %eq.17, bf16[192,256]{1,0:T(8,128)(2,1)} %param.7), kind=kLoop, calls=%fused_computation.5 | loop fusion | flops 98304 | bytes 393218 | tf_op jit(solution)/shard_map/jit(_where)/select_n | solution.py:54
  0.9 0.1 broadcast_select_fusion.2
  1.0 3.0 %collective-permute-start = (bf16[2,192,128]{2,1,0:T(8,128)(2,1)S(1)}, bf16[2,192,128]{2,1,0:T(8,128)(2,1)S(1)}, u32[]{:S(2)}, u32[]{:S(2)}) collective-permute-start(bf16[2,192,128]{2,1,0:T(8,128)(2,1)S(1)} %get-tuple-element.61), channel_id=1, source_target_pairs={{0,2},{2,0},{4,6},{6,4},{8,10},{10,8},{12,14},{14,12},{1,3},{3,1},... | collective-permute-start | bytes 294920 | tf_op jit(solution)/shard_map/ppermute | solution.py:365
  4.0 5.5 %collective-permute-start.3 = (bf16[2,192,128]{2,1,0:T(8,128)(2,1)S(1)}, bf16[2,192,128]{2,1,0:T(8,128)(2,1)S(1)}, u32[]{:S(2)}, u32[]{:S(2)}) collective-permute-start(bf16[2,192,128]{2,1,0:T(8,128)(2,1)S(1)} %get-tuple-element.62.refs_0_), channel_id=1, source_target_pairs={{0,12},{2,14},{1,13},{3,15},{16,28},{18,30},{17,29},{19,31}} | collective-permute-start | bytes 294920 | tf_op jit(solution)/shard_map/ppermute | solution.py:370
  9.5 0.7 %pad_add_fusion.meta_ref = s32[24]{0:T(128)S(1)} fusion(s32[8]{0:T(128)} %bitcast.1, s32[16]{0:T(128)} %param.10), kind=kLoop, calls=%fused_computation.9 | loop fusion | flops 24 | bytes 192 | tf_op jit(solution)/shard_map/concatenate | solution.py:382
  10.3 0.1 slice.27
  10.4 0.1 pad.6.clone
  10.4 0.0 collective-permute-done.refs_1_
  10.5 1.3 %collective-permute-start.2 = (bf16[2,2,192,128]{3,2,1,0:T(8,128)(2,1)S(1)}, bf16[2,2,192,128]{3,2,1,0:T(8,128)(2,1)S(1)}, u32[]{:S(2)}, u32[]{:S(2)}) collective-permute-start(bf16[2,2,192,128]{3,2,1,0:T(8,128)(2,1)S(1)} %shard_map.64.refs_2_), channel_id=1, source_target_pairs={{0,4},{2,6},{4,8},{6,10},{8,12},{10,14},{1,5},{3,7},{5,9},{7,11},{... | collective-permute-start | bytes 589832 | tf_op jit(solution)/shard_map/ppermute | solution.py:370
  11.8 1.1 %broadcast_select_fusion = (bf16[192,512]{1,0:T(8,128)(2,1)S(1)}, bf16[192,512]{1,0:T(8,128)(2,1)S(1)}) fusion(pred[]{:T(512)S(6)} %eq.19, bf16[192,1024]{1,0:T(8,128)(2,1)} %param.6, pred[]{:T(512)S(6)} %eq.17), kind=kLoop, calls=%fused_computation.1 | loop fusion | flops 196608 | bytes 786434 | tf_op jit(solution)/shard_map/jit(_where)/select_n | solution.py:54
  12.8 0.1 pad_maximum_fusion
  12.9 0.6 %collective-permute-start.1 = (bf16[208,512]{1,0:T(8,128)(2,1)S(1)}, bf16[208,512]{1,0:T(8,128)(2,1)S(1)}, u32[]{:S(2)}, u32[]{:S(2)}) collective-permute-start(bf16[208,512]{1,0:T(8,128)(2,1)S(1)} %pad_maximum_fusion), channel_id=1, source_target_pairs={{0,2},{2,0},{4,6},{6,4},{8,10},{10,8},{12,14},{14,12},{1,3},{3,1},... | collective-permute-start | bytes 638984 | tf_op jit(solution)/shard_map/ppermute | solution.py:365
  13.5 1.8 %shard_map.66 = (bf16[2,64,768]{2,1,0:T(8,128)(2,1)S(1)}, f32[16,128]{1,0:T(8,128)S(1)}, bf16[128,4096]{1,0:T(8,128)(2,1)S(1)}) custom-call(s32[24]{0:T(128)S(1)} %pad_add_fusion.meta_ref, bf16[192,512]{1,0:T(8,128)(2,1)S(1)} %get-tuple-element.54.refs_0_._, bf16[1024,4096]{1,0:T(8,128)(2,1)} %refs_4_.3), custom_call_target="tpu_custom_call" | custom-call | flops 4000000000 | bytes 1024 | tf_op jit(solution)/shard_map/pallas_call | solution.py:168
  15.3 3.2 %collective-permute-start.5 = (bf16[2,192,128]{2,1,0:T(8,128)(2,1)S(1)}, bf16[2,192,128]{2,1,0:T(8,128)(2,1)S(1)}, u32[]{:S(2)}, u32[]{:S(2)}) collective-permute-start(bf16[2,192,128]{2,1,0:T(8,128)(2,1)S(1)} %collective-permute-done.refs_1_), channel_id=1, source_target_pairs={{0,12},{2,14},{1,13},{3,15},{16,28},{18,30},{17,29},{19,31}} | collective-permute-start | bytes 294920 | tf_op jit(solution)/shard_map/ppermute | solution.py:370
  18.5 0.0 collective-permute-done.3.refs_0_
  18.5 0.0 collective-permute-done.2.refs_0_
  18.5 0.7 %collective-permute-start.4 = (bf16[2,2,192,128]{3,2,1,0:T(8,128)(2,1)S(1)}, bf16[2,2,192,128]{3,2,1,0:T(8,128)(2,1)S(1)}, u32[]{:S(2)}, u32[]{:S(2)}) collective-permute-start(bf16[2,2,192,128]{3,2,1,0:T(8,128)(2,1)S(1)} %collective-permute-done.2.refs_0_), channel_id=1, source_target_pairs={{4,8},{6,10},{8,12},{10,14},{5,9},{7,11},{9,13},{11,15},{20,24},{2... | collective-permute-start | bytes 589832 | tf_op jit(solution)/shard_map/ppermute | solution.py:370
  19.2 0.2 collective-permute-done.1.refs_1_
  19.4 0.1 broadcast_in_dim.41.own_flags_ref
  19.5 2.6 %shard_map.65 = (bf16[2,128,768]{2,1,0:T(8,128)(2,1)S(1)}, f32[2,16,128]{2,1,0:T(8,128)S(1)}, bf16[512,4096]{1,0:T(8,128)(2,1)S(1)}, f32[2,1,768]{2,1,0:T(1,128)...) custom-call(f32[16,128]{1,0:T(8,128)S(1)} %broadcast_in_dim.41.own_flags_ref, ...), custom_call_target="tpu_custom_call" | custom-call | bytes 1024 | tf_op jit(solution)/shard_map/pallas_call | solution.py:218
  22.1 0.0 collective-permute-done.5.refs_1_
  22.2 1.6 %shard_map.68 = (f32[2,1,768]{2,1,0:T(1,128)S(1)}, f32[2,1,768]{2,1,0:T(1,128)S(1)}, f32[2,128,768]{2,1,0:T(8,128)S(1)}, bf16[256,4096]{1,0:T(8,128)(2,1)S(1)}) custom-call(f32[2,16,128]{2,1,0:T(8,128)S(1)} %get-tuple-element.31.flags_ref, ...), custom_call_target="tpu_custom_call", output_to_operand_aliasing={{0}: (3, {}), {1}: (4, {}), {2}: (5, {})} | custom-call | flops 2000000000 | bytes 1024 | tf_op jit(solution)/shard_map/pallas_call | solution.py:306
  23.8 0.0 collective-permute-done.4.refs_0_
  23.8 1.5 %shard_map.69 = (f32[8,2,512]{2,1,0:T(2,128)S(1)}, bf16[128,4096]{1,0:T(8,128)(2,1)S(1)}) custom-call(f32[2,16,128]{2,1,0:T(8,128)S(1)} %get-tuple-element.31.flags_ref, bf16[2,128,768]{2,1,0:T(8,128)(2,1)S(1)} %get-tuple-element.32.turned_ref, bf16[2,2,192,128]{3,2,1,0:T(8,128)(2,1)S(1)} %collective-permute-done.4.refs_0_, ...), custom_call_target="tpu_custom_call" | custom-call | flops 2000000000 | bytes 1024 | tf_op jit(solution)/shard_map/pallas_call | solution.py:306
  25.3 12.9 %all_to_all.5.parts_ref = f32[8,2,512]{2,1,0:T(2,128)S(1)} all-to-all(f32[8,2,512]{2,1,0:T(2,128)S(1)} %get-tuple-element.48), channel_id=1, replica_groups=mesh['conv'=2,'seq'=8,'head'=2] {'seq'}, dimensions={0} | all-to-all | bytes 65536 | tf_op jit(solution)/shard_map/all_to_all | solution.py:430
  38.2 0.7 %shard_map.71 = f32[2,2048]{1,0:T(2,128)S(1)} custom-call(f32[8,2,512]{2,1,0:T(2,128)S(1)} %all_to_all.5.parts_ref, bf16[128,4096]{1,0:T(8,128)(2,1)S(1)} %get-tuple-element.49.refs_0_, bf16[512,4096]{1,0:T(8,128)(2,1)S(1)} %get-tuple-element.50.refs_1_, bf16[256,4096]{1,0:T(8,128)(2,1)S(1)} %get-tuple-element.51.refs_2_, ...), custom_call_target="tpu_custom_call" | custom-call | bytes 1024 | tf_op jit(solution)/shard_map/pallas_call | solution.py:351
  38.9 0.0 collective-permute-start.6
  38.9 0.7 %shard_map.70 = f32[2,2048]{1,0:T(2,128)S(1)} custom-call(f32[8,2,512]{2,1,0:T(2,128)S(1)} %all_to_all.5.parts_ref, bf16[128,4096]{1,0:T(8,128)(2,1)S(1)} %get-tuple-element.49.refs_0_, bf16[512,4096]{1,0:T(8,128)(2,1)S(1)} %get-tuple-element.50.refs_1_, bf16[256,4096]{1,0:T(8,128)(2,1)S(1)} %get-tuple-element.51.refs_2_, ...), custom_call_target="tpu_custom_call" | custom-call | bytes 1024 | tf_op jit(solution)/shard_map/pallas_call | solution.py:351
  39.5 0.5 %collective-permute-done.6 = f32[2,2048]{1,0:T(2,128)S(1)} collective-permute-done((f32[2,2048]{1,0:T(2,128)S(1)}, f32[2,2048]{1,0:T(2,128)S(1)}, u32[]{:S(2)}, u32[]{:S(2)}) %collective-permute-start.6) | collective-permute-done | bytes 16416 | tf_op jit(solution)/shard_map/ppermute | solution.py:432
  40.1 0.6 %add.10 = f32[2,2048]{1,0:T(2,128)} add(f32[2,2048]{1,0:T(2,128)S(1)} %shard_map.70, f32[2,2048]{1,0:T(2,128)S(1)} %collective-permute-done.6) | non-fusion elementwise | flops 4096 | bytes 49152 | tf_op jit(solution)/shard_map/add | solution.py:433
  (4 shorter events, 0.1 us)
Async XLA Ops:
  1.0 9.5 %collective-permute-start = (bf16[2,192,128]{2,1,0:T(8,128)(2,1)S(1)}, bf16[2,192,128]{2,1,0:T(8,128)(2,1)S(1)}, u32[]{:S(2)}, u32[]{:S(2)}) collective-permute-start(bf16[2,192,128]{2,1,0:T(8,128)(2,1)S(1)} %get-tuple-element.61), channel_id=1, source_target_pairs={{0,2},{2,0},{4,6},{6,4},{8,10},{10,8},{12,14},{14,12},{1,3},{3,1},... | collective-permute-start | bytes 294920 | tf_op jit(solution)/shard_map/ppermute | solution.py:365
  4.0 14.5 %collective-permute-start.3 = (bf16[2,192,128]{2,1,0:T(8,128)(2,1)S(1)}, bf16[2,192,128]{2,1,0:T(8,128)(2,1)S(1)}, u32[]{:S(2)}, u32[]{:S(2)}) collective-permute-start(bf16[2,192,128]{2,1,0:T(8,128)(2,1)S(1)} %get-tuple-element.62.refs_0_), channel_id=1, source_target_pairs={{0,12},{2,14},{1,13},{3,15},{16,28},{18,30},{17,29},{19,31}} | collective-permute-start | bytes 294920 | tf_op jit(solution)/shard_map/ppermute | solution.py:370
  10.5 8.0 %collective-permute-start.2 = (bf16[2,2,192,128]{3,2,1,0:T(8,128)(2,1)S(1)}, bf16[2,2,192,128]{3,2,1,0:T(8,128)(2,1)S(1)}, u32[]{:S(2)}, u32[]{:S(2)}) collective-permute-start(bf16[2,2,192,128]{3,2,1,0:T(8,128)(2,1)S(1)} %shard_map.64.refs_2_), channel_id=1, source_target_pairs={{0,4},{2,6},{4,8},{6,10},{8,12},{10,14},{1,5},{3,7},{5,9},{7,11},{... | collective-permute-start | bytes 589832 | tf_op jit(solution)/shard_map/ppermute | solution.py:370
  12.9 6.5 %collective-permute-start.1 = (bf16[208,512]{1,0:T(8,128)(2,1)S(1)}, bf16[208,512]{1,0:T(8,128)(2,1)S(1)}, u32[]{:S(2)}, u32[]{:S(2)}) collective-permute-start(bf16[208,512]{1,0:T(8,128)(2,1)S(1)} %pad_maximum_fusion), channel_id=1, source_target_pairs={{0,2},{2,0},{4,6},{6,4},{8,10},{10,8},{12,14},{14,12},{1,3},{3,1},... | collective-permute-start | bytes 638984 | tf_op jit(solution)/shard_map/ppermute | solution.py:365
  15.3 6.8 %collective-permute-start.5 = (bf16[2,192,128]{2,1,0:T(8,128)(2,1)S(1)}, bf16[2,192,128]{2,1,0:T(8,128)(2,1)S(1)}, u32[]{:S(2)}, u32[]{:S(2)}) collective-permute-start(bf16[2,192,128]{2,1,0:T(8,128)(2,1)S(1)} %collective-permute-done.refs_1_), channel_id=1, source_target_pairs={{0,12},{2,14},{1,13},{3,15},{16,28},{18,30},{17,29},{19,31}} | collective-permute-start | bytes 294920 | tf_op jit(solution)/shard_map/ppermute | solution.py:370
  18.5 5.3 %collective-permute-start.4 = (bf16[2,2,192,128]{3,2,1,0:T(8,128)(2,1)S(1)}, bf16[2,2,192,128]{3,2,1,0:T(8,128)(2,1)S(1)}, u32[]{:S(2)}, u32[]{:S(2)}) collective-permute-start(bf16[2,2,192,128]{3,2,1,0:T(8,128)(2,1)S(1)} %collective-permute-done.2.refs_0_), channel_id=1, source_target_pairs={{4,8},{6,10},{8,12},{10,14},{5,9},{7,11},{9,13},{11,15},{20,24},{2... | collective-permute-start | bytes 589832 | tf_op jit(solution)/shard_map/ppermute | solution.py:370
  38.9 1.2 %collective-permute-start.6 = (f32[2,2048]{1,0:T(2,128)S(1)}, f32[2,2048]{1,0:T(2,128)S(1)}, u32[]{:S(2)}, u32[]{:S(2)}) collective-permute-start(f32[2,2048]{1,0:T(2,128)S(1)} %shard_map.71), channel_id=1, source_target_pairs={{0,1},{1,0},{2,3},{3,2},{4,5},{5,4},{6,7},{7,6},{8,9},{9,8},{10,11... | collective-permute-start | bytes 49160 | tf_op jit(solution)/shard_map/ppermute | solution.py:432

commit v5 on v3

--- a/solution.py
+++ b/solution.py
@@ -66,7 +66,7 @@
     return call(join_kernel, shape, in_specs=[in_vmem] * len(parts))(*parts)
 
 
-def rows_update(turned_ref, rows_refs, switches, state, first):
+def rows_update(turned_ref, rows_refs, switches, state, first, keep=True):
     top, total_sum, totals = state
     across, _, columns = turned_ref.shape
     rows = rows_refs[0].shape[2]
@@ -82,6 +82,7 @@
         key_pos = lax.broadcasted_iota(jnp.int32, (rows, 1), 0)
         column = lax.broadcasted_iota(jnp.int32, (1, columns), 1)
         causal = key_pos <= lax.rem(column, rows)
+    results = []
     for e in range(across):
         blocks = [
             logits[e][b // across][b % across * rows : (b % across + 1) * rows] for b in range(count)
@@ -112,9 +113,12 @@
             rescale = jnp.exp2(top[e] - new_top)
             block_sum = total_sum[e] * rescale + block_sum
             update = totals[e] * rescale + update
-        top[e] = new_top
-        total_sum[e] = block_sum
-        totals[e] = update
+        if keep:
+            top[e] = new_top
+            total_sum[e] = block_sum
+            totals[e] = update
+        results.append((block_sum, update))
+    return results
 
 
 def switch_of(flags_ref, e, owner, columns, allowed=None):
@@ -241,20 +245,16 @@
             ]
             for e in range(across)
         ]
-        rows_update(turned_ref, rows, switches, state, False)
-
-    for number, distance in enumerate(distances, 1):
-        here = (z >= distance) if number == len(distances) else (z == distance)
-        pl.when(here)(functools.partial(update, below[:number], distances[:number]))
-
-    if weight_at is not None:
-        weight_copy.wait()
-    if last:
+        results = rows_update(turned_ref, rows, switches, state, False, not last)
+        if last:
+            finish(results)
+
+    def finish(results):
         member_ref, inverse_ref, out_ref = refs
         rows = out_ref.shape[1]
         pooled = None
-        for e in range(across):
-            attended = (state[2][e] / state[1][e]).astype(jnp.bfloat16)
+        for e, (sums, totals) in enumerate(results):
+            attended = (totals * (1.0 / sums)).astype(jnp.bfloat16)
             part = lax.dot_general(
                 member_ref[e],
                 attended,
@@ -266,6 +266,18 @@
             mean = pooled[r * turns : (r + 1) * turns] * inverse_ref[...]
             for s in range(out_ref.shape[0]):
                 out_ref[s, :, r * HD : (r + 1) * HD] = mean[s * rows : (s + 1) * rows]
+
+    for number, distance in enumerate(distances, 1):
+        here = (z >= distance) if number == len(distances) else (z == distance)
+        pl.when(here)(functools.partial(update, below[:number], distances[:number]))
+    if last:
+
+        @pl.when(z < distances[0])
+        def _():
+            finish([(state[1][e], state[2][e]) for e in range(across)])
+
+    if weight_at is not None:
+        weight_copy.wait()
 
 
 def attend_next(across, distances, turns, turned, flags, below, state, pool, out_piece, weight, at, piece):
@@ -352,10 +364,13 @@
         return lax.ppermute(rows, "seq", pairs)
 
     _, y = place(across)
-    heads = []
-    for shift in range(across):
+    def head_of(shift):
         at = lax.rem(y + shift, across)
-        heads.append(pair(pick(key_states, at, across), pick(value_states, at, across)))
+        return pair(pick(key_states, at, across), pick(value_states, at, across))
+
+    heads = [head_of(shift) for shift in range(1, across)]
+    *heads, key_states, value_states = lax.optimization_barrier((*heads, key_states, value_states))
+    heads = [head_of(0)] + heads
     rows = join([heads[0]] + [over(heads[shift], shift) for shift in range(1, across)])
     rows, queries = lax.optimization_barrier((rows, queries))
     meta = lax.optimization_barrier(jnp.concatenate([turn_lengths, block_flags[0]]))

time: 40.5 us -> 41 us (1.012)
  other arithmetic: 3.5 us -> 5.22 us
  waiting for transfers between devices: 2.73 us -> 1.14 us
    select_n x2 -> x4, other arithmetic: 1.94 us -> 3.6 us  [pick(): jnp.where(number == part, rows[:, part * width:(part + 1) * width], picked)]
    ppermute x2, waiting for transfers between devices: 2.21 us -> 0.61 us  [over(): return lax.ppermute(rows, 'seq', pairs)]
  transfers between devices with their start and end apart: 6 -> 6, of which waited for: 3 -> 3; matrix products, arithmetic and copies ran while one was open for 5% -> 10% of each run, Pallas kernels for 18% -> 18%
where the time goes in v5:
time: 41 us; the launch traced here: 40.5 us
  blocking collectives  13.3 us (32%)
  starting transfers between devices  12.4 us (30%)
  Pallas kernels  8.2 us (20%)
  other arithmetic  5.22 us (13%)
  waiting for transfers between devices  1.14 us (3%)
    all_to_all x1, blocking collectives, on_device(): lax.all_to_all(state[0], 'seq', split_axis=0, concat_axis=0, tiled=True)  13.3 us
    ppermute x3, starting transfers between devices, up(): return lax.ppermute(rows, 'seq', pairs)  7.77 us
    ppermute x2, starting transfers between devices, over(): return lax.ppermute(rows, 'seq', pairs)  4.61 us
    select_n x4, other arithmetic, pick(): jnp.where(number == part, rows[:, part * width:(part + 1) * width], picked)  3.6 us
    pallas_call x3, Pallas kernels, attend_next(): call(functools.partial(next_kernel, across, distances, turns, last, at),...  3.51 us
    pallas_call x1, Pallas kernels, attend_first(): call(functools.partial(first_kernel, across), [jax.ShapeDtypeStruct((acro...  2.61 us
    pallas_call x2, Pallas kernels, project(): call(functools.partial(project_kernel, across, other), jax.ShapeDtypeStru...  1.34 us
  transfers between devices with their start and end apart: 6, of which 3 were waited for; matrix products, arithmetic and copies ran while one was open for 10% of the time, Pallas kernels for 18%

profile of v5, /device:TPU:0, one launch (start us, length us, event | category | flops | bytes accessed | tf_op | source)
XLA Modules:
  0.0 40.5 jit_solution(8728753413922392990)
XLA Ops:
  0.0 0.9 %slice_select_fusion.2 = (bf16[192,128]{1,0:T(8,128)(2,1)S(1)}, bf16[192,128]{1,0:T(8,128)(2,1)S(1)}) fusion(bf16[192,256]{1,0:T(8,128)(2,1)} %param.8, pred[]{:T(512)S(6)} %eq.19, bf16[192,256]{1,0:T(8,128)(2,1)} %param.7), kind=kLoop, calls=%fused_computation.7 | loop fusion | flops 49152 | bytes 294913 | tf_op jit(solution)/shard_map/jit(_where)/select_n | solution.py:49
  0.9 0.1 broadcast_select_fusion.3
  1.0 3.0 %collective-permute-start = (bf16[2,192,128]{2,1,0:T(8,128)(2,1)S(1)}, bf16[2,192,128]{2,1,0:T(8,128)(2,1)S(1)}, u32[]{:S(2)}, u32[]{:S(2)}) collective-permute-start(bf16[2,192,128]{2,1,0:T(8,128)(2,1)S(1)} %broadcast_select_fusion.3), channel_id=1, source_target_pairs={{0,2},{2,0},{4,6},{6,4},{8,10},{10,8},{12,14},{14,12},{1,3},{3,1},... | collective-permute-start | bytes 294920 | tf_op jit(solution)/shard_map/ppermute | solution.py:359
  4.0 0.7 %pad_add_fusion.meta_ref = s32[24]{0:T(128)S(1)} fusion(s32[8]{0:T(128)} %bitcast.1, s32[16]{0:T(128)} %param.10), kind=kLoop, calls=%fused_computation.9 | loop fusion | flops 24 | bytes 192 | tf_op jit(solution)/shard_map/concatenate | solution.py:376
  4.7 0.1 slice.35
  4.8 0.8 %slice_select_fusion.1 = bf16[192,128]{1,0:T(8,128)(2,1)S(1)} fusion(bf16[192,256]{1,0:T(8,128)(2,1)} %param.7, pred[]{:T(512)S(6)} %eq.17), kind=kLoop, calls=%fused_computation.6 | loop fusion | flops 24576 | bytes 147457 | tf_op jit(solution)/shard_map/jit(_where)/select_n | solution.py:49
  5.7 0.8 %slice_select_fusion = bf16[192,128]{1,0:T(8,128)(2,1)S(1)} fusion(bf16[192,256]{1,0:T(8,128)(2,1)} %param.8, pred[]{:T(512)S(6)} %eq.17), kind=kLoop, calls=%fused_computation.5 | loop fusion | flops 24576 | bytes 147457 | tf_op jit(solution)/shard_map/jit(_where)/select_n | solution.py:49
  6.5 0.1 broadcast_select_fusion.2.refs_0_
  6.6 0.1 pad.6.clone
  6.6 0.1 collective-permute-done.refs_1_
  6.8 3.8 %collective-permute-start.2 = (bf16[2,2,192,128]{3,2,1,0:T(8,128)(2,1)S(1)}, bf16[2,2,192,128]{3,2,1,0:T(8,128)(2,1)S(1)}, u32[]{:S(2)}, u32[]{:S(2)}) collective-permute-start(bf16[2,2,192,128]{3,2,1,0:T(8,128)(2,1)S(1)} %shard_map.64.refs_2_), channel_id=1, source_target_pairs={{0,4},{2,6},{4,8},{6,10},{8,12},{10,14},{1,5},{3,7},{5,9},{7,11},{... | collective-permute-start | bytes 589832 | tf_op jit(solution)/shard_map/ppermute | solution.py:364
  10.6 1.1 %broadcast_select_fusion = (bf16[192,512]{1,0:T(8,128)(2,1)S(1)}, bf16[192,512]{1,0:T(8,128)(2,1)S(1)}) fusion(pred[]{:T(512)S(6)} %eq.19, bf16[192,1024]{1,0:T(8,128)(2,1)} %param.6, pred[]{:T(512)S(6)} %eq.17), kind=kLoop, calls=%fused_computation.1 | loop fusion | flops 196608 | bytes 786434 | tf_op jit(solution)/shard_map/jit(_where)/select_n | solution.py:49
  11.7 0.7 %shard_map.65 = (bf16[2,64,768]{2,1,0:T(8,128)(2,1)S(1)}, f32[16,128]{1,0:T(8,128)S(1)}) custom-call(s32[24]{0:T(128)S(1)} %pad_add_fusion.meta_ref, bf16[192,512]{1,0:T(8,128)(2,1)S(1)} %get-tuple-element.54.after_ref.refs_0_), custom_call_target="tpu_custom_call" | custom-call | flops 1024 | bytes 1024 | tf_op jit(solution)/shard_map/pallas_call | solution.py:161
  12.4 0.1 pad_maximum_fusion
  12.5 1.6 %collective-permute-start.1 = (bf16[208,512]{1,0:T(8,128)(2,1)S(1)}, bf16[208,512]{1,0:T(8,128)(2,1)S(1)}, u32[]{:S(2)}, u32[]{:S(2)}) collective-permute-start(bf16[208,512]{1,0:T(8,128)(2,1)S(1)} %pad_maximum_fusion), channel_id=1, source_target_pairs={{0,2},{2,0},{4,6},{6,4},{8,10},{10,8},{12,14},{14,12},{1,3},{3,1},... | collective-permute-start | bytes 638984 | tf_op jit(solution)/shard_map/ppermute | solution.py:359
  14.1 3.3 %collective-permute-start.4 = (bf16[2,2,192,128]{3,2,1,0:T(8,128)(2,1)S(1)}, bf16[2,2,192,128]{3,2,1,0:T(8,128)(2,1)S(1)}, u32[]{:S(2)}, u32[]{:S(2)}) collective-permute-start(bf16[2,2,192,128]{3,2,1,0:T(8,128)(2,1)S(1)} %shard_map.64.refs_2_), channel_id=1, source_target_pairs={{0,12},{2,14},{1,13},{3,15},{16,28},{18,30},{17,29},{19,31}} | collective-permute-start | bytes 589832 | tf_op jit(solution)/shard_map/ppermute | solution.py:364
  17.4 0.0 collective-permute-done.2.refs_0_
  17.4 0.7 %collective-permute-start.3 = (bf16[2,2,192,128]{3,2,1,0:T(8,128)(2,1)S(1)}, bf16[2,2,192,128]{3,2,1,0:T(8,128)(2,1)S(1)}, u32[]{:S(2)}, u32[]{:S(2)}) collective-permute-start(bf16[2,2,192,128]{3,2,1,0:T(8,128)(2,1)S(1)} %collective-permute-done.2.refs_0_), channel_id=1, source_target_pairs={{4,8},{6,10},{8,12},{10,14},{5,9},{7,11},{9,13},{11,15},{20,24},{2... | collective-permute-start | bytes 589832 | tf_op jit(solution)/shard_map/ppermute | solution.py:364
  18.1 0.5 %collective-permute-done.1.refs_1_ = bf16[208,512]{1,0:T(8,128)(2,1)S(1)} collective-permute-done((bf16[208,512]{1,0:T(8,128)(2,1)S(1)}, bf16[208,512]{1,0:T(8,128)(2,1)S(1)}, u32[]{:S(2)}, u32[]{:S(2)}) %collective-permute-start.1) | collective-permute-done | bytes 213024 | tf_op jit(solution)/shard_map/ppermute | solution.py:359
  18.6 0.1 broadcast_in_dim.41.own_flags_ref
  18.6 2.6 %shard_map.66 = (bf16[2,128,768]{2,1,0:T(8,128)(2,1)S(1)}, f32[2,16,128]{2,1,0:T(8,128)S(1)}, bf16[512,4096]{1,0:T(8,128)(2,1)S(1)}, f32[2,1,768]{2,1,0:T(1,128)...) custom-call(f32[16,128]{1,0:T(8,128)S(1)} %broadcast_in_dim.41.own_flags_ref, ...), custom_call_target="tpu_custom_call" | custom-call | flops 1024 | bytes 1024 | tf_op jit(solution)/shard_map/pallas_call | solution.py:212
  21.2 1.6 %shard_map.67 = (f32[2,1,768]{2,1,0:T(1,128)S(1)}, f32[2,1,768]{2,1,0:T(1,128)S(1)}, f32[2,128,768]{2,1,0:T(8,128)S(1)}, bf16[256,4096]{1,0:T(8,128)(2,1)S(1)}) custom-call(f32[2,16,128]{2,1,0:T(8,128)S(1)} %get-tuple-element.36.flags_ref, ...), custom_call_target="tpu_custom_call", output_to_operand_aliasing={{0}: (3, {}), {1}: (4, {}), {2}: (5, {})} | custom-call | flops 1024 | bytes 1024 | tf_op jit(solution)/shard_map/pallas_call | solution.py:301
  22.9 0.0 collective-permute-done.4.refs_0_
  22.9 1.6 %shard_map.68 = (f32[2,1,768]{2,1,0:T(1,128)S(1)}, f32[2,1,768]{2,1,0:T(1,128)S(1)}, f32[2,128,768]{2,1,0:T(8,128)S(1)}, bf16[256,4096]{1,0:T(8,128)(2,1)S(1)}) custom-call(f32[2,16,128]{2,1,0:T(8,128)S(1)} %get-tuple-element.36.flags_ref, ...), custom_call_target="tpu_custom_call", output_to_operand_aliasing={{0}: (3, {}), {1}: (4, {}), {2}: (5, {})} | custom-call | flops 1024 | bytes 1024 | tf_op jit(solution)/shard_map/pallas_call | solution.py:301
  24.5 0.0 collective-permute-done.3.refs_0_
  24.5 0.3 shard_map.69
  24.8 13.3 %all_to_all.5.parts_ref = f32[8,2,512]{2,1,0:T(2,128)S(1)} all-to-all(f32[8,2,512]{2,1,0:T(2,128)S(1)} %shard_map.69), channel_id=1, replica_groups=mesh['conv'=2,'seq'=8,'head'=2] {'seq'}, dimensions={0} | all-to-all | bytes 65536 | tf_op jit(solution)/shard_map/all_to_all | solution.py:421
  38.1 0.7 %shard_map.71 = f32[2,2048]{1,0:T(2,128)S(1)} custom-call(f32[8,2,512]{2,1,0:T(2,128)S(1)} %all_to_all.5.parts_ref, bf16[512,4096]{1,0:T(8,128)(2,1)S(1)} %get-tuple-element.50.refs_0_, bf16[256,4096]{1,0:T(8,128)(2,1)S(1)} %get-tuple-element.51.refs_1_, bf16[256,4096]{1,0:T(8,128)(2,1)S(1)} %get-tuple-element.52.refs_2_), custom_call_target="tpu_custom_call" | custom-call | flops 1024 | bytes 1024 | tf_op jit(solution)/shard_map/pallas_call | solution.py:345
  38.7 0.0 collective-permute-start.5
  38.7 0.7 %shard_map.70 = f32[2,2048]{1,0:T(2,128)S(1)} custom-call(f32[8,2,512]{2,1,0:T(2,128)S(1)} %all_to_all.5.parts_ref, bf16[512,4096]{1,0:T(8,128)(2,1)S(1)} %get-tuple-element.50.refs_0_, bf16[256,4096]{1,0:T(8,128)(2,1)S(1)} %get-tuple-element.51.refs_1_, bf16[256,4096]{1,0:T(8,128)(2,1)S(1)} %get-tuple-element.52.refs_2_), custom_call_target="tpu_custom_call" | custom-call | flops 1024 | bytes 1024 | tf_op jit(solution)/shard_map/pallas_call | solution.py:345
  39.4 0.5 %collective-permute-done.5 = f32[2,2048]{1,0:T(2,128)S(1)} collective-permute-done((f32[2,2048]{1,0:T(2,128)S(1)}, f32[2,2048]{1,0:T(2,128)S(1)}, u32[]{:S(2)}, u32[]{:S(2)}) %collective-permute-start.5) | collective-permute-done | bytes 16416 | tf_op jit(solution)/shard_map/ppermute | solution.py:423
  39.9 0.6 %add.10 = f32[2,2048]{1,0:T(2,128)} add(f32[2,2048]{1,0:T(2,128)S(1)} %shard_map.70, f32[2,2048]{1,0:T(2,128)S(1)} %collective-permute-done.5) | non-fusion elementwise | flops 4096 | bytes 49152 | tf_op jit(solution)/shard_map/add | solution.py:424
  (3 shorter events, 0.0 us)
Async XLA Ops:
  1.0 5.8 %collective-permute-start = (bf16[2,192,128]{2,1,0:T(8,128)(2,1)S(1)}, bf16[2,192,128]{2,1,0:T(8,128)(2,1)S(1)}, u32[]{:S(2)}, u32[]{:S(2)}) collective-permute-start(bf16[2,192,128]{2,1,0:T(8,128)(2,1)S(1)} %broadcast_select_fusion.3), channel_id=1, source_target_pairs={{0,2},{2,0},{4,6},{6,4},{8,10},{10,8},{12,14},{14,12},{1,3},{3,1},... | collective-permute-start | bytes 294920 | tf_op jit(solution)/shard_map/ppermute | solution.py:359
  6.8 10.6 %collective-permute-start.2 = (bf16[2,2,192,128]{3,2,1,0:T(8,128)(2,1)S(1)}, bf16[2,2,192,128]{3,2,1,0:T(8,128)(2,1)S(1)}, u32[]{:S(2)}, u32[]{:S(2)}) collective-permute-start(bf16[2,2,192,128]{3,2,1,0:T(8,128)(2,1)S(1)} %shard_map.64.refs_2_), channel_id=1, source_target_pairs={{0,4},{2,6},{4,8},{6,10},{8,12},{10,14},{1,5},{3,7},{5,9},{7,11},{... | collective-permute-start | bytes 589832 | tf_op jit(solution)/shard_map/ppermute | solution.py:364
  12.5 6.0 %collective-permute-start.1 = (bf16[208,512]{1,0:T(8,128)(2,1)S(1)}, bf16[208,512]{1,0:T(8,128)(2,1)S(1)}, u32[]{:S(2)}, u32[]{:S(2)}) collective-permute-start(bf16[208,512]{1,0:T(8,128)(2,1)S(1)} %pad_maximum_fusion), channel_id=1, source_target_pairs={{0,2},{2,0},{4,6},{6,4},{8,10},{10,8},{12,14},{14,12},{1,3},{3,1},... | collective-permute-start | bytes 638984 | tf_op jit(solution)/shard_map/ppermute | solution.py:359
  14.1 8.8 %collective-permute-start.4 = (bf16[2,2,192,128]{3,2,1,0:T(8,128)(2,1)S(1)}, bf16[2,2,192,128]{3,2,1,0:T(8,128)(2,1)S(1)}, u32[]{:S(2)}, u32[]{:S(2)}) collective-permute-start(bf16[2,2,192,128]{3,2,1,0:T(8,128)(2,1)S(1)} %shard_map.64.refs_2_), channel_id=1, source_target_pairs={{0,12},{2,14},{1,13},{3,15},{16,28},{18,30},{17,29},{19,31}} | collective-permute-start | bytes 589832 | tf_op jit(solution)/shard_map/ppermute | solution.py:364
  17.4 7.1 %collective-permute-start.3 = (bf16[2,2,192,128]{3,2,1,0:T(8,128)(2,1)S(1)}, bf16[2,2,192,128]{3,2,1,0:T(8,128)(2,1)S(1)}, u32[]{:S(2)}, u32[]{:S(2)}) collective-permute-start(bf16[2,2,192,128]{3,2,1,0:T(8,128)(2,1)S(1)} %collective-permute-done.2.refs_0_), channel_id=1, source_target_pairs={{4,8},{6,10},{8,12},{10,14},{5,9},{7,11},{9,13},{11,15},{20,24},{2... | collective-permute-start | bytes 589832 | tf_op jit(solution)/shard_map/ppermute | solution.py:364
  38.7 1.2 %collective-permute-start.5 = (f32[2,2048]{1,0:T(2,128)S(1)}, f32[2,2048]{1,0:T(2,128)S(1)}, u32[]{:S(2)}, u32[]{:S(2)}) collective-permute-start(f32[2,2048]{1,0:T(2,128)S(1)} %shard_map.71), channel_id=1, source_target_pairs={{0,1},{1,0},{2,3},{3,2},{4,5},{5,4},{6,7},{7,6},{8,9},{9,8},{10,11... | collective-permute-start | bytes 49160 | tf_op jit(solution)/shard_map/ppermute | solution.py:423

commit v6 on v3

--- a/solution.py
+++ b/solution.py
@@ -57,23 +57,35 @@
 
 def join_kernel(*refs):
     *parts, out_ref = refs
-    for e, part in enumerate(parts):
-        out_ref[e] = part[...]
-
-
-def join(parts):
-    shape = jax.ShapeDtypeStruct((len(parts),) + parts[0].shape, parts[0].dtype)
+    at = 0
+    for part in parts:
+        size = min(part.shape[0], out_ref.shape[0] - at)
+        out_ref[at : at + size] = part[:size]
+        at += size
+
+
+def join_parts(parts, count):
+    return join(parts, count)
+
+
+def join(parts, count=None):
+    count = sum(part.shape[0] for part in parts) if count is None else count
+    shape = jax.ShapeDtypeStruct((count,) + parts[0].shape[1:], parts[0].dtype)
     return call(join_kernel, shape, in_specs=[in_vmem] * len(parts))(*parts)
 
 
 def rows_update(turned_ref, rows_refs, switches, state, first):
     top, total_sum, totals = state
     across, _, columns = turned_ref.shape
-    rows = rows_refs[0].shape[2]
+    rows = rows_refs[0].shape[1]
     count = across * len(rows_refs)
     factor = log_two_e / math.sqrt(HD)
-    keys = [kv_ref[:, 0].reshape(across * rows, HD) for kv_ref in rows_refs]
-    values = [kv_ref[:, 1].reshape(across * rows, HD).T for kv_ref in rows_refs]
+    keys = [
+        jnp.concatenate([kv_ref[2 * e] for e in range(across)], axis=0) for kv_ref in rows_refs
+    ]
+    values = [
+        jnp.concatenate([kv_ref[2 * e + 1] for e in range(across)], axis=0).T for kv_ref in rows_refs
+    ]
     logits = [
         [jnp.dot(part, turned_ref[e], preferred_element_type=jnp.float32) for part in keys]
         for e in range(across)
@@ -176,7 +188,7 @@
     weight_copy = weight_piece(weight_ref, weight_out, 0, copied)
     weight_copy.start()
     z, y = place(across)
-    q_rows = kv_ref.shape[2]
+    q_rows = kv_ref.shape[1]
     repeat = queries[0].shape[1] // HD
     columns = repeat * q_rows
     for e in range(across):
@@ -201,7 +213,7 @@
 
 
 def attend_first(across, flags, queries, rows, weight, piece):
-    q_rows = rows.shape[2]
+    q_rows = rows.shape[1]
     repeat = queries[0].shape[1] // HD
     columns = repeat * q_rows
     f32, b16 = jnp.float32, jnp.bfloat16
@@ -356,7 +368,10 @@
     for shift in range(across):
         at = lax.rem(y + shift, across)
         heads.append(pair(pick(key_states, at, across), pick(value_states, at, across)))
-    rows = join([heads[0]] + [over(heads[shift], shift) for shift in range(1, across)])
+    swapped = [over(heads[shift], shift) for shift in range(1, across)]
+    rows = join([heads[0]] + swapped)
+    first = up(heads[0], 1)
+    rest = up(join(swapped), 1)
     rows, queries = lax.optimization_barrier((rows, queries))
     meta = lax.optimization_barrier(jnp.concatenate([turn_lengths, block_flags[0]]))
     padded = -(-count // 16) * 16
@@ -367,14 +382,15 @@
         under = jnp.broadcast_to(flags, (padded, group.shape[1])).astype(group.dtype)
         sent.append(jnp.concatenate([group, under], axis=0))
     flags = jnp.broadcast_to(flags, (padded, HD)).astype(jnp.float32)
-    below = [rows, up(rows, 1)] + [None] * (down - 2)
-    member, inverse = members(across, turns, meta, groups[0])
-    far, inverse, *sent = lax.optimization_barrier((rows, inverse, *sent))
+    below = [rows, join_parts([first, rest], 2 * across)] + [None] * (down - 2)
+    far, *sent = lax.optimization_barrier((rows, *sent))
     others = [over(group, shift) for shift, group in enumerate(sent, 1)]
     for distance in range(3, down):
         below[distance] = up(far, distance)
     if down > 2:
         below[2] = up(below[1], 1, 1)
+    member, inverse = members(across, turns, meta, groups[0])
+    inverse, flags = lax.optimization_barrier((inverse, flags))
     depth = out_weight.shape[0]
     pieces = [4 * depth // 8, 2 * depth // 8, 2 * depth // 8]
     turned, flags, weight, *state = attend_first(

time: 40.5 us -> 39.8 us (0.983)
  starting transfers between devices: 12.4 us -> 14.3 us
  blocking collectives: 13 us -> 11.5 us
  waiting for transfers between devices: 2.73 us -> 1.61 us
    ppermute x3 -> x4, starting transfers between devices: 7.77 us -> 10.7 us  [up(): return lax.ppermute(rows, 'seq', pairs)]
    all_to_all x1, blocking collectives: 13 us -> 11.5 us  [on_device(): lax.all_to_all(state[0], 'seq', split_axis=0, concat_axis=0, tiled=True)]
    ppermute x2, waiting for transfers between devices: 2.21 us -> 1.08 us  [over(): return lax.ppermute(rows, 'seq', pairs)]
    ppermute x2, starting transfers between devices: 4.62 us -> 3.6 us  [over(): return lax.ppermute(rows, 'seq', pairs)]
  transfers between devices with their start and end apart: 6 -> 7, of which waited for: 3 -> 2; matrix products, arithmetic and copies ran while one was open for 5% -> 5% of each run, Pallas kernels for 18% -> 18%
where the time goes in v6:
time: 39.8 us; the launch traced here: 39.4 us
  starting transfers between devices  14.3 us (36%)
  blocking collectives  11.5 us (29%)
  Pallas kernels  8.21 us (21%)
  other arithmetic  3.5 us (9%)
  waiting for transfers between devices  1.61 us (4%)
    all_to_all x1, blocking collectives, on_device(): lax.all_to_all(state[0], 'seq', split_axis=0, concat_axis=0, tiled=True)  11.5 us
    ppermute x4, starting transfers between devices, up(): return lax.ppermute(rows, 'seq', pairs)  10.7 us
    ppermute x2, starting transfers between devices, over(): return lax.ppermute(rows, 'seq', pairs)  3.6 us
    pallas_call x3, Pallas kernels, attend_next(): call(functools.partial(next_kernel, across, distances, turns, last, at),...  3.5 us
    pallas_call x1, Pallas kernels, attend_first(): call(functools.partial(first_kernel, across), [jax.ShapeDtypeStruct((acro...  2.6 us
    select_n x2, other arithmetic, pick(): jnp.where(number == part, rows[:, part * width:(part + 1) * width], picked)  1.94 us
    pallas_call x2, Pallas kernels, project(): call(functools.partial(project_kernel, across, other), jax.ShapeDtypeStru...  1.34 us
    ppermute x2, waiting for transfers between devices, over(): return lax.ppermute(rows, 'seq', pairs)  1.08 us
  transfers between devices with their start and end apart: 7, of which 2 were waited for; matrix products, arithmetic and copies ran while one was open for 5% of the time, Pallas kernels for 18%

profile of v6, /device:TPU:0, one launch (start us, length us, event | category | flops | bytes accessed | tf_op | source)
XLA Modules:
  0.0 39.4 jit_solution(232234808896711996)
XLA Ops:
  0.0 0.9 %broadcast_select_fusion.4 = (bf16[192,128]{1,0:T(8,128)(2,1)S(1)}, bf16[192,128]{1,0:T(8,128)(2,1)S(1)}, bf16[192,128]{1,0:T(8,128)(2,1)S(1)}, bf16[192,128]{1,0:T(8,128)(2,1)S(1)}) fusion(pred[]{:T(512)S(6)} %eq.19, bf16[192,256]{1,0:T(8,128)(2,1)} %param.8, pred[]{:T(512)S(6)} %eq.17, bf16[192,256]{1,0:T(8,128)(2,1)} %param.7), kind=kLoop, calls=%fused_computation.5 | loop fusion | flops 98304 | bytes 393218 | tf_op jit(solution)/shard_map/jit(_where)/select_n | solution.py:49
  0.9 0.1 broadcast_select_fusion.2
  1.0 3.0 %collective-permute-start = (bf16[2,192,128]{2,1,0:T(8,128)(2,1)S(1)}, bf16[2,192,128]{2,1,0:T(8,128)(2,1)S(1)}, u32[]{:S(2)}, u32[]{:S(2)}) collective-permute-start(bf16[2,192,128]{2,1,0:T(8,128)(2,1)S(1)} %get-tuple-element.57), channel_id=1, source_target_pairs={{0,2},{2,0},{4,6},{6,4},{8,10},{10,8},{12,14},{14,12},{1,3},{3,1},... | collective-permute-start | bytes 294920 | tf_op jit(solution)/shard_map/ppermute | solution.py:359
  4.0 3.5 %collective-permute-start.2 = (bf16[2,192,128]{2,1,0:T(8,128)(2,1)S(1)}, bf16[2,192,128]{2,1,0:T(8,128)(2,1)S(1)}, u32[]{:S(2)}, u32[]{:S(2)}) collective-permute-start(bf16[2,192,128]{2,1,0:T(8,128)(2,1)S(1)} %get-tuple-element.58.refs_0_), channel_id=1, source_target_pairs={{0,4},{2,6},{4,8},{6,10},{8,12},{10,14},{1,5},{3,7},{5,9},{7,11},{... | collective-permute-start | bytes 294920 | tf_op jit(solution)/shard_map/ppermute | solution.py:364
  7.5 0.7 %pad_add_fusion.meta_ref = s32[24]{0:T(128)S(1)} fusion(s32[8]{0:T(128)} %bitcast.1, s32[16]{0:T(128)} %param.10), kind=kLoop, calls=%fused_computation.9 | loop fusion | flops 24 | bytes 192 | tf_op jit(solution)/shard_map/concatenate | solution.py:376
  8.3 0.1 slice.33
  8.3 0.1 pad.6.clone
  8.4 0.0 collective-permute-done.refs_1_.refs_0_
  8.4 3.5 %collective-permute-start.3 = (bf16[2,192,128]{2,1,0:T(8,128)(2,1)S(1)}, bf16[2,192,128]{2,1,0:T(8,128)(2,1)S(1)}, u32[]{:S(2)}, u32[]{:S(2)}) collective-permute-start(bf16[2,192,128]{2,1,0:T(8,128)(2,1)S(1)} %shard_map.67), channel_id=1, source_target_pairs={{0,4},{2,6},{4,8},{6,10},{8,12},{10,14},{1,5},{3,7},{5,9},{7,11},{... | collective-permute-start | bytes 294920 | tf_op jit(solution)/shard_map/ppermute | solution.py:364
  11.9 1.1 %broadcast_select_fusion = (bf16[192,512]{1,0:T(8,128)(2,1)S(1)}, bf16[192,512]{1,0:T(8,128)(2,1)S(1)}) fusion(pred[]{:T(512)S(6)} %eq.19, bf16[192,1024]{1,0:T(8,128)(2,1)} %param.6, pred[]{:T(512)S(6)} %eq.17), kind=kLoop, calls=%fused_computation.1 | loop fusion | flops 196608 | bytes 786434 | tf_op jit(solution)/shard_map/jit(_where)/select_n | solution.py:49
  13.0 0.1 pad_maximum_fusion
  13.1 0.6 %collective-permute-start.1 = (bf16[208,512]{1,0:T(8,128)(2,1)S(1)}, bf16[208,512]{1,0:T(8,128)(2,1)S(1)}, u32[]{:S(2)}, u32[]{:S(2)}) collective-permute-start(bf16[208,512]{1,0:T(8,128)(2,1)S(1)} %pad_maximum_fusion), channel_id=1, source_target_pairs={{0,2},{2,0},{4,6},{6,4},{8,10},{10,8},{12,14},{14,12},{1,3},{3,1},... | collective-permute-start | bytes 638984 | tf_op jit(solution)/shard_map/ppermute | solution.py:359
  13.7 3.0 %collective-permute-start.5 = (bf16[4,192,128]{2,1,0:T(8,128)(2,1)S(1)}, bf16[4,192,128]{2,1,0:T(8,128)(2,1)S(1)}, u32[]{:S(2)}, u32[]{:S(2)}) collective-permute-start(bf16[4,192,128]{2,1,0:T(8,128)(2,1)S(1)} %shard_map.64.refs_2_), channel_id=1, source_target_pairs={{0,12},{2,14},{1,13},{3,15},{16,28},{18,30},{17,29},{19,31}} | collective-permute-start | bytes 589832 | tf_op jit(solution)/shard_map/ppermute | solution.py:364
  16.7 0.0 collective-permute-done.2.refs_0_
  16.7 0.0 collective-permute-done.3.refs_1_
  16.8 0.7 %collective-permute-start.4 = (bf16[4,192,128]{2,1,0:T(8,128)(2,1)S(1)}, bf16[4,192,128]{2,1,0:T(8,128)(2,1)S(1)}, u32[]{:S(2)}, u32[]{:S(2)}) collective-permute-start(bf16[4,192,128]{2,1,0:T(8,128)(2,1)S(1)} %shard_map.68.refs_0_), channel_id=1, source_target_pairs={{4,8},{6,10},{8,12},{10,14},{5,9},{7,11},{9,13},{11,15},{20,24},{2... | collective-permute-start | bytes 589832 | tf_op jit(solution)/shard_map/ppermute | solution.py:364
  17.4 0.7 %shard_map.65 = (bf16[2,64,768]{2,1,0:T(8,128)(2,1)S(1)}, f32[16,128]{1,0:T(8,128)S(1)}) custom-call(s32[24]{0:T(128)S(1)} %pad_add_fusion.meta_ref, bf16[192,512]{1,0:T(8,128)(2,1)S(1)} %get-tuple-element.50.after_ref.refs_0_), custom_call_target="tpu_custom_call" | custom-call | flops 1024 | bytes 1024 | tf_op jit(solution)/shard_map/pallas_call | solution.py:169
  18.2 0.1 broadcast_in_dim.45.own_flags_ref
  18.2 1.1 %collective-permute-done.1.refs_1_ = bf16[208,512]{1,0:T(8,128)(2,1)S(1)} collective-permute-done((bf16[208,512]{1,0:T(8,128)(2,1)S(1)}, bf16[208,512]{1,0:T(8,128)(2,1)S(1)}, u32[]{:S(2)}, u32[]{:S(2)}) %collective-permute-start.1) | collective-permute-done | bytes 213024 | tf_op jit(solution)/shard_map/ppermute | solution.py:359
  19.3 2.6 %shard_map.66 = (bf16[2,128,768]{2,1,0:T(8,128)(2,1)S(1)}, f32[2,16,128]{2,1,0:T(8,128)S(1)}, bf16[512,4096]{1,0:T(8,128)(2,1)S(1)}, f32[2,1,768]{2,1,0:T(1,128)...) custom-call(f32[16,128]{1,0:T(8,128)S(1)} %broadcast_in_dim.45.own_flags_ref, ...), custom_call_target="tpu_custom_call" | custom-call | flops 1024 | bytes 1024 | tf_op jit(solution)/shard_map/pallas_call | solution.py:220
  21.9 1.6 %shard_map.69 = (f32[2,1,768]{2,1,0:T(1,128)S(1)}, f32[2,1,768]{2,1,0:T(1,128)S(1)}, f32[2,128,768]{2,1,0:T(8,128)S(1)}, bf16[256,4096]{1,0:T(8,128)(2,1)S(1)}) custom-call(f32[2,16,128]{2,1,0:T(8,128)S(1)} %get-tuple-element.32.flags_ref, ...), custom_call_target="tpu_custom_call", output_to_operand_aliasing={{0}: (3, {}), {1}: (4, {}), {2}: (5, {})} | custom-call | flops 1024 | bytes 1024 | tf_op jit(solution)/shard_map/pallas_call | solution.py:301
  23.5 0.0 collective-permute-done.5.refs_0_
  23.6 1.6 %shard_map.70 = (f32[2,1,768]{2,1,0:T(1,128)S(1)}, f32[2,1,768]{2,1,0:T(1,128)S(1)}, f32[2,128,768]{2,1,0:T(8,128)S(1)}, bf16[256,4096]{1,0:T(8,128)(2,1)S(1)}) custom-call(f32[2,16,128]{2,1,0:T(8,128)S(1)} %get-tuple-element.32.flags_ref, ...), custom_call_target="tpu_custom_call", output_to_operand_aliasing={{0}: (3, {}), {1}: (4, {}), {2}: (5, {})} | custom-call | flops 1024 | bytes 1024 | tf_op jit(solution)/shard_map/pallas_call | solution.py:301
  25.2 0.0 collective-permute-done.4.refs_0_
  25.2 0.3 shard_map.71
  25.5 11.5 %all_to_all.5.parts_ref = f32[8,2,512]{2,1,0:T(2,128)S(1)} all-to-all(f32[8,2,512]{2,1,0:T(2,128)S(1)} %shard_map.71), channel_id=1, replica_groups=mesh['conv'=2,'seq'=8,'head'=2] {'seq'}, dimensions={0} | all-to-all | bytes 65536 | tf_op jit(solution)/shard_map/all_to_all | solution.py:422
  37.0 0.7 %shard_map.73 = f32[2,2048]{1,0:T(2,128)S(1)} custom-call(f32[8,2,512]{2,1,0:T(2,128)S(1)} %all_to_all.5.parts_ref, bf16[512,4096]{1,0:T(8,128)(2,1)S(1)} %get-tuple-element.46.refs_0_, bf16[256,4096]{1,0:T(8,128)(2,1)S(1)} %get-tuple-element.47.refs_1_, bf16[256,4096]{1,0:T(8,128)(2,1)S(1)} %get-tuple-element.48.refs_2_), custom_call_target="tpu_custom_call" | custom-call | flops 1024 | bytes 1024 | tf_op jit(solution)/shard_map/pallas_call | solution.py:345
  37.6 0.0 collective-permute-start.6
  37.6 0.7 %shard_map.72 = f32[2,2048]{1,0:T(2,128)S(1)} custom-call(f32[8,2,512]{2,1,0:T(2,128)S(1)} %all_to_all.5.parts_ref, bf16[512,4096]{1,0:T(8,128)(2,1)S(1)} %get-tuple-element.46.refs_0_, bf16[256,4096]{1,0:T(8,128)(2,1)S(1)} %get-tuple-element.47.refs_1_, bf16[256,4096]{1,0:T(8,128)(2,1)S(1)} %get-tuple-element.48.refs_2_), custom_call_target="tpu_custom_call" | custom-call | flops 1024 | bytes 1024 | tf_op jit(solution)/shard_map/pallas_call | solution.py:345
  38.3 0.5 %collective-permute-done.6 = f32[2,2048]{1,0:T(2,128)S(1)} collective-permute-done((f32[2,2048]{1,0:T(2,128)S(1)}, f32[2,2048]{1,0:T(2,128)S(1)}, u32[]{:S(2)}, u32[]{:S(2)}) %collective-permute-start.6) | collective-permute-done | bytes 16416 | tf_op jit(solution)/shard_map/ppermute | solution.py:424
  38.8 0.6 %add.10 = f32[2,2048]{1,0:T(2,128)} add(f32[2,2048]{1,0:T(2,128)S(1)} %shard_map.72, f32[2,2048]{1,0:T(2,128)S(1)} %collective-permute-done.6) | non-fusion elementwise | flops 4096 | bytes 49152 | tf_op jit(solution)/shard_map/add | solution.py:425
  (5 shorter events, 0.1 us)
Async XLA Ops:
  1.0 7.4 %collective-permute-start = (bf16[2,192,128]{2,1,0:T(8,128)(2,1)S(1)}, bf16[2,192,128]{2,1,0:T(8,128)(2,1)S(1)}, u32[]{:S(2)}, u32[]{:S(2)}) collective-permute-start(bf16[2,192,128]{2,1,0:T(8,128)(2,1)S(1)} %get-tuple-element.57), channel_id=1, source_target_pairs={{0,2},{2,0},{4,6},{6,4},{8,10},{10,8},{12,14},{14,12},{1,3},{3,1},... | collective-permute-start | bytes 294920 | tf_op jit(solution)/shard_map/ppermute | solution.py:359
  4.0 12.7 %collective-permute-start.2 = (bf16[2,192,128]{2,1,0:T(8,128)(2,1)S(1)}, bf16[2,192,128]{2,1,0:T(8,128)(2,1)S(1)}, u32[]{:S(2)}, u32[]{:S(2)}) collective-permute-start(bf16[2,192,128]{2,1,0:T(8,128)(2,1)S(1)} %get-tuple-element.58.refs_0_), channel_id=1, source_target_pairs={{0,4},{2,6},{4,8},{6,10},{8,12},{10,14},{1,5},{3,7},{5,9},{7,11},{... | collective-permute-start | bytes 294920 | tf_op jit(solution)/shard_map/ppermute | solution.py:364
  8.4 8.3 %collective-permute-start.3 = (bf16[2,192,128]{2,1,0:T(8,128)(2,1)S(1)}, bf16[2,192,128]{2,1,0:T(8,128)(2,1)S(1)}, u32[]{:S(2)}, u32[]{:S(2)}) collective-permute-start(bf16[2,192,128]{2,1,0:T(8,128)(2,1)S(1)} %shard_map.67), channel_id=1, source_target_pairs={{0,4},{2,6},{4,8},{6,10},{8,12},{10,14},{1,5},{3,7},{5,9},{7,11},{... | collective-permute-start | bytes 294920 | tf_op jit(solution)/shard_map/ppermute | solution.py:364
  13.1 6.2 %collective-permute-start.1 = (bf16[208,512]{1,0:T(8,128)(2,1)S(1)}, bf16[208,512]{1,0:T(8,128)(2,1)S(1)}, u32[]{:S(2)}, u32[]{:S(2)}) collective-permute-start(bf16[208,512]{1,0:T(8,128)(2,1)S(1)} %pad_maximum_fusion), channel_id=1, source_target_pairs={{0,2},{2,0},{4,6},{6,4},{8,10},{10,8},{12,14},{14,12},{1,3},{3,1},... | collective-permute-start | bytes 638984 | tf_op jit(solution)/shard_map/ppermute | solution.py:359
  13.7 9.9 %collective-permute-start.5 = (bf16[4,192,128]{2,1,0:T(8,128)(2,1)S(1)}, bf16[4,192,128]{2,1,0:T(8,128)(2,1)S(1)}, u32[]{:S(2)}, u32[]{:S(2)}) collective-permute-start(bf16[4,192,128]{2,1,0:T(8,128)(2,1)S(1)} %shard_map.64.refs_2_), channel_id=1, source_target_pairs={{0,12},{2,14},{1,13},{3,15},{16,28},{18,30},{17,29},{19,31}} | collective-permute-start | bytes 589832 | tf_op jit(solution)/shard_map/ppermute | solution.py:364
  16.8 8.4 %collective-permute-start.4 = (bf16[4,192,128]{2,1,0:T(8,128)(2,1)S(1)}, bf16[4,192,128]{2,1,0:T(8,128)(2,1)S(1)}, u32[]{:S(2)}, u32[]{:S(2)}) collective-permute-start(bf16[4,192,128]{2,1,0:T(8,128)(2,1)S(1)} %shard_map.68.refs_0_), channel_id=1, source_target_pairs={{4,8},{6,10},{8,12},{10,14},{5,9},{7,11},{9,13},{11,15},{20,24},{2... | collective-permute-start | bytes 589832 | tf_op jit(solution)/shard_map/ppermute | solution.py:364
  37.6 1.2 %collective-permute-start.6 = (f32[2,2048]{1,0:T(2,128)S(1)}, f32[2,2048]{1,0:T(2,128)S(1)}, u32[]{:S(2)}, u32[]{:S(2)}) collective-permute-start(f32[2,2048]{1,0:T(2,128)S(1)} %shard_map.73), channel_id=1, source_target_pairs={{0,1},{1,0},{2,3},{3,2},{4,5},{5,4},{6,7},{7,6},{8,9},{9,8},{10,11... | collective-permute-start | bytes 49160 | tf_op jit(solution)/shard_map/ppermute | solution.py:424

commit v7 on v6

--- a/solution.py
+++ b/solution.py
@@ -14,7 +14,7 @@
 log_two_e = 1.4426950408889634
 
 big_limit = 45 * 1024 * 1024
-small_cost = pl.CostEstimate(flops=1024, bytes_accessed=1024, transcendentals=0)
+long_flops = 4 * 10**9
 
 in_vmem = pl.BlockSpec(memory_space=pltpu.VMEM)
 in_smem = pl.BlockSpec(memory_space=pltpu.SMEM)
@@ -32,12 +32,13 @@
 
 def call(kernel, out_shape, **settings):
     limit = settings.pop("limit", 16 * 1024 * 1024)
+    flops = settings.pop("flops", 1024)
     return pl.pallas_call(
         kernel,
         out_shape=out_shape,
         out_specs=jax.tree.map(lambda _: in_vmem, out_shape),
         compiler_params=pltpu.CompilerParams(vmem_limit_bytes=limit),
-        cost_estimate=small_cost,
+        cost_estimate=pl.CostEstimate(flops=flops, bytes_accessed=1024, transcendentals=0),
         **settings,
     )
 
@@ -59,19 +60,14 @@
     *parts, out_ref = refs
     at = 0
     for part in parts:
-        size = min(part.shape[0], out_ref.shape[0] - at)
-        out_ref[at : at + size] = part[:size]
-        at += size
-
-
-def join_parts(parts, count):
-    return join(parts, count)
-
-
-def join(parts, count=None):
-    count = sum(part.shape[0] for part in parts) if count is None else count
+        out_ref[at : at + part.shape[0]] = part[...]
+        at += part.shape[0]
+
+
+def join(parts, flops=1024):
+    count = sum(part.shape[0] for part in parts)
     shape = jax.ShapeDtypeStruct((count,) + parts[0].shape[1:], parts[0].dtype)
-    return call(join_kernel, shape, in_specs=[in_vmem] * len(parts))(*parts)
+    return call(join_kernel, shape, in_specs=[in_vmem] * len(parts), flops=flops)(*parts)
 
 
 def rows_update(turned_ref, rows_refs, switches, state, first):
@@ -382,17 +378,17 @@
         under = jnp.broadcast_to(flags, (padded, group.shape[1])).astype(group.dtype)
         sent.append(jnp.concatenate([group, under], axis=0))
     flags = jnp.broadcast_to(flags, (padded, HD)).astype(jnp.float32)
-    below = [rows, join_parts([first, rest], 2 * across)] + [None] * (down - 2)
-    far, *sent = lax.optimization_barrier((rows, *sent))
+    below = [rows, join([first, rest], long_flops)] + [None] * (down - 2)
+    member, inverse = members(across, turns, meta, groups[0])
+    far, inverse = lax.optimization_barrier((rows, inverse))
+    inverse, *sent = lax.optimization_barrier((inverse, *sent))
     others = [over(group, shift) for shift, group in enumerate(sent, 1)]
     for distance in range(3, down):
         below[distance] = up(far, distance)
     if down > 2:
         below[2] = up(below[1], 1, 1)
-    member, inverse = members(across, turns, meta, groups[0])
-    inverse, flags = lax.optimization_barrier((inverse, flags))
     depth = out_weight.shape[0]
-    pieces = [4 * depth // 8, 2 * depth // 8, 2 * depth // 8]
+    pieces = [4 * depth // 8, 2 * depth // 8, depth // 8, depth // 8]
     turned, flags, weight, *state = attend_first(
         across, flags, [groups[0], *others], rows, out_weight, pieces[0]
     )
@@ -401,7 +397,7 @@
     stages = [[1]] + [list(range(d, min(d + 2, down))) for d in range(3, down, 2)] + [[2]]
     for number, distances in enumerate(stages):
         last = number == len(stages) - 1
-        with_weight = number < 2
+        with_weight = number < 2 or last
         state = attend_next(
             across,
             distances,

time: 39.8 us -> 41.1 us (1.033)
  waiting for transfers between devices: 1.61 us -> 4.15 us
  blocking collectives: 11.5 us -> 9.28 us
  Pallas kernels: 8.21 us -> 9.07 us
    ppermute x2, waiting for transfers between devices: 1.08 us -> 3.62 us  [over(): return lax.ppermute(rows, 'seq', pairs)]
    all_to_all x1, blocking collectives: 11.5 us -> 9.28 us  [on_device(): lax.all_to_all(state[0], 'seq', split_axis=0, concat_axis=0, tiled=True)]
    ppermute x2, starting transfers between devices: 3.6 us -> 4.62 us  [over(): return lax.ppermute(rows, 'seq', pairs)]
    ppermute x4, starting transfers between devices: 10.7 us -> 9.66 us  [up(): return lax.ppermute(rows, 'seq', pairs)]
    pallas_call x3, Pallas kernels: 3.5 us -> 4.36 us  [attend_next(): call(functools.partial(next_kernel, across, distances, turns, last, at),...]
  transfers between devices with their start and end apart: 7 -> 7, of which waited for: 2 -> 2; matrix products, arithmetic and copies ran while one was open for 5% -> 5% of each run, Pallas kernels for 18% -> 17%
where the time goes in v7:
time: 41.1 us; the launch traced here: 40.6 us
  starting transfers between devices  14.3 us (35%)
  blocking collectives  9.28 us (23%)
  Pallas kernels  9.07 us (22%)
  waiting for transfers between devices  4.15 us (10%)
  other arithmetic  3.5 us (9%)
    ppermute x4, starting transfers between devices, up(): return lax.ppermute(rows, 'seq', pairs)  9.66 us
    all_to_all x1, blocking collectives, on_device(): lax.all_to_all(state[0], 'seq', split_axis=0, concat_axis=0, tiled=True)  9.28 us
    ppermute x2, starting transfers between devices, over(): return lax.ppermute(rows, 'seq', pairs)  4.62 us
    pallas_call x3, Pallas kernels, attend_next(): call(functools.partial(next_kernel, across, distances, turns, last, at),...  4.36 us
    ppermute x2, waiting for transfers between devices, over(): return lax.ppermute(rows, 'seq', pairs)  3.62 us
    pallas_call x1, Pallas kernels, attend_first(): call(functools.partial(first_kernel, across), [jax.ShapeDtypeStruct((acro...  2.61 us
    select_n x2, other arithmetic, pick(): jnp.where(number == part, rows[:, part * width:(part + 1) * width], picked)  1.94 us
    pallas_call x2, Pallas kernels, project(): call(functools.partial(project_kernel, across, other), jax.ShapeDtypeStru...  1.34 us
  transfers between devices with their start and end apart: 7, of which 2 were waited for; matrix products, arithmetic and copies ran while one was open for 5% of the time, Pallas kernels for 17%

profile of v7, /device:TPU:0, one launch (start us, length us, event | category | flops | bytes accessed | tf_op | source)
XLA Modules:
  0.0 40.6 jit_solution(12121350822927194869)
XLA Ops:
  0.0 0.9 %broadcast_select_fusion.4 = (bf16[192,128]{1,0:T(8,128)(2,1)S(1)}, bf16[192,128]{1,0:T(8,128)(2,1)S(1)}, bf16[192,128]{1,0:T(8,128)(2,1)S(1)}, bf16[192,128]{1,0:T(8,128)(2,1)S(1)}) fusion(pred[]{:T(512)S(6)} %eq.19, bf16[192,256]{1,0:T(8,128)(2,1)} %param.8, pred[]{:T(512)S(6)} %eq.17, bf16[192,256]{1,0:T(8,128)(2,1)} %param.7), kind=kLoop, calls=%fused_computation.5 | loop fusion | flops 98304 | bytes 393218 | tf_op jit(solution)/shard_map/jit(_where)/select_n | solution.py:50
  0.9 0.1 broadcast_select_fusion.2
  1.0 3.0 %collective-permute-start = (bf16[2,192,128]{2,1,0:T(8,128)(2,1)S(1)}, bf16[2,192,128]{2,1,0:T(8,128)(2,1)S(1)}, u32[]{:S(2)}, u32[]{:S(2)}) collective-permute-start(bf16[2,192,128]{2,1,0:T(8,128)(2,1)S(1)} %get-tuple-element.61), channel_id=1, source_target_pairs={{0,2},{2,0},{4,6},{6,4},{8,10},{10,8},{12,14},{14,12},{1,3},{3,1},... | collective-permute-start | bytes 294920 | tf_op jit(solution)/shard_map/ppermute | solution.py:355
  4.0 3.5 %collective-permute-start.2 = (bf16[2,192,128]{2,1,0:T(8,128)(2,1)S(1)}, bf16[2,192,128]{2,1,0:T(8,128)(2,1)S(1)}, u32[]{:S(2)}, u32[]{:S(2)}) collective-permute-start(bf16[2,192,128]{2,1,0:T(8,128)(2,1)S(1)} %get-tuple-element.62.refs_0_), channel_id=1, source_target_pairs={{0,4},{2,6},{4,8},{6,10},{8,12},{10,14},{1,5},{3,7},{5,9},{7,11},{... | collective-permute-start | bytes 294920 | tf_op jit(solution)/shard_map/ppermute | solution.py:360
  7.5 0.7 %pad_add_fusion.meta_ref = s32[24]{0:T(128)S(1)} fusion(s32[8]{0:T(128)} %bitcast.1, s32[16]{0:T(128)} %param.10), kind=kLoop, calls=%fused_computation.9 | loop fusion | flops 24 | bytes 192 | tf_op jit(solution)/shard_map/concatenate | solution.py:372
  8.3 0.1 slice.27
  8.3 0.1 pad.6.clone
  8.4 0.0 collective-permute-done.refs_1_.refs_0_
  8.4 3.5 %collective-permute-start.3 = (bf16[2,192,128]{2,1,0:T(8,128)(2,1)S(1)}, bf16[2,192,128]{2,1,0:T(8,128)(2,1)S(1)}, u32[]{:S(2)}, u32[]{:S(2)}) collective-permute-start(bf16[2,192,128]{2,1,0:T(8,128)(2,1)S(1)} %shard_map.67), channel_id=1, source_target_pairs={{0,4},{2,6},{4,8},{6,10},{8,12},{10,14},{1,5},{3,7},{5,9},{7,11},{... | collective-permute-start | bytes 294920 | tf_op jit(solution)/shard_map/ppermute | solution.py:360
  11.9 1.1 %broadcast_select_fusion = (bf16[192,512]{1,0:T(8,128)(2,1)S(1)}, bf16[192,512]{1,0:T(8,128)(2,1)S(1)}) fusion(pred[]{:T(512)S(6)} %eq.19, bf16[192,1024]{1,0:T(8,128)(2,1)} %param.6, pred[]{:T(512)S(6)} %eq.17), kind=kLoop, calls=%fused_computation.1 | loop fusion | flops 196608 | bytes 786434 | tf_op jit(solution)/shard_map/jit(_where)/select_n | solution.py:50
  13.0 0.1 pad_maximum_fusion
  13.1 0.7 %shard_map.65 = (bf16[2,64,768]{2,1,0:T(8,128)(2,1)S(1)}, f32[16,128]{1,0:T(8,128)S(1)}) custom-call(s32[24]{0:T(128)S(1)} %pad_add_fusion.meta_ref, bf16[192,512]{1,0:T(8,128)(2,1)S(1)} %get-tuple-element.54.after_ref.refs_0_), custom_call_target="tpu_custom_call" | custom-call | flops 1024 | bytes 1024 | tf_op jit(solution)/shard_map/pallas_call | solution.py:165
  13.8 2.0 %collective-permute-start.5 = (bf16[4,192,128]{2,1,0:T(8,128)(2,1)S(1)}, bf16[4,192,128]{2,1,0:T(8,128)(2,1)S(1)}, u32[]{:S(2)}, u32[]{:S(2)}) collective-permute-start(bf16[4,192,128]{2,1,0:T(8,128)(2,1)S(1)} %shard_map.64.refs_2_), channel_id=1, source_target_pairs={{0,12},{2,14},{1,13},{3,15},{16,28},{18,30},{17,29},{19,31}} | collective-permute-start | bytes 589832 | tf_op jit(solution)/shard_map/ppermute | solution.py:360
  15.9 1.6 %collective-permute-start.1 = (bf16[208,512]{1,0:T(8,128)(2,1)S(1)}, bf16[208,512]{1,0:T(8,128)(2,1)S(1)}, u32[]{:S(2)}, u32[]{:S(2)}) collective-permute-start(bf16[208,512]{1,0:T(8,128)(2,1)S(1)} %pad_maximum_fusion), channel_id=1, source_target_pairs={{0,2},{2,0},{4,6},{6,4},{8,10},{10,8},{12,14},{14,12},{1,3},{3,1},... | collective-permute-start | bytes 638984 | tf_op jit(solution)/shard_map/ppermute | solution.py:355
  17.5 0.0 collective-permute-done.2.refs_0_
  17.5 0.0 collective-permute-done.3.refs_1_
  17.5 0.7 %collective-permute-start.4 = (bf16[4,192,128]{2,1,0:T(8,128)(2,1)S(1)}, bf16[4,192,128]{2,1,0:T(8,128)(2,1)S(1)}, u32[]{:S(2)}, u32[]{:S(2)}) collective-permute-start(bf16[4,192,128]{2,1,0:T(8,128)(2,1)S(1)} %shard_map.68.refs_0_), channel_id=1, source_target_pairs={{4,8},{6,10},{8,12},{10,14},{5,9},{7,11},{9,13},{11,15},{20,24},{2... | collective-permute-start | bytes 589832 | tf_op jit(solution)/shard_map/ppermute | solution.py:360
  18.2 3.6 %collective-permute-done.1.refs_1_ = bf16[208,512]{1,0:T(8,128)(2,1)S(1)} collective-permute-done((bf16[208,512]{1,0:T(8,128)(2,1)S(1)}, bf16[208,512]{1,0:T(8,128)(2,1)S(1)}, u32[]{:S(2)}, u32[]{:S(2)}) %collective-permute-start.1) | collective-permute-done | bytes 213024 | tf_op jit(solution)/shard_map/ppermute | solution.py:355
  21.8 0.1 broadcast_in_dim.41.own_flags_ref
  21.9 2.6 %shard_map.66 = (bf16[2,128,768]{2,1,0:T(8,128)(2,1)S(1)}, f32[2,16,128]{2,1,0:T(8,128)S(1)}, bf16[512,4096]{1,0:T(8,128)(2,1)S(1)}, f32[2,1,768]{2,1,0:T(1,128)...) custom-call(f32[16,128]{1,0:T(8,128)S(1)} %broadcast_in_dim.41.own_flags_ref, ...), custom_call_target="tpu_custom_call" | custom-call | flops 1024 | bytes 1024 | tf_op jit(solution)/shard_map/pallas_call | solution.py:216
  24.5 1.6 %shard_map.69 = (f32[2,1,768]{2,1,0:T(1,128)S(1)}, f32[2,1,768]{2,1,0:T(1,128)S(1)}, f32[2,128,768]{2,1,0:T(8,128)S(1)}, bf16[256,4096]{1,0:T(8,128)(2,1)S(1)}) custom-call(f32[2,16,128]{2,1,0:T(8,128)S(1)} %get-tuple-element.34.flags_ref, ...), custom_call_target="tpu_custom_call", output_to_operand_aliasing={{0}: (3, {}), {1}: (4, {}), {2}: (5, {})} | custom-call | flops 1024 | bytes 1024 | tf_op jit(solution)/shard_map/pallas_call | solution.py:297
  26.1 0.0 collective-permute-done.5.refs_0_
  26.1 1.2 %shard_map.70 = (f32[2,1,768]{2,1,0:T(1,128)S(1)}, f32[2,1,768]{2,1,0:T(1,128)S(1)}, f32[2,128,768]{2,1,0:T(8,128)S(1)}, bf16[128,4096]{1,0:T(8,128)(2,1)S(1)}) custom-call(f32[2,16,128]{2,1,0:T(8,128)S(1)} %get-tuple-element.34.flags_ref, ...), custom_call_target="tpu_custom_call", output_to_operand_aliasing={{0}: (3, {}), {1}: (4, {}), {2}: (5, {})} | custom-call | flops 1024 | bytes 1024 | tf_op jit(solution)/shard_map/pallas_call | solution.py:297
  27.3 0.0 collective-permute-done.4.refs_0_
  27.3 1.5 %shard_map.71 = (f32[8,2,512]{2,1,0:T(2,128)S(1)}, bf16[128,4096]{1,0:T(8,128)(2,1)S(1)}) custom-call(f32[2,16,128]{2,1,0:T(8,128)S(1)} %get-tuple-element.34.flags_ref, bf16[2,128,768]{2,1,0:T(8,128)(2,1)S(1)} %get-tuple-element.35.turned_ref, bf16[4,192,128]{2,1,0:T(8,128)(2,1)S(1)} %collective-permute-done.4.refs_0_, ...), custom_call_target="tpu_custom_call" | custom-call | flops 1024 | bytes 1024 | tf_op jit(solution)/shard_map/pallas_call | solution.py:297
  28.9 9.3 %all_to_all.5.parts_ref = f32[8,2,512]{2,1,0:T(2,128)S(1)} all-to-all(f32[8,2,512]{2,1,0:T(2,128)S(1)} %get-tuple-element.48), channel_id=1, replica_groups=mesh['conv'=2,'seq'=8,'head'=2] {'seq'}, dimensions={0} | all-to-all | bytes 65536 | tf_op jit(solution)/shard_map/all_to_all | solution.py:418
  38.1 0.7 %shard_map.73 = f32[2,2048]{1,0:T(2,128)S(1)} custom-call(f32[8,2,512]{2,1,0:T(2,128)S(1)} %all_to_all.5.parts_ref, bf16[512,4096]{1,0:T(8,128)(2,1)S(1)} %get-tuple-element.49.refs_0_, bf16[256,4096]{1,0:T(8,128)(2,1)S(1)} %get-tuple-element.50.refs_1_, bf16[128,4096]{1,0:T(8,128)(2,1)S(1)} %get-tuple-element.51.refs_2_, ...), custom_call_target="tpu_custom_call" | custom-call | flops 1024 | bytes 1024 | tf_op jit(solution)/shard_map/pallas_call | solution.py:341
  38.8 0.0 collective-permute-start.6
  38.8 0.7 %shard_map.72 = f32[2,2048]{1,0:T(2,128)S(1)} custom-call(f32[8,2,512]{2,1,0:T(2,128)S(1)} %all_to_all.5.parts_ref, bf16[512,4096]{1,0:T(8,128)(2,1)S(1)} %get-tuple-element.49.refs_0_, bf16[256,4096]{1,0:T(8,128)(2,1)S(1)} %get-tuple-element.50.refs_1_, bf16[128,4096]{1,0:T(8,128)(2,1)S(1)} %get-tuple-element.51.refs_2_, ...), custom_call_target="tpu_custom_call" | custom-call | flops 1024 | bytes 1024 | tf_op jit(solution)/shard_map/pallas_call | solution.py:341
  39.5 0.5 %collective-permute-done.6 = f32[2,2048]{1,0:T(2,128)S(1)} collective-permute-done((f32[2,2048]{1,0:T(2,128)S(1)}, f32[2,2048]{1,0:T(2,128)S(1)}, u32[]{:S(2)}, u32[]{:S(2)}) %collective-permute-start.6) | collective-permute-done | bytes 16416 | tf_op jit(solution)/shard_map/ppermute | solution.py:420
  40.0 0.6 %add.10 = f32[2,2048]{1,0:T(2,128)} add(f32[2,2048]{1,0:T(2,128)S(1)} %shard_map.72, f32[2,2048]{1,0:T(2,128)S(1)} %collective-permute-done.6) | non-fusion elementwise | flops 4096 | bytes 49152 | tf_op jit(solution)/shard_map/add | solution.py:421
  (5 shorter events, 0.0 us)
Async XLA Ops:
  1.0 7.4 %collective-permute-start = (bf16[2,192,128]{2,1,0:T(8,128)(2,1)S(1)}, bf16[2,192,128]{2,1,0:T(8,128)(2,1)S(1)}, u32[]{:S(2)}, u32[]{:S(2)}) collective-permute-start(bf16[2,192,128]{2,1,0:T(8,128)(2,1)S(1)} %get-tuple-element.61), channel_id=1, source_target_pairs={{0,2},{2,0},{4,6},{6,4},{8,10},{10,8},{12,14},{14,12},{1,3},{3,1},... | collective-permute-start | bytes 294920 | tf_op jit(solution)/shard_map/ppermute | solution.py:355
  4.0 13.4 %collective-permute-start.2 = (bf16[2,192,128]{2,1,0:T(8,128)(2,1)S(1)}, bf16[2,192,128]{2,1,0:T(8,128)(2,1)S(1)}, u32[]{:S(2)}, u32[]{:S(2)}) collective-permute-start(bf16[2,192,128]{2,1,0:T(8,128)(2,1)S(1)} %get-tuple-element.62.refs_0_), channel_id=1, source_target_pairs={{0,4},{2,6},{4,8},{6,10},{8,12},{10,14},{1,5},{3,7},{5,9},{7,11},{... | collective-permute-start | bytes 294920 | tf_op jit(solution)/shard_map/ppermute | solution.py:360
  8.4 9.0 %collective-permute-start.3 = (bf16[2,192,128]{2,1,0:T(8,128)(2,1)S(1)}, bf16[2,192,128]{2,1,0:T(8,128)(2,1)S(1)}, u32[]{:S(2)}, u32[]{:S(2)}) collective-permute-start(bf16[2,192,128]{2,1,0:T(8,128)(2,1)S(1)} %shard_map.67), channel_id=1, source_target_pairs={{0,4},{2,6},{4,8},{6,10},{8,12},{10,14},{1,5},{3,7},{5,9},{7,11},{... | collective-permute-start | bytes 294920 | tf_op jit(solution)/shard_map/ppermute | solution.py:360
  13.8 12.2 %collective-permute-start.5 = (bf16[4,192,128]{2,1,0:T(8,128)(2,1)S(1)}, bf16[4,192,128]{2,1,0:T(8,128)(2,1)S(1)}, u32[]{:S(2)}, u32[]{:S(2)}) collective-permute-start(bf16[4,192,128]{2,1,0:T(8,128)(2,1)S(1)} %shard_map.64.refs_2_), channel_id=1, source_target_pairs={{0,12},{2,14},{1,13},{3,15},{16,28},{18,30},{17,29},{19,31}} | collective-permute-start | bytes 589832 | tf_op jit(solution)/shard_map/ppermute | solution.py:360
  15.9 5.9 %collective-permute-start.1 = (bf16[208,512]{1,0:T(8,128)(2,1)S(1)}, bf16[208,512]{1,0:T(8,128)(2,1)S(1)}, u32[]{:S(2)}, u32[]{:S(2)}) collective-permute-start(bf16[208,512]{1,0:T(8,128)(2,1)S(1)} %pad_maximum_fusion), channel_id=1, source_target_pairs={{0,2},{2,0},{4,6},{6,4},{8,10},{10,8},{12,14},{14,12},{1,3},{3,1},... | collective-permute-start | bytes 638984 | tf_op jit(solution)/shard_map/ppermute | solution.py:355
  17.5 9.9 %collective-permute-start.4 = (bf16[4,192,128]{2,1,0:T(8,128)(2,1)S(1)}, bf16[4,192,128]{2,1,0:T(8,128)(2,1)S(1)}, u32[]{:S(2)}, u32[]{:S(2)}) collective-permute-start(bf16[4,192,128]{2,1,0:T(8,128)(2,1)S(1)} %shard_map.68.refs_0_), channel_id=1, source_target_pairs={{4,8},{6,10},{8,12},{10,14},{5,9},{7,11},{9,13},{11,15},{20,24},{2... | collective-permute-start | bytes 589832 | tf_op jit(solution)/shard_map/ppermute | solution.py:360
  38.8 1.2 %collective-permute-start.6 = (f32[2,2048]{1,0:T(2,128)S(1)}, f32[2,2048]{1,0:T(2,128)S(1)}, u32[]{:S(2)}, u32[]{:S(2)}) collective-permute-start(f32[2,2048]{1,0:T(2,128)S(1)} %shard_map.73), channel_id=1, source_target_pairs={{0,1},{1,0},{2,3},{3,2},{4,5},{5,4},{6,7},{7,6},{8,9},{9,8},{10,11... | collective-permute-start | bytes 49160 | tf_op jit(solution)/shard_map/ppermute | solution.py:420

commit v8 on v7

--- a/solution.py
+++ b/solution.py
@@ -32,7 +32,7 @@
 
 def call(kernel, out_shape, **settings):
     limit = settings.pop("limit", 16 * 1024 * 1024)
-    flops = settings.pop("flops", 1024)
+    flops = settings.pop("flops", 0)
     return pl.pallas_call(
         kernel,
         out_shape=out_shape,
@@ -64,10 +64,10 @@
         at += part.shape[0]
 
 
-def join(parts, flops=1024):
+def join(parts):
     count = sum(part.shape[0] for part in parts)
     shape = jax.ShapeDtypeStruct((count,) + parts[0].shape[1:], parts[0].dtype)
-    return call(join_kernel, shape, in_specs=[in_vmem] * len(parts), flops=flops)(*parts)
+    return call(join_kernel, shape, in_specs=[in_vmem] * len(parts))(*parts)
 
 
 def rows_update(turned_ref, rows_refs, switches, state, first):
@@ -170,6 +170,7 @@
         ],
         in_specs=[in_smem, anywhere],
         scratch_shapes=[pltpu.VMEM((turns, columns), jnp.float32)],
+        flops=long_flops,
     )(meta, group)
 
 
@@ -378,17 +379,17 @@
         under = jnp.broadcast_to(flags, (padded, group.shape[1])).astype(group.dtype)
         sent.append(jnp.concatenate([group, under], axis=0))
     flags = jnp.broadcast_to(flags, (padded, HD)).astype(jnp.float32)
-    below = [rows, join([first, rest], long_flops)] + [None] * (down - 2)
-    member, inverse = members(across, turns, meta, groups[0])
-    far, inverse = lax.optimization_barrier((rows, inverse))
-    inverse, *sent = lax.optimization_barrier((inverse, *sent))
+    below = [rows, join([first, rest])] + [None] * (down - 2)
+    far, groups[0] = lax.optimization_barrier((rows, groups[0]))
     others = [over(group, shift) for shift, group in enumerate(sent, 1)]
     for distance in range(3, down):
         below[distance] = up(far, distance)
     if down > 2:
         below[2] = up(below[1], 1, 1)
+    member, inverse = members(across, turns, meta, groups[0])
+    inverse, flags = lax.optimization_barrier((inverse, flags))
     depth = out_weight.shape[0]
-    pieces = [4 * depth // 8, 2 * depth // 8, depth // 8, depth // 8]
+    pieces = [4 * depth // 8, 2 * depth // 8, 2 * depth // 8]
     turned, flags, weight, *state = attend_first(
         across, flags, [groups[0], *others], rows, out_weight, pieces[0]
     )
@@ -397,7 +398,7 @@
     stages = [[1]] + [list(range(d, min(d + 2, down))) for d in range(3, down, 2)] + [[2]]
     for number, distances in enumerate(stages):
         last = number == len(stages) - 1
-        with_weight = number < 2 or last
+        with_weight = number < 2
         state = attend_next(
             across,
             distances,

time: 41.1 us -> 42.3 us (1.029)
  blocking collectives: 9.28 us -> 12.2 us
  Pallas kernels: 9.07 us -> 8.21 us
  waiting for transfers between devices: 4.15 us -> 3.35 us
    all_to_all x1, blocking collectives: 9.28 us -> 12.2 us  [on_device(): lax.all_to_all(state[0], 'seq', split_axis=0, concat_axis=0, tiled=True)]
    pallas_call x3, Pallas kernels: 4.36 us -> 3.5 us  [attend_next(): call(functools.partial(next_kernel, across, distances, turns, last, at),...]
    ppermute x2, waiting for transfers between devices: 3.62 us -> 2.82 us  [over(): return lax.ppermute(rows, 'seq', pairs)]
where the time goes in v8:
time: 42.3 us; the launch traced here: 41.9 us
  starting transfers between devices  14.3 us (34%)
  blocking collectives  12.2 us (29%)
  Pallas kernels  8.21 us (19%)
  other arithmetic  3.5 us (8%)
  waiting for transfers between devices  3.35 us (8%)
    all_to_all x1, blocking collectives, on_device(): lax.all_to_all(state[0], 'seq', split_axis=0, concat_axis=0, tiled=True)  12.2 us
    ppermute x4, starting transfers between devices, up(): return lax.ppermute(rows, 'seq', pairs)  9.66 us
    ppermute x2, starting transfers between devices, over(): return lax.ppermute(rows, 'seq', pairs)  4.62 us
    pallas_call x3, Pallas kernels, attend_next(): call(functools.partial(next_kernel, across, distances, turns, last, at),...  3.5 us
    ppermute x2, waiting for transfers between devices, over(): return lax.ppermute(rows, 'seq', pairs)  2.82 us
    pallas_call x1, Pallas kernels, attend_first(): call(functools.partial(first_kernel, across), [jax.ShapeDtypeStruct((acro...  2.6 us
    select_n x2, other arithmetic, pick(): jnp.where(number == part, rows[:, part * width:(part + 1) * width], picked)  1.94 us
    pallas_call x2, Pallas kernels, project(): call(functools.partial(project_kernel, across, other), jax.ShapeDtypeStru...  1.34 us
  transfers between devices with their start and end apart: 7, of which 2 were waited for; matrix products, arithmetic and copies ran while one was open for 5% of the time, Pallas kernels for 17%

profile of v8, /device:TPU:0, one launch (start us, length us, event | category | flops | bytes accessed | tf_op | source)
XLA Modules:
  0.0 41.9 jit_solution(1597167905441719907)
XLA Ops:
  0.0 0.9 %broadcast_select_fusion.4 = (bf16[192,128]{1,0:T(8,128)(2,1)S(1)}, bf16[192,128]{1,0:T(8,128)(2,1)S(1)}, bf16[192,128]{1,0:T(8,128)(2,1)S(1)}, bf16[192,128]{1,0:T(8,128)(2,1)S(1)}) fusion(pred[]{:T(512)S(6)} %eq.19, bf16[192,256]{1,0:T(8,128)(2,1)} %param.8, pred[]{:T(512)S(6)} %eq.18, bf16[192,256]{1,0:T(8,128)(2,1)} %param.7), kind=kLoop, calls=%fused_computation.5 | loop fusion | flops 98304 | bytes 393218 | tf_op jit(solution)/shard_map/jit(_where)/select_n | solution.py:50
  0.9 0.1 broadcast_select_fusion.2
  1.0 3.0 %collective-permute-start = (bf16[2,192,128]{2,1,0:T(8,128)(2,1)S(1)}, bf16[2,192,128]{2,1,0:T(8,128)(2,1)S(1)}, u32[]{:S(2)}, u32[]{:S(2)}) collective-permute-start(bf16[2,192,128]{2,1,0:T(8,128)(2,1)S(1)} %get-tuple-element.57), channel_id=1, source_target_pairs={{0,2},{2,0},{4,6},{6,4},{8,10},{10,8},{12,14},{14,12},{1,3},{3,1},... | collective-permute-start | bytes 294920 | tf_op jit(solution)/shard_map/ppermute | solution.py:356
  4.0 3.5 %collective-permute-start.2 = (bf16[2,192,128]{2,1,0:T(8,128)(2,1)S(1)}, bf16[2,192,128]{2,1,0:T(8,128)(2,1)S(1)}, u32[]{:S(2)}, u32[]{:S(2)}) collective-permute-start(bf16[2,192,128]{2,1,0:T(8,128)(2,1)S(1)} %get-tuple-element.58.refs_0_), channel_id=1, source_target_pairs={{0,4},{2,6},{4,8},{6,10},{8,12},{10,14},{1,5},{3,7},{5,9},{7,11},{... | collective-permute-start | bytes 294920 | tf_op jit(solution)/shard_map/ppermute | solution.py:361
  7.5 0.7 %pad_add_fusion.meta_ref = s32[24]{0:T(128)S(1)} fusion(s32[8]{0:T(128)} %bitcast.1, s32[16]{0:T(128)} %param.10), kind=kLoop, calls=%fused_computation.9 | loop fusion | flops 24 | bytes 192 | tf_op jit(solution)/shard_map/concatenate | solution.py:373
  8.3 0.1 slice.33
  8.3 0.1 pad.6.clone
  8.4 0.0 collective-permute-done.refs_1_.refs_0_
  8.4 3.5 %collective-permute-start.3 = (bf16[2,192,128]{2,1,0:T(8,128)(2,1)S(1)}, bf16[2,192,128]{2,1,0:T(8,128)(2,1)S(1)}, u32[]{:S(2)}, u32[]{:S(2)}) collective-permute-start(bf16[2,192,128]{2,1,0:T(8,128)(2,1)S(1)} %shard_map.67), channel_id=1, source_target_pairs={{0,4},{2,6},{4,8},{6,10},{8,12},{10,14},{1,5},{3,7},{5,9},{7,11},{... | collective-permute-start | bytes 294920 | tf_op jit(solution)/shard_map/ppermute | solution.py:361
  11.9 1.1 %broadcast_select_fusion = (bf16[192,512]{1,0:T(8,128)(2,1)S(1)}, bf16[192,512]{1,0:T(8,128)(2,1)S(1)}) fusion(pred[]{:T(512)S(6)} %eq.19, bf16[192,1024]{1,0:T(8,128)(2,1)} %param.6, pred[]{:T(512)S(6)} %eq.18), kind=kLoop, calls=%fused_computation.1 | loop fusion | flops 196608 | bytes 786434 | tf_op jit(solution)/shard_map/jit(_where)/select_n | solution.py:50
  13.0 2.0 %collective-permute-start.5 = (bf16[4,192,128]{2,1,0:T(8,128)(2,1)S(1)}, bf16[4,192,128]{2,1,0:T(8,128)(2,1)S(1)}, u32[]{:S(2)}, u32[]{:S(2)}) collective-permute-start(bf16[4,192,128]{2,1,0:T(8,128)(2,1)S(1)} %shard_map.64.refs_2_), channel_id=1, source_target_pairs={{0,12},{2,14},{1,13},{3,15},{16,28},{18,30},{17,29},{19,31}} | collective-permute-start | bytes 589832 | tf_op jit(solution)/shard_map/ppermute | solution.py:361
  15.0 0.1 pad_maximum_fusion
  15.1 1.6 %collective-permute-start.1 = (bf16[208,512]{1,0:T(8,128)(2,1)S(1)}, bf16[208,512]{1,0:T(8,128)(2,1)S(1)}, u32[]{:S(2)}, u32[]{:S(2)}) collective-permute-start(bf16[208,512]{1,0:T(8,128)(2,1)S(1)} %pad_maximum_fusion), channel_id=1, source_target_pairs={{0,2},{2,0},{4,6},{6,4},{8,10},{10,8},{12,14},{14,12},{1,3},{3,1},... | collective-permute-start | bytes 638984 | tf_op jit(solution)/shard_map/ppermute | solution.py:356
  16.7 0.0 collective-permute-done.2.refs_0_
  16.7 0.0 collective-permute-done.3.refs_1_
  16.8 0.7 %collective-permute-start.4 = (bf16[4,192,128]{2,1,0:T(8,128)(2,1)S(1)}, bf16[4,192,128]{2,1,0:T(8,128)(2,1)S(1)}, u32[]{:S(2)}, u32[]{:S(2)}) collective-permute-start(bf16[4,192,128]{2,1,0:T(8,128)(2,1)S(1)} %shard_map.68.refs_0_), channel_id=1, source_target_pairs={{4,8},{6,10},{8,12},{10,14},{5,9},{7,11},{9,13},{11,15},{20,24},{2... | collective-permute-start | bytes 589832 | tf_op jit(solution)/shard_map/ppermute | solution.py:361
  17.4 0.7 %shard_map.65 = (bf16[2,64,768]{2,1,0:T(8,128)(2,1)S(1)}, f32[16,128]{1,0:T(8,128)S(1)}) custom-call(s32[24]{0:T(128)S(1)} %pad_add_fusion.meta_ref, bf16[192,512]{1,0:T(8,128)(2,1)S(1)} %get-tuple-element.29.after_ref.refs_0_), custom_call_target="tpu_custom_call" | custom-call | flops 4000000000 | bytes 1024 | tf_op jit(solution)/shard_map/pallas_call | solution.py:165
  18.2 0.1 broadcast_in_dim.45.own_flags_ref
  18.2 2.8 %collective-permute-done.1.refs_1_ = bf16[208,512]{1,0:T(8,128)(2,1)S(1)} collective-permute-done((bf16[208,512]{1,0:T(8,128)(2,1)S(1)}, bf16[208,512]{1,0:T(8,128)(2,1)S(1)}, u32[]{:S(2)}, u32[]{:S(2)}) %collective-permute-start.1) | collective-permute-done | bytes 213024 | tf_op jit(solution)/shard_map/ppermute | solution.py:356
  21.1 2.6 %shard_map.66 = (bf16[2,128,768]{2,1,0:T(8,128)(2,1)S(1)}, f32[2,16,128]{2,1,0:T(8,128)S(1)}, bf16[512,4096]{1,0:T(8,128)(2,1)S(1)}, f32[2,1,768]{2,1,0:T(1,128)...) custom-call(f32[16,128]{1,0:T(8,128)S(1)} %broadcast_in_dim.45.own_flags_ref, ...), custom_call_target="tpu_custom_call" | custom-call | bytes 1024 | tf_op jit(solution)/shard_map/pallas_call | solution.py:217
  23.7 1.6 %shard_map.69 = (f32[2,1,768]{2,1,0:T(1,128)S(1)}, f32[2,1,768]{2,1,0:T(1,128)S(1)}, f32[2,128,768]{2,1,0:T(8,128)S(1)}, bf16[256,4096]{1,0:T(8,128)(2,1)S(1)}) custom-call(f32[2,16,128]{2,1,0:T(8,128)S(1)} %get-tuple-element.32.flags_ref, ...), custom_call_target="tpu_custom_call", output_to_operand_aliasing={{0}: (3, {}), {1}: (4, {}), {2}: (5, {})} | custom-call | bytes 1024 | tf_op jit(solution)/shard_map/pallas_call | solution.py:298
  25.3 0.0 collective-permute-done.5.refs_0_
  25.3 1.6 %shard_map.70 = (f32[2,1,768]{2,1,0:T(1,128)S(1)}, f32[2,1,768]{2,1,0:T(1,128)S(1)}, f32[2,128,768]{2,1,0:T(8,128)S(1)}, bf16[256,4096]{1,0:T(8,128)(2,1)S(1)}) custom-call(f32[2,16,128]{2,1,0:T(8,128)S(1)} %get-tuple-element.32.flags_ref, ...), custom_call_target="tpu_custom_call", output_to_operand_aliasing={{0}: (3, {}), {1}: (4, {}), {2}: (5, {})} | custom-call | bytes 1024 | tf_op jit(solution)/shard_map/pallas_call | solution.py:298
  26.9 0.0 collective-permute-done.4.refs_0_
  26.9 0.3 shard_map.71
  27.2 12.2 %all_to_all.5.parts_ref = f32[8,2,512]{2,1,0:T(2,128)S(1)} all-to-all(f32[8,2,512]{2,1,0:T(2,128)S(1)} %shard_map.71), channel_id=1, replica_groups=mesh['conv'=2,'seq'=8,'head'=2] {'seq'}, dimensions={0} | all-to-all | bytes 65536 | tf_op jit(solution)/shard_map/all_to_all | solution.py:419
  39.4 0.7 %shard_map.73 = f32[2,2048]{1,0:T(2,128)S(1)} custom-call(f32[8,2,512]{2,1,0:T(2,128)S(1)} %all_to_all.5.parts_ref, bf16[512,4096]{1,0:T(8,128)(2,1)S(1)} %get-tuple-element.46.refs_0_, bf16[256,4096]{1,0:T(8,128)(2,1)S(1)} %get-tuple-element.47.refs_1_, bf16[256,4096]{1,0:T(8,128)(2,1)S(1)} %get-tuple-element.48.refs_2_), custom_call_target="tpu_custom_call" | custom-call | bytes 1024 | tf_op jit(solution)/shard_map/pallas_call | solution.py:342
  40.1 0.0 collective-permute-start.6
  40.1 0.7 %shard_map.72 = f32[2,2048]{1,0:T(2,128)S(1)} custom-call(f32[8,2,512]{2,1,0:T(2,128)S(1)} %all_to_all.5.parts_ref, bf16[512,4096]{1,0:T(8,128)(2,1)S(1)} %get-tuple-element.46.refs_0_, bf16[256,4096]{1,0:T(8,128)(2,1)S(1)} %get-tuple-element.47.refs_1_, bf16[256,4096]{1,0:T(8,128)(2,1)S(1)} %get-tuple-element.48.refs_2_), custom_call_target="tpu_custom_call" | custom-call | bytes 1024 | tf_op jit(solution)/shard_map/pallas_call | solution.py:342
  40.8 0.5 %collective-permute-done.6 = f32[2,2048]{1,0:T(2,128)S(1)} collective-permute-done((f32[2,2048]{1,0:T(2,128)S(1)}, f32[2,2048]{1,0:T(2,128)S(1)}, u32[]{:S(2)}, u32[]{:S(2)}) %collective-permute-start.6) | collective-permute-done | bytes 16416 | tf_op jit(solution)/shard_map/ppermute | solution.py:421
  41.3 0.6 %add.10 = f32[2,2048]{1,0:T(2,128)} add(f32[2,2048]{1,0:T(2,128)S(1)} %shard_map.72, f32[2,2048]{1,0:T(2,128)S(1)} %collective-permute-done.6) | non-fusion elementwise | flops 4096 | bytes 49152 | tf_op jit(solution)/shard_map/add | solution.py:422
  (5 shorter events, 0.0 us)
Async XLA Ops:
  1.0 7.4 %collective-permute-start = (bf16[2,192,128]{2,1,0:T(8,128)(2,1)S(1)}, bf16[2,192,128]{2,1,0:T(8,128)(2,1)S(1)}, u32[]{:S(2)}, u32[]{:S(2)}) collective-permute-start(bf16[2,192,128]{2,1,0:T(8,128)(2,1)S(1)} %get-tuple-element.57), channel_id=1, source_target_pairs={{0,2},{2,0},{4,6},{6,4},{8,10},{10,8},{12,14},{14,12},{1,3},{3,1},... | collective-permute-start | bytes 294920 | tf_op jit(solution)/shard_map/ppermute | solution.py:356
  4.0 12.7 %collective-permute-start.2 = (bf16[2,192,128]{2,1,0:T(8,128)(2,1)S(1)}, bf16[2,192,128]{2,1,0:T(8,128)(2,1)S(1)}, u32[]{:S(2)}, u32[]{:S(2)}) collective-permute-start(bf16[2,192,128]{2,1,0:T(8,128)(2,1)S(1)} %get-tuple-element.58.refs_0_), channel_id=1, source_target_pairs={{0,4},{2,6},{4,8},{6,10},{8,12},{10,14},{1,5},{3,7},{5,9},{7,11},{... | collective-permute-start | bytes 294920 | tf_op jit(solution)/shard_map/ppermute | solution.py:361
  8.4 8.3 %collective-permute-start.3 = (bf16[2,192,128]{2,1,0:T(8,128)(2,1)S(1)}, bf16[2,192,128]{2,1,0:T(8,128)(2,1)S(1)}, u32[]{:S(2)}, u32[]{:S(2)}) collective-permute-start(bf16[2,192,128]{2,1,0:T(8,128)(2,1)S(1)} %shard_map.67), channel_id=1, source_target_pairs={{0,4},{2,6},{4,8},{6,10},{8,12},{10,14},{1,5},{3,7},{5,9},{7,11},{... | collective-permute-start | bytes 294920 | tf_op jit(solution)/shard_map/ppermute | solution.py:361
  13.0 12.3 %collective-permute-start.5 = (bf16[4,192,128]{2,1,0:T(8,128)(2,1)S(1)}, bf16[4,192,128]{2,1,0:T(8,128)(2,1)S(1)}, u32[]{:S(2)}, u32[]{:S(2)}) collective-permute-start(bf16[4,192,128]{2,1,0:T(8,128)(2,1)S(1)} %shard_map.64.refs_2_), channel_id=1, source_target_pairs={{0,12},{2,14},{1,13},{3,15},{16,28},{18,30},{17,29},{19,31}} | collective-permute-start | bytes 589832 | tf_op jit(solution)/shard_map/ppermute | solution.py:361
  15.1 5.9 %collective-permute-start.1 = (bf16[208,512]{1,0:T(8,128)(2,1)S(1)}, bf16[208,512]{1,0:T(8,128)(2,1)S(1)}, u32[]{:S(2)}, u32[]{:S(2)}) collective-permute-start(bf16[208,512]{1,0:T(8,128)(2,1)S(1)} %pad_maximum_fusion), channel_id=1, source_target_pairs={{0,2},{2,0},{4,6},{6,4},{8,10},{10,8},{12,14},{14,12},{1,3},{3,1},... | collective-permute-start | bytes 638984 | tf_op jit(solution)/shard_map/ppermute | solution.py:356
  16.8 10.2 %collective-permute-start.4 = (bf16[4,192,128]{2,1,0:T(8,128)(2,1)S(1)}, bf16[4,192,128]{2,1,0:T(8,128)(2,1)S(1)}, u32[]{:S(2)}, u32[]{:S(2)}) collective-permute-start(bf16[4,192,128]{2,1,0:T(8,128)(2,1)S(1)} %shard_map.68.refs_0_), channel_id=1, source_target_pairs={{4,8},{6,10},{8,12},{10,14},{5,9},{7,11},{9,13},{11,15},{20,24},{2... | collective-permute-start | bytes 589832 | tf_op jit(solution)/shard_map/ppermute | solution.py:361
  40.1 1.2 %collective-permute-start.6 = (f32[2,2048]{1,0:T(2,128)S(1)}, f32[2,2048]{1,0:T(2,128)S(1)}, u32[]{:S(2)}, u32[]{:S(2)}) collective-permute-start(f32[2,2048]{1,0:T(2,128)S(1)} %shard_map.73), channel_id=1, source_target_pairs={{0,1},{1,0},{2,3},{3,2},{4,5},{5,4},{6,7},{7,6},{8,9},{9,8},{10,11... | collective-permute-start | bytes 49160 | tf_op jit(solution)/shard_map/ppermute | solution.py:421

commit v9 on v6

--- a/solution.py
+++ b/solution.py
@@ -263,7 +263,7 @@
         weight_copy.wait()
     if last:
         member_ref, inverse_ref, out_ref = refs
-        rows = out_ref.shape[1]
+        rows = out_ref.shape[1] * turns // member_ref.shape[1]
         pooled = None
         for e in range(across):
             attended = (state[2][e] / state[1][e]).astype(jnp.bfloat16)
@@ -277,7 +277,7 @@
         for r in range(pooled.shape[0] // turns):
             mean = pooled[r * turns : (r + 1) * turns] * inverse_ref[...]
             for s in range(out_ref.shape[0]):
-                out_ref[s, :, r * HD : (r + 1) * HD] = mean[s * rows : (s + 1) * rows]
+                out_ref[s, r * rows : (r + 1) * rows, :] = mean[s * rows : (s + 1) * rows]
 
 
 def attend_next(across, distances, turns, turned, flags, below, state, pool, out_piece, weight, at, piece):
@@ -310,6 +310,7 @@
 
 def project_kernel(across, other, parts_ref, *refs):
     weights, out_ref = refs[:-1], refs[-1]
+    rows = out_ref.shape[0]
     side = lax.axis_index("head")
     if other:
         side = 1 - side
@@ -318,9 +319,8 @@
         total = parts_ref[y]
         for s in range(y + across, parts_ref.shape[0], across):
             total = total + parts_ref[s]
-        groups.append(total)
+        groups += [total[at : at + rows] for at in range(0, total.shape[0], rows)]
     total = jnp.concatenate(groups, axis=1)
-    rows = total.shape[0]
     high = total.astype(jnp.bfloat16)
     low = (total - high.astype(jnp.float32)).astype(jnp.bfloat16)
     both = jnp.concatenate([high, low], axis=0)
@@ -341,10 +341,10 @@
         out_ref[:, c * step : (c + 1) * step] = product[:rows] + product[rows:]
 
 
-def project(across, other, parts, weights):
+def project(across, other, rows, parts, weights):
     return call(
         functools.partial(project_kernel, across, other),
-        jax.ShapeDtypeStruct((parts.shape[1], weights[0].shape[1] // 2), jnp.float32),
+        jax.ShapeDtypeStruct((rows, weights[0].shape[1] // 2), jnp.float32),
         in_specs=[in_vmem] * (1 + len(weights)),
     )(parts, *weights)
 
@@ -397,7 +397,7 @@
         across, flags, [groups[0], *others], rows, out_weight, pieces[0]
     )
     weights = [weight]
-    out_piece = (count, turns // count, queries.shape[1] // across)
+    out_piece = (count, turns // count * (queries.shape[1] // across // HD), HD)
     stages = [[1]] + [list(range(d, min(d + 2, down))) for d in range(3, down, 2)] + [[2]]
     for number, distances in enumerate(stages):
         last = number == len(stages) - 1
@@ -420,9 +420,9 @@
             *state, weight = state
             weights.append(weight)
     parts = lax.all_to_all(state[0], "seq", split_axis=0, concat_axis=0, tiled=True)
-    theirs = project(across, True, parts, weights)
+    theirs = project(across, True, turns // count, parts, weights)
     theirs = lax.ppermute(theirs, "head", [(0, 1), (1, 0)])
-    return project(across, False, parts, weights) + theirs
+    return project(across, False, turns // count, parts, weights) + theirs
 
 
 def solution(mesh):

time: 39.8 us -> 39.8 us (level)
  no operation moved by 1% of the time
where the time goes in v9:
time: 39.8 us; the launch traced here: 39.4 us
  starting transfers between devices  14.3 us (36%)
  blocking collectives  11.5 us (29%)
  Pallas kernels  8.2 us (21%)
  other arithmetic  3.5 us (9%)
  waiting for transfers between devices  1.61 us (4%)
    all_to_all x1, blocking collectives, on_device(): lax.all_to_all(state[0], 'seq', split_axis=0, concat_axis=0, tiled=True)  11.5 us
    ppermute x4, starting transfers between devices, up(): return lax.ppermute(rows, 'seq', pairs)  10.7 us
    ppermute x2, starting transfers between devices, over(): return lax.ppermute(rows, 'seq', pairs)  3.6 us
    pallas_call x3, Pallas kernels, attend_next(): call(functools.partial(next_kernel, across, distances, turns, last, at),...  3.49 us
    pallas_call x1, Pallas kernels, attend_first(): call(functools.partial(first_kernel, across), [jax.ShapeDtypeStruct((acro...  2.6 us
    select_n x2, other arithmetic, pick(): jnp.where(number == part, rows[:, part * width:(part + 1) * width], picked)  1.94 us
    pallas_call x2, Pallas kernels, project(): call(functools.partial(project_kernel, across, other), jax.ShapeDtypeStru...  1.34 us
    ppermute x2, waiting for transfers between devices, over(): return lax.ppermute(rows, 'seq', pairs)  1.08 us
  transfers between devices with their start and end apart: 7, of which 2 were waited for; matrix products, arithmetic and copies ran while one was open for 5% of the time, Pallas kernels for 18%

profile of v9, /device:TPU:0, one launch (start us, length us, event | category | flops | bytes accessed | tf_op | source)
XLA Modules:
  0.0 39.4 jit_solution(267741373762779920)
XLA Ops:
  0.0 0.9 %broadcast_select_fusion.4 = (bf16[192,128]{1,0:T(8,128)(2,1)S(1)}, bf16[192,128]{1,0:T(8,128)(2,1)S(1)}, bf16[192,128]{1,0:T(8,128)(2,1)S(1)}, bf16[192,128]{1,0:T(8,128)(2,1)S(1)}) fusion(pred[]{:T(512)S(6)} %eq.19, bf16[192,256]{1,0:T(8,128)(2,1)} %param.8, pred[]{:T(512)S(6)} %eq.17, bf16[192,256]{1,0:T(8,128)(2,1)} %param.7), kind=kLoop, calls=%fused_computation.5 | loop fusion | flops 98304 | bytes 393218 | tf_op jit(solution)/shard_map/jit(_where)/select_n | solution.py:49
  0.9 0.1 broadcast_select_fusion.2
  1.0 3.0 %collective-permute-start = (bf16[2,192,128]{2,1,0:T(8,128)(2,1)S(1)}, bf16[2,192,128]{2,1,0:T(8,128)(2,1)S(1)}, u32[]{:S(2)}, u32[]{:S(2)}) collective-permute-start(bf16[2,192,128]{2,1,0:T(8,128)(2,1)S(1)} %get-tuple-element.57), channel_id=1, source_target_pairs={{0,2},{2,0},{4,6},{6,4},{8,10},{10,8},{12,14},{14,12},{1,3},{3,1},... | collective-permute-start | bytes 294920 | tf_op jit(solution)/shard_map/ppermute | solution.py:359
  4.0 3.5 %collective-permute-start.2 = (bf16[2,192,128]{2,1,0:T(8,128)(2,1)S(1)}, bf16[2,192,128]{2,1,0:T(8,128)(2,1)S(1)}, u32[]{:S(2)}, u32[]{:S(2)}) collective-permute-start(bf16[2,192,128]{2,1,0:T(8,128)(2,1)S(1)} %get-tuple-element.58.refs_0_), channel_id=1, source_target_pairs={{0,4},{2,6},{4,8},{6,10},{8,12},{10,14},{1,5},{3,7},{5,9},{7,11},{... | collective-permute-start | bytes 294920 | tf_op jit(solution)/shard_map/ppermute | solution.py:364
  7.5 0.7 %pad_add_fusion.meta_ref = s32[24]{0:T(128)S(1)} fusion(s32[8]{0:T(128)} %bitcast.1, s32[16]{0:T(128)} %param.10), kind=kLoop, calls=%fused_computation.9 | loop fusion | flops 24 | bytes 192 | tf_op jit(solution)/shard_map/concatenate | solution.py:376
  8.3 0.1 slice.33
  8.3 0.1 pad.6.clone
  8.4 0.0 collective-permute-done.refs_1_.refs_0_
  8.4 3.5 %collective-permute-start.3 = (bf16[2,192,128]{2,1,0:T(8,128)(2,1)S(1)}, bf16[2,192,128]{2,1,0:T(8,128)(2,1)S(1)}, u32[]{:S(2)}, u32[]{:S(2)}) collective-permute-start(bf16[2,192,128]{2,1,0:T(8,128)(2,1)S(1)} %shard_map.67), channel_id=1, source_target_pairs={{0,4},{2,6},{4,8},{6,10},{8,12},{10,14},{1,5},{3,7},{5,9},{7,11},{... | collective-permute-start | bytes 294920 | tf_op jit(solution)/shard_map/ppermute | solution.py:364
  11.9 1.1 %broadcast_select_fusion = (bf16[192,512]{1,0:T(8,128)(2,1)S(1)}, bf16[192,512]{1,0:T(8,128)(2,1)S(1)}) fusion(pred[]{:T(512)S(6)} %eq.19, bf16[192,1024]{1,0:T(8,128)(2,1)} %param.6, pred[]{:T(512)S(6)} %eq.17), kind=kLoop, calls=%fused_computation.1 | loop fusion | flops 196608 | bytes 786434 | tf_op jit(solution)/shard_map/jit(_where)/select_n | solution.py:49
  13.0 0.1 pad_maximum_fusion
  13.1 0.6 %collective-permute-start.1 = (bf16[208,512]{1,0:T(8,128)(2,1)S(1)}, bf16[208,512]{1,0:T(8,128)(2,1)S(1)}, u32[]{:S(2)}, u32[]{:S(2)}) collective-permute-start(bf16[208,512]{1,0:T(8,128)(2,1)S(1)} %pad_maximum_fusion), channel_id=1, source_target_pairs={{0,2},{2,0},{4,6},{6,4},{8,10},{10,8},{12,14},{14,12},{1,3},{3,1},... | collective-permute-start | bytes 638984 | tf_op jit(solution)/shard_map/ppermute | solution.py:359
  13.7 3.0 %collective-permute-start.5 = (bf16[4,192,128]{2,1,0:T(8,128)(2,1)S(1)}, bf16[4,192,128]{2,1,0:T(8,128)(2,1)S(1)}, u32[]{:S(2)}, u32[]{:S(2)}) collective-permute-start(bf16[4,192,128]{2,1,0:T(8,128)(2,1)S(1)} %shard_map.64.refs_2_), channel_id=1, source_target_pairs={{0,12},{2,14},{1,13},{3,15},{16,28},{18,30},{17,29},{19,31}} | collective-permute-start | bytes 589832 | tf_op jit(solution)/shard_map/ppermute | solution.py:364
  16.7 0.0 collective-permute-done.2.refs_0_
  16.7 0.0 collective-permute-done.3.refs_1_
  16.8 0.7 %collective-permute-start.4 = (bf16[4,192,128]{2,1,0:T(8,128)(2,1)S(1)}, bf16[4,192,128]{2,1,0:T(8,128)(2,1)S(1)}, u32[]{:S(2)}, u32[]{:S(2)}) collective-permute-start(bf16[4,192,128]{2,1,0:T(8,128)(2,1)S(1)} %shard_map.68.refs_0_), channel_id=1, source_target_pairs={{4,8},{6,10},{8,12},{10,14},{5,9},{7,11},{9,13},{11,15},{20,24},{2... | collective-permute-start | bytes 589832 | tf_op jit(solution)/shard_map/ppermute | solution.py:364
  17.4 0.7 %shard_map.65 = (bf16[2,64,768]{2,1,0:T(8,128)(2,1)S(1)}, f32[16,128]{1,0:T(8,128)S(1)}) custom-call(s32[24]{0:T(128)S(1)} %pad_add_fusion.meta_ref, bf16[192,512]{1,0:T(8,128)(2,1)S(1)} %get-tuple-element.50.after_ref.refs_0_), custom_call_target="tpu_custom_call" | custom-call | flops 1024 | bytes 1024 | tf_op jit(solution)/shard_map/pallas_call | solution.py:169
  18.2 0.1 broadcast_in_dim.45.own_flags_ref
  18.2 1.1 %collective-permute-done.1.refs_1_ = bf16[208,512]{1,0:T(8,128)(2,1)S(1)} collective-permute-done((bf16[208,512]{1,0:T(8,128)(2,1)S(1)}, bf16[208,512]{1,0:T(8,128)(2,1)S(1)}, u32[]{:S(2)}, u32[]{:S(2)}) %collective-permute-start.1) | collective-permute-done | bytes 213024 | tf_op jit(solution)/shard_map/ppermute | solution.py:359
  19.3 2.6 %shard_map.66 = (bf16[2,128,768]{2,1,0:T(8,128)(2,1)S(1)}, f32[2,16,128]{2,1,0:T(8,128)S(1)}, bf16[512,4096]{1,0:T(8,128)(2,1)S(1)}, f32[2,1,768]{2,1,0:T(1,128)...) custom-call(f32[16,128]{1,0:T(8,128)S(1)} %broadcast_in_dim.45.own_flags_ref, ...), custom_call_target="tpu_custom_call" | custom-call | flops 1024 | bytes 1024 | tf_op jit(solution)/shard_map/pallas_call | solution.py:220
  21.9 1.6 %shard_map.69 = (f32[2,1,768]{2,1,0:T(1,128)S(1)}, f32[2,1,768]{2,1,0:T(1,128)S(1)}, f32[2,128,768]{2,1,0:T(8,128)S(1)}, bf16[256,4096]{1,0:T(8,128)(2,1)S(1)}) custom-call(f32[2,16,128]{2,1,0:T(8,128)S(1)} %get-tuple-element.32.flags_ref, ...), custom_call_target="tpu_custom_call", output_to_operand_aliasing={{0}: (3, {}), {1}: (4, {}), {2}: (5, {})} | custom-call | flops 1024 | bytes 1024 | tf_op jit(solution)/shard_map/pallas_call | solution.py:301
  23.5 0.0 collective-permute-done.5.refs_0_
  23.6 1.6 %shard_map.70 = (f32[2,1,768]{2,1,0:T(1,128)S(1)}, f32[2,1,768]{2,1,0:T(1,128)S(1)}, f32[2,128,768]{2,1,0:T(8,128)S(1)}, bf16[256,4096]{1,0:T(8,128)(2,1)S(1)}) custom-call(f32[2,16,128]{2,1,0:T(8,128)S(1)} %get-tuple-element.32.flags_ref, ...), custom_call_target="tpu_custom_call", output_to_operand_aliasing={{0}: (3, {}), {1}: (4, {}), {2}: (5, {})} | custom-call | flops 1024 | bytes 1024 | tf_op jit(solution)/shard_map/pallas_call | solution.py:301
  25.2 0.0 collective-permute-done.4.refs_0_
  25.2 0.3 shard_map.71
  25.5 11.5 %all_to_all.5.parts_ref = f32[8,8,128]{2,1,0:T(8,128)S(1)} all-to-all(f32[8,8,128]{2,1,0:T(8,128)S(1)} %shard_map.71), channel_id=1, replica_groups=mesh['conv'=2,'seq'=8,'head'=2] {'seq'}, dimensions={0} | all-to-all | bytes 65536 | tf_op jit(solution)/shard_map/all_to_all | solution.py:422
  37.0 0.7 %shard_map.73 = f32[2,2048]{1,0:T(2,128)S(1)} custom-call(f32[8,8,128]{2,1,0:T(8,128)S(1)} %all_to_all.5.parts_ref, bf16[512,4096]{1,0:T(8,128)(2,1)S(1)} %get-tuple-element.46.refs_0_, bf16[256,4096]{1,0:T(8,128)(2,1)S(1)} %get-tuple-element.47.refs_1_, bf16[256,4096]{1,0:T(8,128)(2,1)S(1)} %get-tuple-element.48.refs_2_), custom_call_target="tpu_custom_call" | custom-call | flops 1024 | bytes 1024 | tf_op jit(solution)/shard_map/pallas_call | solution.py:345
  37.6 0.0 collective-permute-start.6
  37.6 0.7 %shard_map.72 = f32[2,2048]{1,0:T(2,128)S(1)} custom-call(f32[8,8,128]{2,1,0:T(8,128)S(1)} %all_to_all.5.parts_ref, bf16[512,4096]{1,0:T(8,128)(2,1)S(1)} %get-tuple-element.46.refs_0_, bf16[256,4096]{1,0:T(8,128)(2,1)S(1)} %get-tuple-element.47.refs_1_, bf16[256,4096]{1,0:T(8,128)(2,1)S(1)} %get-tuple-element.48.refs_2_), custom_call_target="tpu_custom_call" | custom-call | flops 1024 | bytes 1024 | tf_op jit(solution)/shard_map/pallas_call | solution.py:345
  38.3 0.5 %collective-permute-done.6 = f32[2,2048]{1,0:T(2,128)S(1)} collective-permute-done((f32[2,2048]{1,0:T(2,128)S(1)}, f32[2,2048]{1,0:T(2,128)S(1)}, u32[]{:S(2)}, u32[]{:S(2)}) %collective-permute-start.6) | collective-permute-done | bytes 16416 | tf_op jit(solution)/shard_map/ppermute | solution.py:424
  38.8 0.6 %add.10 = f32[2,2048]{1,0:T(2,128)} add(f32[2,2048]{1,0:T(2,128)S(1)} %shard_map.72, f32[2,2048]{1,0:T(2,128)S(1)} %collective-permute-done.6) | non-fusion elementwise | flops 4096 | bytes 49152 | tf_op jit(solution)/shard_map/add | solution.py:425
  (5 shorter events, 0.1 us)
Async XLA Ops:
  1.0 7.4 %collective-permute-start = (bf16[2,192,128]{2,1,0:T(8,128)(2,1)S(1)}, bf16[2,192,128]{2,1,0:T(8,128)(2,1)S(1)}, u32[]{:S(2)}, u32[]{:S(2)}) collective-permute-start(bf16[2,192,128]{2,1,0:T(8,128)(2,1)S(1)} %get-tuple-element.57), channel_id=1, source_target_pairs={{0,2},{2,0},{4,6},{6,4},{8,10},{10,8},{12,14},{14,12},{1,3},{3,1},... | collective-permute-start | bytes 294920 | tf_op jit(solution)/shard_map/ppermute | solution.py:359
  4.0 12.7 %collective-permute-start.2 = (bf16[2,192,128]{2,1,0:T(8,128)(2,1)S(1)}, bf16[2,192,128]{2,1,0:T(8,128)(2,1)S(1)}, u32[]{:S(2)}, u32[]{:S(2)}) collective-permute-start(bf16[2,192,128]{2,1,0:T(8,128)(2,1)S(1)} %get-tuple-element.58.refs_0_), channel_id=1, source_target_pairs={{0,4},{2,6},{4,8},{6,10},{8,12},{10,14},{1,5},{3,7},{5,9},{7,11},{... | collective-permute-start | bytes 294920 | tf_op jit(solution)/shard_map/ppermute | solution.py:364
  8.4 8.3 %collective-permute-start.3 = (bf16[2,192,128]{2,1,0:T(8,128)(2,1)S(1)}, bf16[2,192,128]{2,1,0:T(8,128)(2,1)S(1)}, u32[]{:S(2)}, u32[]{:S(2)}) collective-permute-start(bf16[2,192,128]{2,1,0:T(8,128)(2,1)S(1)} %shard_map.67), channel_id=1, source_target_pairs={{0,4},{2,6},{4,8},{6,10},{8,12},{10,14},{1,5},{3,7},{5,9},{7,11},{... | collective-permute-start | bytes 294920 | tf_op jit(solution)/shard_map/ppermute | solution.py:364
  13.1 6.2 %collective-permute-start.1 = (bf16[208,512]{1,0:T(8,128)(2,1)S(1)}, bf16[208,512]{1,0:T(8,128)(2,1)S(1)}, u32[]{:S(2)}, u32[]{:S(2)}) collective-permute-start(bf16[208,512]{1,0:T(8,128)(2,1)S(1)} %pad_maximum_fusion), channel_id=1, source_target_pairs={{0,2},{2,0},{4,6},{6,4},{8,10},{10,8},{12,14},{14,12},{1,3},{3,1},... | collective-permute-start | bytes 638984 | tf_op jit(solution)/shard_map/ppermute | solution.py:359
  13.7 9.9 %collective-permute-start.5 = (bf16[4,192,128]{2,1,0:T(8,128)(2,1)S(1)}, bf16[4,192,128]{2,1,0:T(8,128)(2,1)S(1)}, u32[]{:S(2)}, u32[]{:S(2)}) collective-permute-start(bf16[4,192,128]{2,1,0:T(8,128)(2,1)S(1)} %shard_map.64.refs_2_), channel_id=1, source_target_pairs={{0,12},{2,14},{1,13},{3,15},{16,28},{18,30},{17,29},{19,31}} | collective-permute-start | bytes 589832 | tf_op jit(solution)/shard_map/ppermute | solution.py:364
  16.8 8.4 %collective-permute-start.4 = (bf16[4,192,128]{2,1,0:T(8,128)(2,1)S(1)}, bf16[4,192,128]{2,1,0:T(8,128)(2,1)S(1)}, u32[]{:S(2)}, u32[]{:S(2)}) collective-permute-start(bf16[4,192,128]{2,1,0:T(8,128)(2,1)S(1)} %shard_map.68.refs_0_), channel_id=1, source_target_pairs={{4,8},{6,10},{8,12},{10,14},{5,9},{7,11},{9,13},{11,15},{20,24},{2... | collective-permute-start | bytes 589832 | tf_op jit(solution)/shard_map/ppermute | solution.py:364
  37.6 1.2 %collective-permute-start.6 = (f32[2,2048]{1,0:T(2,128)S(1)}, f32[2,2048]{1,0:T(2,128)S(1)}, u32[]{:S(2)}, u32[]{:S(2)}) collective-permute-start(f32[2,2048]{1,0:T(2,128)S(1)} %shard_map.73), channel_id=1, source_target_pairs={{0,1},{1,0},{2,3},{3,2},{4,5},{5,4},{6,7},{7,6},{8,9},{9,8},{10,11... | collective-permute-start | bytes 49160 | tf_op jit(solution)/shard_map/ppermute | solution.py:424

commit v10 on v6

--- a/solution.py
+++ b/solution.py
@@ -86,31 +86,33 @@
     values = [
         jnp.concatenate([kv_ref[2 * e + 1] for e in range(across)], axis=0).T for kv_ref in rows_refs
     ]
+    span = columns // 2 if columns % 256 == 0 else columns
+    pieces = [(e, slice(at, at + span)) for e in range(across) for at in range(0, columns, span)]
     logits = [
-        [jnp.dot(part, turned_ref[e], preferred_element_type=jnp.float32) for part in keys]
-        for e in range(across)
+        [jnp.dot(part, turned_ref[e, :, cut], preferred_element_type=jnp.float32) for part in keys]
+        for e, cut in pieces
     ]
-    if first:
-        key_pos = lax.broadcasted_iota(jnp.int32, (rows, 1), 0)
-        column = lax.broadcasted_iota(jnp.int32, (1, columns), 1)
-        causal = key_pos <= lax.rem(column, rows)
-    for e in range(across):
+    for number, (e, cut) in enumerate(pieces):
         blocks = [
-            logits[e][b // across][b % across * rows : (b % across + 1) * rows] for b in range(count)
+            logits[number][b // across][b % across * rows : (b % across + 1) * rows]
+            for b in range(count)
         ]
+        on = [None if switch is None else switch[:, cut] for switch in switches[e]]
         if first:
-            blocks[e] = jnp.where(causal, blocks[e], big_negative)
-        new_top = None if first else top[e]
+            key_pos = lax.broadcasted_iota(jnp.int32, (rows, 1), 0)
+            column = cut.start + lax.broadcasted_iota(jnp.int32, (1, span), 1)
+            blocks[e] = jnp.where(key_pos <= lax.rem(column, rows), blocks[e], big_negative)
+        new_top = None if first else top[e, :, cut]
         for b in range(count):
             block_top = jnp.ceil(jnp.max(blocks[b], axis=0, keepdims=True) * factor)
-            if switches[e][b] is not None:
-                block_top = jnp.where(switches[e][b], block_top, big_negative)
+            if on[b] is not None:
+                block_top = jnp.where(on[b], block_top, big_negative)
             new_top = block_top if new_top is None else jnp.maximum(new_top, block_top)
         weights, block_sum = [], None
         for b in range(count):
             against = new_top
-            if switches[e][b] is not None:
-                against = jnp.where(switches[e][b], new_top, -big_negative)
+            if on[b] is not None:
+                against = jnp.where(on[b], new_top, -big_negative)
             weights.append(jnp.exp2(blocks[b] * factor - against))
             part = jnp.sum(weights[b], axis=0, keepdims=True)
             block_sum = part if block_sum is None else block_sum + part
@@ -121,12 +123,12 @@
             part = jnp.dot(part, mine, preferred_element_type=jnp.float32)
             update = part if update is None else update + part
         if not first:
-            rescale = jnp.exp2(top[e] - new_top)
-            block_sum = total_sum[e] * rescale + block_sum
-            update = totals[e] * rescale + update
-        top[e] = new_top
-        total_sum[e] = block_sum
-        totals[e] = update
+            rescale = jnp.exp2(top[e, :, cut] - new_top)
+            block_sum = total_sum[e, :, cut] * rescale + block_sum
+            update = totals[e, :, cut] * rescale + update
+        top[e, :, cut] = new_top
+        total_sum[e, :, cut] = block_sum
+        totals[e, :, cut] = update
 
 
 def switch_of(flags_ref, e, owner, columns, allowed=None):

time: 39.8 us -> 39.8 us (level)
  no operation moved by 1% of the time
where the time goes in v10:
time: 39.8 us; the launch traced here: 39.4 us
  starting transfers between devices  14.3 us (36%)
  blocking collectives  11.8 us (30%)
  Pallas kernels  7.89 us (20%)
  other arithmetic  3.5 us (9%)
  waiting for transfers between devices  1.61 us (4%)
    all_to_all x1, blocking collectives, on_device(): lax.all_to_all(state[0], 'seq', split_axis=0, concat_axis=0, tiled=True)  11.8 us
    ppermute x4, starting transfers between devices, up(): return lax.ppermute(rows, 'seq', pairs)  10.7 us
    ppermute x2, starting transfers between devices, over(): return lax.ppermute(rows, 'seq', pairs)  3.6 us
    pallas_call x3, Pallas kernels, attend_next(): call(functools.partial(next_kernel, across, distances, turns, last, at),...  3.5 us
    pallas_call x1, Pallas kernels, attend_first(): call(functools.partial(first_kernel, across), [jax.ShapeDtypeStruct((acro...  2.29 us
    select_n x2, other arithmetic, pick(): jnp.where(number == part, rows[:, part * width:(part + 1) * width], picked)  1.94 us
    pallas_call x2, Pallas kernels, project(): call(functools.partial(project_kernel, across, other), jax.ShapeDtypeStru...  1.34 us
    ppermute x2, waiting for transfers between devices, over(): return lax.ppermute(rows, 'seq', pairs)  1.08 us
  transfers between devices with their start and end apart: 7, of which 2 were waited for; matrix products, arithmetic and copies ran while one was open for 5% of the time, Pallas kernels for 18%

profile of v10, /device:TPU:0, one launch (start us, length us, event | category | flops | bytes accessed | tf_op | source)
XLA Modules:
  0.0 39.4 jit_solution(8887972551368039001)
XLA Ops:
  0.0 0.9 %broadcast_select_fusion.4 = (bf16[192,128]{1,0:T(8,128)(2,1)S(1)}, bf16[192,128]{1,0:T(8,128)(2,1)S(1)}, bf16[192,128]{1,0:T(8,128)(2,1)S(1)}, bf16[192,128]{1,0:T(8,128)(2,1)S(1)}) fusion(pred[]{:T(512)S(6)} %eq.19, bf16[192,256]{1,0:T(8,128)(2,1)} %param.8, pred[]{:T(512)S(6)} %eq.17, bf16[192,256]{1,0:T(8,128)(2,1)} %param.7), kind=kLoop, calls=%fused_computation.5 | loop fusion | flops 98304 | bytes 393218 | tf_op jit(solution)/shard_map/jit(_where)/select_n | solution.py:49
  0.9 0.1 broadcast_select_fusion.2
  1.0 3.0 %collective-permute-start = (bf16[2,192,128]{2,1,0:T(8,128)(2,1)S(1)}, bf16[2,192,128]{2,1,0:T(8,128)(2,1)S(1)}, u32[]{:S(2)}, u32[]{:S(2)}) collective-permute-start(bf16[2,192,128]{2,1,0:T(8,128)(2,1)S(1)} %get-tuple-element.57), channel_id=1, source_target_pairs={{0,2},{2,0},{4,6},{6,4},{8,10},{10,8},{12,14},{14,12},{1,3},{3,1},... | collective-permute-start | bytes 294920 | tf_op jit(solution)/shard_map/ppermute | solution.py:361
  4.0 3.5 %collective-permute-start.2 = (bf16[2,192,128]{2,1,0:T(8,128)(2,1)S(1)}, bf16[2,192,128]{2,1,0:T(8,128)(2,1)S(1)}, u32[]{:S(2)}, u32[]{:S(2)}) collective-permute-start(bf16[2,192,128]{2,1,0:T(8,128)(2,1)S(1)} %get-tuple-element.58.refs_0_), channel_id=1, source_target_pairs={{0,4},{2,6},{4,8},{6,10},{8,12},{10,14},{1,5},{3,7},{5,9},{7,11},{... | collective-permute-start | bytes 294920 | tf_op jit(solution)/shard_map/ppermute | solution.py:366
  7.5 0.7 %pad_add_fusion.meta_ref = s32[24]{0:T(128)S(1)} fusion(s32[8]{0:T(128)} %bitcast.1, s32[16]{0:T(128)} %param.10), kind=kLoop, calls=%fused_computation.9 | loop fusion | flops 24 | bytes 192 | tf_op jit(solution)/shard_map/concatenate | solution.py:378
  8.3 0.1 slice.33
  8.3 0.1 pad.6.clone
  8.4 0.0 collective-permute-done.refs_1_.refs_0_
  8.4 3.5 %collective-permute-start.3 = (bf16[2,192,128]{2,1,0:T(8,128)(2,1)S(1)}, bf16[2,192,128]{2,1,0:T(8,128)(2,1)S(1)}, u32[]{:S(2)}, u32[]{:S(2)}) collective-permute-start(bf16[2,192,128]{2,1,0:T(8,128)(2,1)S(1)} %shard_map.67), channel_id=1, source_target_pairs={{0,4},{2,6},{4,8},{6,10},{8,12},{10,14},{1,5},{3,7},{5,9},{7,11},{... | collective-permute-start | bytes 294920 | tf_op jit(solution)/shard_map/ppermute | solution.py:366
  11.9 1.1 %broadcast_select_fusion = (bf16[192,512]{1,0:T(8,128)(2,1)S(1)}, bf16[192,512]{1,0:T(8,128)(2,1)S(1)}) fusion(pred[]{:T(512)S(6)} %eq.19, bf16[192,1024]{1,0:T(8,128)(2,1)} %param.6, pred[]{:T(512)S(6)} %eq.17), kind=kLoop, calls=%fused_computation.1 | loop fusion | flops 196608 | bytes 786434 | tf_op jit(solution)/shard_map/jit(_where)/select_n | solution.py:49
  13.0 0.1 pad_maximum_fusion
  13.1 0.6 %collective-permute-start.1 = (bf16[208,512]{1,0:T(8,128)(2,1)S(1)}, bf16[208,512]{1,0:T(8,128)(2,1)S(1)}, u32[]{:S(2)}, u32[]{:S(2)}) collective-permute-start(bf16[208,512]{1,0:T(8,128)(2,1)S(1)} %pad_maximum_fusion), channel_id=1, source_target_pairs={{0,2},{2,0},{4,6},{6,4},{8,10},{10,8},{12,14},{14,12},{1,3},{3,1},... | collective-permute-start | bytes 638984 | tf_op jit(solution)/shard_map/ppermute | solution.py:361
  13.7 3.0 %collective-permute-start.5 = (bf16[4,192,128]{2,1,0:T(8,128)(2,1)S(1)}, bf16[4,192,128]{2,1,0:T(8,128)(2,1)S(1)}, u32[]{:S(2)}, u32[]{:S(2)}) collective-permute-start(bf16[4,192,128]{2,1,0:T(8,128)(2,1)S(1)} %shard_map.64.refs_2_), channel_id=1, source_target_pairs={{0,12},{2,14},{1,13},{3,15},{16,28},{18,30},{17,29},{19,31}} | collective-permute-start | bytes 589832 | tf_op jit(solution)/shard_map/ppermute | solution.py:366
  16.7 0.0 collective-permute-done.2.refs_0_
  16.7 0.0 collective-permute-done.3.refs_1_
  16.8 0.7 %collective-permute-start.4 = (bf16[4,192,128]{2,1,0:T(8,128)(2,1)S(1)}, bf16[4,192,128]{2,1,0:T(8,128)(2,1)S(1)}, u32[]{:S(2)}, u32[]{:S(2)}) collective-permute-start(bf16[4,192,128]{2,1,0:T(8,128)(2,1)S(1)} %shard_map.68.refs_0_), channel_id=1, source_target_pairs={{4,8},{6,10},{8,12},{10,14},{5,9},{7,11},{9,13},{11,15},{20,24},{2... | collective-permute-start | bytes 589832 | tf_op jit(solution)/shard_map/ppermute | solution.py:366
  17.4 0.7 %shard_map.65 = (bf16[2,64,768]{2,1,0:T(8,128)(2,1)S(1)}, f32[16,128]{1,0:T(8,128)S(1)}) custom-call(s32[24]{0:T(128)S(1)} %pad_add_fusion.meta_ref, bf16[192,512]{1,0:T(8,128)(2,1)S(1)} %get-tuple-element.50.after_ref.refs_0_), custom_call_target="tpu_custom_call" | custom-call | flops 1024 | bytes 1024 | tf_op jit(solution)/shard_map/pallas_call | solution.py:171
  18.2 0.1 broadcast_in_dim.45.own_flags_ref
  18.2 1.1 %collective-permute-done.1.refs_1_ = bf16[208,512]{1,0:T(8,128)(2,1)S(1)} collective-permute-done((bf16[208,512]{1,0:T(8,128)(2,1)S(1)}, bf16[208,512]{1,0:T(8,128)(2,1)S(1)}, u32[]{:S(2)}, u32[]{:S(2)}) %collective-permute-start.1) | collective-permute-done | bytes 213024 | tf_op jit(solution)/shard_map/ppermute | solution.py:361
  19.3 2.3 %shard_map.66 = (bf16[2,128,768]{2,1,0:T(8,128)(2,1)S(1)}, f32[2,16,128]{2,1,0:T(8,128)S(1)}, bf16[512,4096]{1,0:T(8,128)(2,1)S(1)}, f32[2,1,768]{2,1,0:T(1,128)...) custom-call(f32[16,128]{1,0:T(8,128)S(1)} %broadcast_in_dim.45.own_flags_ref, ...), custom_call_target="tpu_custom_call" | custom-call | flops 1024 | bytes 1024 | tf_op jit(solution)/shard_map/pallas_call | solution.py:222
  21.6 1.6 %shard_map.69 = (f32[2,1,768]{2,1,0:T(1,128)S(1)}, f32[2,1,768]{2,1,0:T(1,128)S(1)}, f32[2,128,768]{2,1,0:T(8,128)S(1)}, bf16[256,4096]{1,0:T(8,128)(2,1)S(1)}) custom-call(f32[2,16,128]{2,1,0:T(8,128)S(1)} %get-tuple-element.32.flags_ref, ...), custom_call_target="tpu_custom_call", output_to_operand_aliasing={{0}: (3, {}), {1}: (4, {}), {2}: (5, {})} | custom-call | flops 1024 | bytes 1024 | tf_op jit(solution)/shard_map/pallas_call | solution.py:303
  23.2 0.0 collective-permute-done.5.refs_0_
  23.2 1.6 %shard_map.70 = (f32[2,1,768]{2,1,0:T(1,128)S(1)}, f32[2,1,768]{2,1,0:T(1,128)S(1)}, f32[2,128,768]{2,1,0:T(8,128)S(1)}, bf16[256,4096]{1,0:T(8,128)(2,1)S(1)}) custom-call(f32[2,16,128]{2,1,0:T(8,128)S(1)} %get-tuple-element.32.flags_ref, ...), custom_call_target="tpu_custom_call", output_to_operand_aliasing={{0}: (3, {}), {1}: (4, {}), {2}: (5, {})} | custom-call | flops 1024 | bytes 1024 | tf_op jit(solution)/shard_map/pallas_call | solution.py:303
  24.9 0.0 collective-permute-done.4.refs_0_
  24.9 0.3 shard_map.71
  25.2 11.8 %all_to_all.5.parts_ref = f32[8,2,512]{2,1,0:T(2,128)S(1)} all-to-all(f32[8,2,512]{2,1,0:T(2,128)S(1)} %shard_map.71), channel_id=1, replica_groups=mesh['conv'=2,'seq'=8,'head'=2] {'seq'}, dimensions={0} | all-to-all | bytes 65536 | tf_op jit(solution)/shard_map/all_to_all | solution.py:424
  36.9 0.7 %shard_map.73 = f32[2,2048]{1,0:T(2,128)S(1)} custom-call(f32[8,2,512]{2,1,0:T(2,128)S(1)} %all_to_all.5.parts_ref, bf16[512,4096]{1,0:T(8,128)(2,1)S(1)} %get-tuple-element.46.refs_0_, bf16[256,4096]{1,0:T(8,128)(2,1)S(1)} %get-tuple-element.47.refs_1_, bf16[256,4096]{1,0:T(8,128)(2,1)S(1)} %get-tuple-element.48.refs_2_), custom_call_target="tpu_custom_call" | custom-call | flops 1024 | bytes 1024 | tf_op jit(solution)/shard_map/pallas_call | solution.py:347
  37.6 0.0 collective-permute-start.6
  37.6 0.7 %shard_map.72 = f32[2,2048]{1,0:T(2,128)S(1)} custom-call(f32[8,2,512]{2,1,0:T(2,128)S(1)} %all_to_all.5.parts_ref, bf16[512,4096]{1,0:T(8,128)(2,1)S(1)} %get-tuple-element.46.refs_0_, bf16[256,4096]{1,0:T(8,128)(2,1)S(1)} %get-tuple-element.47.refs_1_, bf16[256,4096]{1,0:T(8,128)(2,1)S(1)} %get-tuple-element.48.refs_2_), custom_call_target="tpu_custom_call" | custom-call | flops 1024 | bytes 1024 | tf_op jit(solution)/shard_map/pallas_call | solution.py:347
  38.3 0.5 %collective-permute-done.6 = f32[2,2048]{1,0:T(2,128)S(1)} collective-permute-done((f32[2,2048]{1,0:T(2,128)S(1)}, f32[2,2048]{1,0:T(2,128)S(1)}, u32[]{:S(2)}, u32[]{:S(2)}) %collective-permute-start.6) | collective-permute-done | bytes 16416 | tf_op jit(solution)/shard_map/ppermute | solution.py:426
  38.8 0.6 %add.10 = f32[2,2048]{1,0:T(2,128)} add(f32[2,2048]{1,0:T(2,128)S(1)} %shard_map.72, f32[2,2048]{1,0:T(2,128)S(1)} %collective-permute-done.6) | non-fusion elementwise | flops 4096 | bytes 49152 | tf_op jit(solution)/shard_map/add | solution.py:427
  (5 shorter events, 0.1 us)
Async XLA Ops:
  1.0 7.4 %collective-permute-start = (bf16[2,192,128]{2,1,0:T(8,128)(2,1)S(1)}, bf16[2,192,128]{2,1,0:T(8,128)(2,1)S(1)}, u32[]{:S(2)}, u32[]{:S(2)}) collective-permute-start(bf16[2,192,128]{2,1,0:T(8,128)(2,1)S(1)} %get-tuple-element.57), channel_id=1, source_target_pairs={{0,2},{2,0},{4,6},{6,4},{8,10},{10,8},{12,14},{14,12},{1,3},{3,1},... | collective-permute-start | bytes 294920 | tf_op jit(solution)/shard_map/ppermute | solution.py:361
  4.0 12.7 %collective-permute-start.2 = (bf16[2,192,128]{2,1,0:T(8,128)(2,1)S(1)}, bf16[2,192,128]{2,1,0:T(8,128)(2,1)S(1)}, u32[]{:S(2)}, u32[]{:S(2)}) collective-permute-start(bf16[2,192,128]{2,1,0:T(8,128)(2,1)S(1)} %get-tuple-element.58.refs_0_), channel_id=1, source_target_pairs={{0,4},{2,6},{4,8},{6,10},{8,12},{10,14},{1,5},{3,7},{5,9},{7,11},{... | collective-permute-start | bytes 294920 | tf_op jit(solution)/shard_map/ppermute | solution.py:366
  8.4 8.3 %collective-permute-start.3 = (bf16[2,192,128]{2,1,0:T(8,128)(2,1)S(1)}, bf16[2,192,128]{2,1,0:T(8,128)(2,1)S(1)}, u32[]{:S(2)}, u32[]{:S(2)}) collective-permute-start(bf16[2,192,128]{2,1,0:T(8,128)(2,1)S(1)} %shard_map.67), channel_id=1, source_target_pairs={{0,4},{2,6},{4,8},{6,10},{8,12},{10,14},{1,5},{3,7},{5,9},{7,11},{... | collective-permute-start | bytes 294920 | tf_op jit(solution)/shard_map/ppermute | solution.py:366
  13.1 6.2 %collective-permute-start.1 = (bf16[208,512]{1,0:T(8,128)(2,1)S(1)}, bf16[208,512]{1,0:T(8,128)(2,1)S(1)}, u32[]{:S(2)}, u32[]{:S(2)}) collective-permute-start(bf16[208,512]{1,0:T(8,128)(2,1)S(1)} %pad_maximum_fusion), channel_id=1, source_target_pairs={{0,2},{2,0},{4,6},{6,4},{8,10},{10,8},{12,14},{14,12},{1,3},{3,1},... | collective-permute-start | bytes 638984 | tf_op jit(solution)/shard_map/ppermute | solution.py:361
  13.7 9.6 %collective-permute-start.5 = (bf16[4,192,128]{2,1,0:T(8,128)(2,1)S(1)}, bf16[4,192,128]{2,1,0:T(8,128)(2,1)S(1)}, u32[]{:S(2)}, u32[]{:S(2)}) collective-permute-start(bf16[4,192,128]{2,1,0:T(8,128)(2,1)S(1)} %shard_map.64.refs_2_), channel_id=1, source_target_pairs={{0,12},{2,14},{1,13},{3,15},{16,28},{18,30},{17,29},{19,31}} | collective-permute-start | bytes 589832 | tf_op jit(solution)/shard_map/ppermute | solution.py:366
  16.8 8.1 %collective-permute-start.4 = (bf16[4,192,128]{2,1,0:T(8,128)(2,1)S(1)}, bf16[4,192,128]{2,1,0:T(8,128)(2,1)S(1)}, u32[]{:S(2)}, u32[]{:S(2)}) collective-permute-start(bf16[4,192,128]{2,1,0:T(8,128)(2,1)S(1)} %shard_map.68.refs_0_), channel_id=1, source_target_pairs={{4,8},{6,10},{8,12},{10,14},{5,9},{7,11},{9,13},{11,15},{20,24},{2... | collective-permute-start | bytes 589832 | tf_op jit(solution)/shard_map/ppermute | solution.py:366
  37.6 1.2 %collective-permute-start.6 = (f32[2,2048]{1,0:T(2,128)S(1)}, f32[2,2048]{1,0:T(2,128)S(1)}, u32[]{:S(2)}, u32[]{:S(2)}) collective-permute-start(f32[2,2048]{1,0:T(2,128)S(1)} %shard_map.73), channel_id=1, source_target_pairs={{0,1},{1,0},{2,3},{3,2},{4,5},{5,4},{6,7},{7,6},{8,9},{9,8},{10,11... | collective-permute-start | bytes 49160 | tf_op jit(solution)/shard_map/ppermute | solution.py:426

commit v11 on v10

--- a/solution.py
+++ b/solution.py
@@ -14,7 +14,7 @@
 log_two_e = 1.4426950408889634
 
 big_limit = 45 * 1024 * 1024
-small_cost = pl.CostEstimate(flops=1024, bytes_accessed=1024, transcendentals=0)
+long_flops = 4 * 10**9
 
 in_vmem = pl.BlockSpec(memory_space=pltpu.VMEM)
 in_smem = pl.BlockSpec(memory_space=pltpu.SMEM)
@@ -32,12 +32,13 @@
 
 def call(kernel, out_shape, **settings):
     limit = settings.pop("limit", 16 * 1024 * 1024)
+    flops = settings.pop("flops", 0)
     return pl.pallas_call(
         kernel,
         out_shape=out_shape,
         out_specs=jax.tree.map(lambda _: in_vmem, out_shape),
         compiler_params=pltpu.CompilerParams(vmem_limit_bytes=limit),
-        cost_estimate=small_cost,
+        cost_estimate=pl.CostEstimate(flops=flops, bytes_accessed=1024, transcendentals=0),
         **settings,
     )
 
@@ -176,11 +177,32 @@
         ],
         in_specs=[in_smem, anywhere],
         scratch_shapes=[pltpu.VMEM((turns, columns), jnp.float32)],
+        flops=long_flops,
     )(meta, group)
 
 
 def weight_piece(weight_ref, out_ref, start, sem):
     return pltpu.make_async_copy(weight_ref.at[start : start + out_ref.shape[0]], out_ref, sem)
+
+
+def early_kernel(across, start, weight_ref, _, out_ref, copied):
+    z, _ = place(across)
+
+    @pl.when(z == 0)
+    def _():
+        copy = weight_piece(weight_ref, out_ref, start, copied)
+        copy.start()
+        copy.wait()
+
+
+def early_piece(across, weight, start, piece, after):
+    return call(
+        functools.partial(early_kernel, across, start),
+        jax.ShapeDtypeStruct((piece, weight.shape[1]), weight.dtype),
+        in_specs=[anywhere] * 2,
+        scratch_shapes=[pltpu.SemaphoreType.DMA(())],
+        limit=big_limit,
+    )(weight, after)
 
 
 def first_kernel(across, own_flags_ref, *refs):
@@ -235,7 +257,7 @@
     )(flags, *queries, rows, weight)
 
 
-def next_kernel(across, distances, turns, last, weight_at, flags_ref, turned_ref, *refs):
+def next_kernel(across, distances, turns, last, weight_at, early_at, flags_ref, turned_ref, *refs):
     below_count = len(distances)
     below, state, refs = refs[:below_count], refs[below_count : below_count + 3], refs[below_count + 3 :]
     if weight_at is not None:
@@ -244,6 +266,13 @@
         weight_copy = weight_piece(weight_ref, weight_out, weight_at, copied)
         weight_copy.start()
     z, y = place(across)
+    if early_at is not None:
+        weight_ref, early_out, copied = refs[1], refs[-2], refs[-1]
+
+        @pl.when(z != 0)
+        def _():
+            weight_piece(weight_ref, early_out, early_at, copied).start()
+
     columns = turned_ref.shape[2]
 
     def update(rows, from_distances):
@@ -263,6 +292,12 @@
 
     if weight_at is not None:
         weight_copy.wait()
+    if early_at is not None:
+
+        @pl.when(z != 0)
+        def _():
+            weight_piece(weight_ref, early_out, early_at, copied).wait()
+
     if last:
         member_ref, inverse_ref, out_ref = refs
         rows = out_ref.shape[1]
@@ -282,7 +317,7 @@
                 out_ref[s, :, r * HD : (r + 1) * HD] = mean[s * rows : (s + 1) * rows]
 
 
-def attend_next(across, distances, turns, turned, flags, below, state, pool, out_piece, weight, at, piece):
+def attend_next(across, distances, turns, turned, flags, below, state, pool, out_piece, weight, at, piece, early=None):
     last = pool is not None
     args = [flags, turned, *below, *state]
     in_specs = [in_vmem] * len(args)
@@ -291,6 +326,14 @@
         args.append(weight)
         in_specs.append(anywhere)
         scratch = [pltpu.SemaphoreType.DMA(())]
+    if early is not None:
+        early_at = weight.shape[0] - early.shape[0]
+        early_aliases = {len(args): len(state)}
+        args += [early, weight]
+        in_specs += [in_vmem, anywhere]
+        scratch = [pltpu.SemaphoreType.DMA(())]
+    else:
+        early_at, early_aliases = None, {}
     if last:
         args += list(pool)
         in_specs += [in_vmem] * len(pool)
@@ -300,13 +343,16 @@
         aliases = {2 + len(below) + i: i for i in range(len(state))}
     if at is not None:
         out_shape.append(jax.ShapeDtypeStruct((piece, weight.shape[1]), weight.dtype))
+    if early is not None:
+        out_shape.append(jax.ShapeDtypeStruct(early.shape, early.dtype))
+        aliases.update(early_aliases)
     return call(
-        functools.partial(next_kernel, across, distances, turns, last, at),
+        functools.partial(next_kernel, across, distances, turns, last, at, early_at),
         out_shape,
         in_specs=in_specs,
         scratch_shapes=scratch,
         input_output_aliases=aliases,
-        limit=big_limit if at is not None else 16 * 1024 * 1024,
+        limit=big_limit if scratch else 16 * 1024 * 1024,
     )(*args)
 
 
@@ -385,7 +431,9 @@
         sent.append(jnp.concatenate([group, under], axis=0))
     flags = jnp.broadcast_to(flags, (padded, HD)).astype(jnp.float32)
     below = [rows, join_parts([first, rest], 2 * across)] + [None] * (down - 2)
-    far, *sent = lax.optimization_barrier((rows, *sent))
+    early = early_piece(across, out_weight, out_weight.shape[0] - out_weight.shape[0] // 8, out_weight.shape[0] // 8, groups[0])
+    far, early = lax.optimization_barrier((rows, early))
+    early, *sent = lax.optimization_barrier((early, *sent))
     others = [over(group, shift) for shift, group in enumerate(sent, 1)]
     for distance in range(3, down):
         below[distance] = up(far, distance)
@@ -394,7 +442,7 @@
     member, inverse = members(across, turns, meta, groups[0])
     inverse, flags = lax.optimization_barrier((inverse, flags))
     depth = out_weight.shape[0]
-    pieces = [4 * depth // 8, 2 * depth // 8, 2 * depth // 8]
+    pieces = [4 * depth // 8, 3 * depth // 8, depth // 8]
     turned, flags, weight, *state = attend_first(
         across, flags, [groups[0], *others], rows, out_weight, pieces[0]
     )
@@ -403,7 +451,7 @@
     stages = [[1]] + [list(range(d, min(d + 2, down))) for d in range(3, down, 2)] + [[2]]
     for number, distances in enumerate(stages):
         last = number == len(stages) - 1
-        with_weight = number < 2
+        with_weight = number == 0
         state = attend_next(
             across,
             distances,
@@ -417,8 +465,9 @@
             out_weight,
             sum(pieces[: len(weights)]) if with_weight else None,
             pieces[len(weights)] if with_weight else None,
+            early if number == 1 else None,
         )
-        if with_weight:
+        if with_weight or number == 1:
             *state, weight = state
             weights.append(weight)
     parts = lax.all_to_all(state[0], "seq", split_axis=0, concat_axis=0, tiled=True)

time: 39.8 us -> 39.6 us (level)
  waiting for transfers between devices: 1.61 us -> 4.15 us
  blocking collectives: 11.8 us -> 10.3 us
  starting transfers between devices: 14.3 us -> 13.1 us
    ppermute x2, waiting for transfers between devices: 1.08 us -> 3.62 us  [over(): return lax.ppermute(rows, 'seq', pairs)]
    ppermute x4, starting transfers between devices: 10.7 us -> 8.93 us  [up(): return lax.ppermute(rows, 'seq', pairs)]
    all_to_all x1, blocking collectives: 11.8 us -> 10.3 us  [on_device(): lax.all_to_all(state[0], 'seq', split_axis=0, concat_axis=0, tiled=True)]
    ppermute x2, starting transfers between devices: 3.6 us -> 4.12 us  [over(): return lax.ppermute(rows, 'seq', pairs)]
    pallas_call x3 -> x4, Pallas kernels: 3.5 us -> 3.48 us  [the longest x3 2.23 us: attend_next(): call(functools.partial(next_kernel, across, distances, turns, last, at, e...]
where the time goes in v11:
time: 39.6 us; the launch traced here: 39.2 us
  starting transfers between devices  13.1 us (33%)
  blocking collectives  10.3 us (26%)
  Pallas kernels  7.87 us (20%)
  waiting for transfers between devices  4.15 us (10%)
  other arithmetic  3.5 us (9%)
    all_to_all x1, blocking collectives, on_device(): lax.all_to_all(state[0], 'seq', split_axis=0, concat_axis=0, tiled=True)  10.3 us
    ppermute x4, starting transfers between devices, up(): return lax.ppermute(rows, 'seq', pairs)  8.93 us
    ppermute x2, starting transfers between devices, over(): return lax.ppermute(rows, 'seq', pairs)  4.12 us
    ppermute x2, waiting for transfers between devices, over(): return lax.ppermute(rows, 'seq', pairs)  3.62 us
    pallas_call x1, Pallas kernels, attend_first(): call(functools.partial(first_kernel, across), [jax.ShapeDtypeStruct((acro...  2.29 us
    pallas_call x3, Pallas kernels, attend_next(): call(functools.partial(next_kernel, across, distances, turns, last, at, e...  2.23 us
    select_n x2, other arithmetic, pick(): jnp.where(number == part, rows[:, part * width:(part + 1) * width], picked)  1.94 us
    pallas_call x2, Pallas kernels, project(): call(functools.partial(project_kernel, across, other), jax.ShapeDtypeStru...  1.34 us
  transfers between devices with their start and end apart: 7, of which 2 were waited for; matrix products, arithmetic and copies ran while one was open for 5% of the time, Pallas kernels for 18%

profile of v11, /device:TPU:0, one launch (start us, length us, event | category | flops | bytes accessed | tf_op | source)
XLA Modules:
  0.0 39.2 jit_solution(7976040575816294049)
XLA Ops:
  0.0 0.9 %broadcast_select_fusion.4 = (bf16[192,128]{1,0:T(8,128)(2,1)S(1)}, bf16[192,128]{1,0:T(8,128)(2,1)S(1)}, bf16[192,128]{1,0:T(8,128)(2,1)S(1)}, bf16[192,128]{1,0:T(8,128)(2,1)S(1)}) fusion(pred[]{:T(512)S(6)} %eq.19, bf16[192,256]{1,0:T(8,128)(2,1)} %param.8, pred[]{:T(512)S(6)} %eq.17, bf16[192,256]{1,0:T(8,128)(2,1)} %param.7), kind=kLoop, calls=%fused_computation.5 | loop fusion | flops 98304 | bytes 393218 | tf_op jit(solution)/shard_map/jit(_where)/select_n | solution.py:50
  0.9 0.1 broadcast_select_fusion.2
  1.0 3.0 %collective-permute-start = (bf16[2,192,128]{2,1,0:T(8,128)(2,1)S(1)}, bf16[2,192,128]{2,1,0:T(8,128)(2,1)S(1)}, u32[]{:S(2)}, u32[]{:S(2)}) collective-permute-start(bf16[2,192,128]{2,1,0:T(8,128)(2,1)S(1)} %get-tuple-element.61), channel_id=1, source_target_pairs={{0,2},{2,0},{4,6},{6,4},{8,10},{10,8},{12,14},{14,12},{1,3},{3,1},... | collective-permute-start | bytes 294920 | tf_op jit(solution)/shard_map/ppermute | solution.py:407
  4.0 3.5 %collective-permute-start.2 = (bf16[2,192,128]{2,1,0:T(8,128)(2,1)S(1)}, bf16[2,192,128]{2,1,0:T(8,128)(2,1)S(1)}, u32[]{:S(2)}, u32[]{:S(2)}) collective-permute-start(bf16[2,192,128]{2,1,0:T(8,128)(2,1)S(1)} %get-tuple-element.62.refs_0_), channel_id=1, source_target_pairs={{0,4},{2,6},{4,8},{6,10},{8,12},{10,14},{1,5},{3,7},{5,9},{7,11},{... | collective-permute-start | bytes 294920 | tf_op jit(solution)/shard_map/ppermute | solution.py:412
  7.5 0.7 %pad_add_fusion.meta_ref = s32[24]{0:T(128)S(1)} fusion(s32[8]{0:T(128)} %bitcast.1, s32[16]{0:T(128)} %param.10), kind=kLoop, calls=%fused_computation.9 | loop fusion | flops 24 | bytes 192 | tf_op jit(solution)/shard_map/concatenate | solution.py:424
  8.3 0.1 slice.33
  8.3 0.1 pad.6.clone
  8.4 0.0 collective-permute-done.refs_1_.refs_0_
  8.4 3.5 %collective-permute-start.3 = (bf16[2,192,128]{2,1,0:T(8,128)(2,1)S(1)}, bf16[2,192,128]{2,1,0:T(8,128)(2,1)S(1)}, u32[]{:S(2)}, u32[]{:S(2)}) collective-permute-start(bf16[2,192,128]{2,1,0:T(8,128)(2,1)S(1)} %shard_map.68), channel_id=1, source_target_pairs={{0,4},{2,6},{4,8},{6,10},{8,12},{10,14},{1,5},{3,7},{5,9},{7,11},{... | collective-permute-start | bytes 294920 | tf_op jit(solution)/shard_map/ppermute | solution.py:412
  11.9 1.1 %broadcast_select_fusion = (bf16[192,512]{1,0:T(8,128)(2,1)S(1)}, bf16[192,512]{1,0:T(8,128)(2,1)S(1)}) fusion(pred[]{:T(512)S(6)} %eq.19, bf16[192,1024]{1,0:T(8,128)(2,1)} %param.6, pred[]{:T(512)S(6)} %eq.17), kind=kLoop, calls=%fused_computation.1 | loop fusion | flops 196608 | bytes 786434 | tf_op jit(solution)/shard_map/jit(_where)/select_n | solution.py:50
  13.0 0.1 pad_maximum_fusion
  13.1 1.2 %shard_map.66.refs_4_ = bf16[128,4096]{1,0:T(8,128)(2,1)S(1)} custom-call(bf16[1024,4096]{1,0:T(8,128)(2,1)} %refs_5_.1, bf16[192,512]{1,0:T(8,128)(2,1)S(1)} %get-tuple-element.54.after_ref._.refs_0_), custom_call_target="tpu_custom_call" | custom-call | bytes 1024 | tf_op jit(solution)/shard_map/pallas_call | solution.py:199
  14.4 1.3 %collective-permute-start.5 = (bf16[4,192,128]{2,1,0:T(8,128)(2,1)S(1)}, bf16[4,192,128]{2,1,0:T(8,128)(2,1)S(1)}, u32[]{:S(2)}, u32[]{:S(2)}) collective-permute-start(bf16[4,192,128]{2,1,0:T(8,128)(2,1)S(1)} %shard_map.64.refs_2_), channel_id=1, source_target_pairs={{0,12},{2,14},{1,13},{3,15},{16,28},{18,30},{17,29},{19,31}} | collective-permute-start | bytes 589832 | tf_op jit(solution)/shard_map/ppermute | solution.py:412
  15.7 1.1 %collective-permute-start.1 = (bf16[208,512]{1,0:T(8,128)(2,1)S(1)}, bf16[208,512]{1,0:T(8,128)(2,1)S(1)}, u32[]{:S(2)}, u32[]{:S(2)}) collective-permute-start(bf16[208,512]{1,0:T(8,128)(2,1)S(1)} %pad_maximum_fusion), channel_id=1, source_target_pairs={{0,2},{2,0},{4,6},{6,4},{8,10},{10,8},{12,14},{14,12},{1,3},{3,1},... | collective-permute-start | bytes 638984 | tf_op jit(solution)/shard_map/ppermute | solution.py:407
  16.8 0.0 collective-permute-done.2.refs_0_
  16.8 0.0 collective-permute-done.3.refs_1_
  16.8 0.7 %collective-permute-start.4 = (bf16[4,192,128]{2,1,0:T(8,128)(2,1)S(1)}, bf16[4,192,128]{2,1,0:T(8,128)(2,1)S(1)}, u32[]{:S(2)}, u32[]{:S(2)}) collective-permute-start(bf16[4,192,128]{2,1,0:T(8,128)(2,1)S(1)} %shard_map.69.refs_0_), channel_id=1, source_target_pairs={{4,8},{6,10},{8,12},{10,14},{5,9},{7,11},{9,13},{11,15},{20,24},{2... | collective-permute-start | bytes 589832 | tf_op jit(solution)/shard_map/ppermute | solution.py:412
  17.5 0.7 %shard_map.65 = (bf16[2,64,768]{2,1,0:T(8,128)(2,1)S(1)}, f32[16,128]{1,0:T(8,128)S(1)}) custom-call(s32[24]{0:T(128)S(1)} %pad_add_fusion.meta_ref, bf16[192,512]{1,0:T(8,128)(2,1)S(1)} %get-tuple-element.54.after_ref._.refs_0_), custom_call_target="tpu_custom_call" | custom-call | flops 4000000000 | bytes 1024 | tf_op jit(solution)/shard_map/pallas_call | solution.py:172
  18.2 0.1 broadcast_in_dim.45.own_flags_ref
  18.3 3.6 %collective-permute-done.1.refs_1_ = bf16[208,512]{1,0:T(8,128)(2,1)S(1)} collective-permute-done((bf16[208,512]{1,0:T(8,128)(2,1)S(1)}, bf16[208,512]{1,0:T(8,128)(2,1)S(1)}, u32[]{:S(2)}, u32[]{:S(2)}) %collective-permute-start.1) | collective-permute-done | bytes 213024 | tf_op jit(solution)/shard_map/ppermute | solution.py:407
  21.9 2.3 %shard_map.67 = (bf16[2,128,768]{2,1,0:T(8,128)(2,1)S(1)}, f32[2,16,128]{2,1,0:T(8,128)S(1)}, bf16[512,4096]{1,0:T(8,128)(2,1)S(1)}, f32[2,1,768]{2,1,0:T(1,128)...) custom-call(f32[16,128]{1,0:T(8,128)S(1)} %broadcast_in_dim.45.own_flags_ref, ...), custom_call_target="tpu_custom_call" | custom-call | bytes 1024 | tf_op jit(solution)/shard_map/pallas_call | solution.py:244
  24.2 1.9 %shard_map.70 = (f32[2,1,768]{2,1,0:T(1,128)S(1)}, f32[2,1,768]{2,1,0:T(1,128)S(1)}, f32[2,128,768]{2,1,0:T(8,128)S(1)}, bf16[384,4096]{1,0:T(8,128)(2,1)S(1)}) custom-call(f32[2,16,128]{2,1,0:T(8,128)S(1)} %get-tuple-element.35.flags_ref, ...), custom_call_target="tpu_custom_call", output_to_operand_aliasing={{0}: (3, {}), {1}: (4, {}), {2}: (5, {})} | custom-call | bytes 1024 | tf_op jit(solution)/shard_map/pallas_call | solution.py:349
  26.1 0.0 collective-permute-done.5.refs_0_
  26.1 0.0 collective-permute-done.4.refs_0_
  26.2 0.3 shard_map.72
  26.4 10.3 %all_to_all.5.parts_ref = f32[8,2,512]{2,1,0:T(2,128)S(1)} all-to-all(f32[8,2,512]{2,1,0:T(2,128)S(1)} %shard_map.72), channel_id=1, replica_groups=mesh['conv'=2,'seq'=8,'head'=2] {'seq'}, dimensions={0} | all-to-all | bytes 65536 | tf_op jit(solution)/shard_map/all_to_all | solution.py:473
  36.8 0.7 %shard_map.74 = f32[2,2048]{1,0:T(2,128)S(1)} custom-call(f32[8,2,512]{2,1,0:T(2,128)S(1)} %all_to_all.5.parts_ref, bf16[512,4096]{1,0:T(8,128)(2,1)S(1)} %get-tuple-element.50.refs_0_, bf16[384,4096]{1,0:T(8,128)(2,1)S(1)} %get-tuple-element.51.refs_1_, bf16[128,4096]{1,0:T(8,128)(2,1)S(1)} %get-tuple-element.52.refs_2_), custom_call_target="tpu_custom_call" | custom-call | bytes 1024 | tf_op jit(solution)/shard_map/pallas_call | solution.py:393
  37.4 0.0 collective-permute-start.6
  37.4 0.7 %shard_map.73 = f32[2,2048]{1,0:T(2,128)S(1)} custom-call(f32[8,2,512]{2,1,0:T(2,128)S(1)} %all_to_all.5.parts_ref, bf16[512,4096]{1,0:T(8,128)(2,1)S(1)} %get-tuple-element.50.refs_0_, bf16[384,4096]{1,0:T(8,128)(2,1)S(1)} %get-tuple-element.51.refs_1_, bf16[128,4096]{1,0:T(8,128)(2,1)S(1)} %get-tuple-element.52.refs_2_), custom_call_target="tpu_custom_call" | custom-call | bytes 1024 | tf_op jit(solution)/shard_map/pallas_call | solution.py:393
  38.1 0.5 %collective-permute-done.6 = f32[2,2048]{1,0:T(2,128)S(1)} collective-permute-done((f32[2,2048]{1,0:T(2,128)S(1)}, f32[2,2048]{1,0:T(2,128)S(1)}, u32[]{:S(2)}, u32[]{:S(2)}) %collective-permute-start.6) | collective-permute-done | bytes 16416 | tf_op jit(solution)/shard_map/ppermute | solution.py:475
  38.6 0.6 %add.10 = f32[2,2048]{1,0:T(2,128)} add(f32[2,2048]{1,0:T(2,128)S(1)} %shard_map.73, f32[2,2048]{1,0:T(2,128)S(1)} %collective-permute-done.6) | non-fusion elementwise | flops 4096 | bytes 49152 | tf_op jit(solution)/shard_map/add | solution.py:476
  (6 shorter events, 0.1 us)
Async XLA Ops:
  1.0 7.4 %collective-permute-start = (bf16[2,192,128]{2,1,0:T(8,128)(2,1)S(1)}, bf16[2,192,128]{2,1,0:T(8,128)(2,1)S(1)}, u32[]{:S(2)}, u32[]{:S(2)}) collective-permute-start(bf16[2,192,128]{2,1,0:T(8,128)(2,1)S(1)} %get-tuple-element.61), channel_id=1, source_target_pairs={{0,2},{2,0},{4,6},{6,4},{8,10},{10,8},{12,14},{14,12},{1,3},{3,1},... | collective-permute-start | bytes 294920 | tf_op jit(solution)/shard_map/ppermute | solution.py:407
  4.0 12.7 %collective-permute-start.2 = (bf16[2,192,128]{2,1,0:T(8,128)(2,1)S(1)}, bf16[2,192,128]{2,1,0:T(8,128)(2,1)S(1)}, u32[]{:S(2)}, u32[]{:S(2)}) collective-permute-start(bf16[2,192,128]{2,1,0:T(8,128)(2,1)S(1)} %get-tuple-element.62.refs_0_), channel_id=1, source_target_pairs={{0,4},{2,6},{4,8},{6,10},{8,12},{10,14},{1,5},{3,7},{5,9},{7,11},{... | collective-permute-start | bytes 294920 | tf_op jit(solution)/shard_map/ppermute | solution.py:412
  8.4 8.3 %collective-permute-start.3 = (bf16[2,192,128]{2,1,0:T(8,128)(2,1)S(1)}, bf16[2,192,128]{2,1,0:T(8,128)(2,1)S(1)}, u32[]{:S(2)}, u32[]{:S(2)}) collective-permute-start(bf16[2,192,128]{2,1,0:T(8,128)(2,1)S(1)} %shard_map.68), channel_id=1, source_target_pairs={{0,4},{2,6},{4,8},{6,10},{8,12},{10,14},{1,5},{3,7},{5,9},{7,11},{... | collective-permute-start | bytes 294920 | tf_op jit(solution)/shard_map/ppermute | solution.py:412
  14.4 11.7 %collective-permute-start.5 = (bf16[4,192,128]{2,1,0:T(8,128)(2,1)S(1)}, bf16[4,192,128]{2,1,0:T(8,128)(2,1)S(1)}, u32[]{:S(2)}, u32[]{:S(2)}) collective-permute-start(bf16[4,192,128]{2,1,0:T(8,128)(2,1)S(1)} %shard_map.64.refs_2_), channel_id=1, source_target_pairs={{0,12},{2,14},{1,13},{3,15},{16,28},{18,30},{17,29},{19,31}} | collective-permute-start | bytes 589832 | tf_op jit(solution)/shard_map/ppermute | solution.py:412
  15.7 6.2 %collective-permute-start.1 = (bf16[208,512]{1,0:T(8,128)(2,1)S(1)}, bf16[208,512]{1,0:T(8,128)(2,1)S(1)}, u32[]{:S(2)}, u32[]{:S(2)}) collective-permute-start(bf16[208,512]{1,0:T(8,128)(2,1)S(1)} %pad_maximum_fusion), channel_id=1, source_target_pairs={{0,2},{2,0},{4,6},{6,4},{8,10},{10,8},{12,14},{14,12},{1,3},{3,1},... | collective-permute-start | bytes 638984 | tf_op jit(solution)/shard_map/ppermute | solution.py:407
  16.8 9.4 %collective-permute-start.4 = (bf16[4,192,128]{2,1,0:T(8,128)(2,1)S(1)}, bf16[4,192,128]{2,1,0:T(8,128)(2,1)S(1)}, u32[]{:S(2)}, u32[]{:S(2)}) collective-permute-start(bf16[4,192,128]{2,1,0:T(8,128)(2,1)S(1)} %shard_map.69.refs_0_), channel_id=1, source_target_pairs={{4,8},{6,10},{8,12},{10,14},{5,9},{7,11},{9,13},{11,15},{20,24},{2... | collective-permute-start | bytes 589832 | tf_op jit(solution)/shard_map/ppermute | solution.py:412
  37.4 1.2 %collective-permute-start.6 = (f32[2,2048]{1,0:T(2,128)S(1)}, f32[2,2048]{1,0:T(2,128)S(1)}, u32[]{:S(2)}, u32[]{:S(2)}) collective-permute-start(f32[2,2048]{1,0:T(2,128)S(1)} %shard_map.74), channel_id=1, source_target_pairs={{0,1},{1,0},{2,3},{3,2},{4,5},{5,4},{6,7},{7,6},{8,9},{9,8},{10,11... | collective-permute-start | bytes 49160 | tf_op jit(solution)/shard_map/ppermute | solution.py:475

commit v12 on v11

--- a/solution.py
+++ b/solution.py
@@ -431,7 +431,9 @@
         sent.append(jnp.concatenate([group, under], axis=0))
     flags = jnp.broadcast_to(flags, (padded, HD)).astype(jnp.float32)
     below = [rows, join_parts([first, rest], 2 * across)] + [None] * (down - 2)
-    early = early_piece(across, out_weight, out_weight.shape[0] - out_weight.shape[0] // 8, out_weight.shape[0] // 8, groups[0])
+    early = early_piece(
+        across, out_weight, out_weight.shape[0] * 3 // 4, out_weight.shape[0] // 4, groups[0]
+    )
     far, early = lax.optimization_barrier((rows, early))
     early, *sent = lax.optimization_barrier((early, *sent))
     others = [over(group, shift) for shift, group in enumerate(sent, 1)]
@@ -442,7 +444,7 @@
     member, inverse = members(across, turns, meta, groups[0])
     inverse, flags = lax.optimization_barrier((inverse, flags))
     depth = out_weight.shape[0]
-    pieces = [4 * depth // 8, 3 * depth // 8, depth // 8]
+    pieces = [4 * depth // 8, 2 * depth // 8]
     turned, flags, weight, *state = attend_first(
         across, flags, [groups[0], *others], rows, out_weight, pieces[0]
     )

time: 39.6 us -> 40 us (1.010)
  starting transfers between devices: 13.1 us -> 12.7 us
where the time goes in v12:
time: 40 us; the launch traced here: 39.6 us
  starting transfers between devices  12.7 us (32%)
  blocking collectives  10.6 us (26%)
  Pallas kernels  7.94 us (20%)
  waiting for transfers between devices  4.52 us (11%)
  other arithmetic  3.5 us (9%)
    all_to_all x1, blocking collectives, on_device(): lax.all_to_all(state[0], 'seq', split_axis=0, concat_axis=0, tiled=True)  10.6 us
    ppermute x4, starting transfers between devices, up(): return lax.ppermute(rows, 'seq', pairs)  8.93 us
    ppermute x2, waiting for transfers between devices, over(): return lax.ppermute(rows, 'seq', pairs)  3.99 us
    ppermute x2, starting transfers between devices, over(): return lax.ppermute(rows, 'seq', pairs)  3.75 us
    pallas_call x1, Pallas kernels, attend_first(): call(functools.partial(first_kernel, across), [jax.ShapeDtypeStruct((acro...  2.29 us
    select_n x2, other arithmetic, pick(): jnp.where(number == part, rows[:, part * width:(part + 1) * width], picked)  1.94 us
    pallas_call x3, Pallas kernels, attend_next(): call(functools.partial(next_kernel, across, distances, turns, last, at, e...  1.93 us
    pallas_call x1, Pallas kernels, early_piece(): call(functools.partial(early_kernel, across, start), jax.ShapeDtypeStruct...  1.62 us
  transfers between devices with their start and end apart: 7, of which 2 were waited for; matrix products, arithmetic and copies ran while one was open for 5% of the time, Pallas kernels for 18%

profile of v12, /device:TPU:0, one launch (start us, length us, event | category | flops | bytes accessed | tf_op | source)
XLA Modules:
  0.0 39.6 jit_solution(4820944013438058618)
XLA Ops:
  0.0 0.9 %broadcast_select_fusion.4 = (bf16[192,128]{1,0:T(8,128)(2,1)S(1)}, bf16[192,128]{1,0:T(8,128)(2,1)S(1)}, bf16[192,128]{1,0:T(8,128)(2,1)S(1)}, bf16[192,128]{1,0:T(8,128)(2,1)S(1)}) fusion(pred[]{:T(512)S(6)} %eq.19, bf16[192,256]{1,0:T(8,128)(2,1)} %param.8, pred[]{:T(512)S(6)} %eq.17, bf16[192,256]{1,0:T(8,128)(2,1)} %param.7), kind=kLoop, calls=%fused_computation.5 | loop fusion | flops 98304 | bytes 393218 | tf_op jit(solution)/shard_map/jit(_where)/select_n | solution.py:50
  0.9 0.1 broadcast_select_fusion.2
  1.0 3.0 %collective-permute-start = (bf16[2,192,128]{2,1,0:T(8,128)(2,1)S(1)}, bf16[2,192,128]{2,1,0:T(8,128)(2,1)S(1)}, u32[]{:S(2)}, u32[]{:S(2)}) collective-permute-start(bf16[2,192,128]{2,1,0:T(8,128)(2,1)S(1)} %get-tuple-element.61), channel_id=1, source_target_pairs={{0,2},{2,0},{4,6},{6,4},{8,10},{10,8},{12,14},{14,12},{1,3},{3,1},... | collective-permute-start | bytes 294920 | tf_op jit(solution)/shard_map/ppermute | solution.py:407
  4.0 3.5 %collective-permute-start.2 = (bf16[2,192,128]{2,1,0:T(8,128)(2,1)S(1)}, bf16[2,192,128]{2,1,0:T(8,128)(2,1)S(1)}, u32[]{:S(2)}, u32[]{:S(2)}) collective-permute-start(bf16[2,192,128]{2,1,0:T(8,128)(2,1)S(1)} %get-tuple-element.62.refs_0_), channel_id=1, source_target_pairs={{0,4},{2,6},{4,8},{6,10},{8,12},{10,14},{1,5},{3,7},{5,9},{7,11},{... | collective-permute-start | bytes 294920 | tf_op jit(solution)/shard_map/ppermute | solution.py:412
  7.5 0.7 %pad_add_fusion.meta_ref = s32[24]{0:T(128)S(1)} fusion(s32[8]{0:T(128)} %bitcast.1, s32[16]{0:T(128)} %param.10), kind=kLoop, calls=%fused_computation.9 | loop fusion | flops 24 | bytes 192 | tf_op jit(solution)/shard_map/concatenate | solution.py:424
  8.3 0.1 slice.33
  8.3 0.1 pad.6.clone
  8.4 0.0 collective-permute-done.refs_1_.refs_0_
  8.4 3.5 %collective-permute-start.3 = (bf16[2,192,128]{2,1,0:T(8,128)(2,1)S(1)}, bf16[2,192,128]{2,1,0:T(8,128)(2,1)S(1)}, u32[]{:S(2)}, u32[]{:S(2)}) collective-permute-start(bf16[2,192,128]{2,1,0:T(8,128)(2,1)S(1)} %shard_map.68), channel_id=1, source_target_pairs={{0,4},{2,6},{4,8},{6,10},{8,12},{10,14},{1,5},{3,7},{5,9},{7,11},{... | collective-permute-start | bytes 294920 | tf_op jit(solution)/shard_map/ppermute | solution.py:412
  11.9 1.1 %broadcast_select_fusion = (bf16[192,512]{1,0:T(8,128)(2,1)S(1)}, bf16[192,512]{1,0:T(8,128)(2,1)S(1)}) fusion(pred[]{:T(512)S(6)} %eq.19, bf16[192,1024]{1,0:T(8,128)(2,1)} %param.6, pred[]{:T(512)S(6)} %eq.17), kind=kLoop, calls=%fused_computation.1 | loop fusion | flops 196608 | bytes 786434 | tf_op jit(solution)/shard_map/jit(_where)/select_n | solution.py:50
  13.0 0.1 pad_maximum_fusion
  13.1 1.6 %shard_map.66.refs_4_ = bf16[256,4096]{1,0:T(8,128)(2,1)S(1)} custom-call(bf16[1024,4096]{1,0:T(8,128)(2,1)} %refs_5_.1, bf16[192,512]{1,0:T(8,128)(2,1)S(1)} %get-tuple-element.54.after_ref._.refs_0_), custom_call_target="tpu_custom_call" | custom-call | bytes 1024 | tf_op jit(solution)/shard_map/pallas_call | solution.py:199
  14.7 1.3 %collective-permute-start.5 = (bf16[4,192,128]{2,1,0:T(8,128)(2,1)S(1)}, bf16[4,192,128]{2,1,0:T(8,128)(2,1)S(1)}, u32[]{:S(2)}, u32[]{:S(2)}) collective-permute-start(bf16[4,192,128]{2,1,0:T(8,128)(2,1)S(1)} %shard_map.64.refs_2_), channel_id=1, source_target_pairs={{0,12},{2,14},{1,13},{3,15},{16,28},{18,30},{17,29},{19,31}} | collective-permute-start | bytes 589832 | tf_op jit(solution)/shard_map/ppermute | solution.py:412
  16.0 0.7 %collective-permute-start.1 = (bf16[208,512]{1,0:T(8,128)(2,1)S(1)}, bf16[208,512]{1,0:T(8,128)(2,1)S(1)}, u32[]{:S(2)}, u32[]{:S(2)}) collective-permute-start(bf16[208,512]{1,0:T(8,128)(2,1)S(1)} %pad_maximum_fusion), channel_id=1, source_target_pairs={{0,2},{2,0},{4,6},{6,4},{8,10},{10,8},{12,14},{14,12},{1,3},{3,1},... | collective-permute-start | bytes 638984 | tf_op jit(solution)/shard_map/ppermute | solution.py:407
  16.8 0.0 collective-permute-done.2.refs_0_
  16.8 0.0 collective-permute-done.3.refs_1_
  16.8 0.7 %collective-permute-start.4 = (bf16[4,192,128]{2,1,0:T(8,128)(2,1)S(1)}, bf16[4,192,128]{2,1,0:T(8,128)(2,1)S(1)}, u32[]{:S(2)}, u32[]{:S(2)}) collective-permute-start(bf16[4,192,128]{2,1,0:T(8,128)(2,1)S(1)} %shard_map.69.refs_0_), channel_id=1, source_target_pairs={{4,8},{6,10},{8,12},{10,14},{5,9},{7,11},{9,13},{11,15},{20,24},{2... | collective-permute-start | bytes 589832 | tf_op jit(solution)/shard_map/ppermute | solution.py:412
  17.5 0.7 %shard_map.65 = (bf16[2,64,768]{2,1,0:T(8,128)(2,1)S(1)}, f32[16,128]{1,0:T(8,128)S(1)}) custom-call(s32[24]{0:T(128)S(1)} %pad_add_fusion.meta_ref, bf16[192,512]{1,0:T(8,128)(2,1)S(1)} %get-tuple-element.54.after_ref._.refs_0_), custom_call_target="tpu_custom_call" | custom-call | flops 4000000000 | bytes 1024 | tf_op jit(solution)/shard_map/pallas_call | solution.py:172
  18.2 0.1 broadcast_in_dim.45.own_flags_ref
  18.3 4.0 %collective-permute-done.1.refs_1_ = bf16[208,512]{1,0:T(8,128)(2,1)S(1)} collective-permute-done((bf16[208,512]{1,0:T(8,128)(2,1)S(1)}, bf16[208,512]{1,0:T(8,128)(2,1)S(1)}, u32[]{:S(2)}, u32[]{:S(2)}) %collective-permute-start.1) | collective-permute-done | bytes 213024 | tf_op jit(solution)/shard_map/ppermute | solution.py:407
  22.3 2.3 %shard_map.67 = (bf16[2,128,768]{2,1,0:T(8,128)(2,1)S(1)}, f32[2,16,128]{2,1,0:T(8,128)S(1)}, bf16[512,4096]{1,0:T(8,128)(2,1)S(1)}, f32[2,1,768]{2,1,0:T(1,128)...) custom-call(f32[16,128]{1,0:T(8,128)S(1)} %broadcast_in_dim.45.own_flags_ref, ...), custom_call_target="tpu_custom_call" | custom-call | bytes 1024 | tf_op jit(solution)/shard_map/pallas_call | solution.py:244
  24.6 1.6 %shard_map.70 = (f32[2,1,768]{2,1,0:T(1,128)S(1)}, f32[2,1,768]{2,1,0:T(1,128)S(1)}, f32[2,128,768]{2,1,0:T(8,128)S(1)}, bf16[256,4096]{1,0:T(8,128)(2,1)S(1)}) custom-call(f32[2,16,128]{2,1,0:T(8,128)S(1)} %get-tuple-element.35.flags_ref, ...), custom_call_target="tpu_custom_call", output_to_operand_aliasing={{0}: (3, {}), {1}: (4, {}), {2}: (5, {})} | custom-call | bytes 1024 | tf_op jit(solution)/shard_map/pallas_call | solution.py:349
  26.2 0.0 collective-permute-done.5.refs_0_
  26.2 0.0 collective-permute-done.4.refs_0_
  26.2 0.3 shard_map.72
  26.5 10.6 %all_to_all.5.parts_ref = f32[8,2,512]{2,1,0:T(2,128)S(1)} all-to-all(f32[8,2,512]{2,1,0:T(2,128)S(1)} %shard_map.72), channel_id=1, replica_groups=mesh['conv'=2,'seq'=8,'head'=2] {'seq'}, dimensions={0} | all-to-all | bytes 65536 | tf_op jit(solution)/shard_map/all_to_all | solution.py:475
  37.1 0.7 %shard_map.74 = f32[2,2048]{1,0:T(2,128)S(1)} custom-call(f32[8,2,512]{2,1,0:T(2,128)S(1)} %all_to_all.5.parts_ref, bf16[512,4096]{1,0:T(8,128)(2,1)S(1)} %get-tuple-element.50.refs_0_, bf16[256,4096]{1,0:T(8,128)(2,1)S(1)} %get-tuple-element.51.refs_1_, bf16[256,4096]{1,0:T(8,128)(2,1)S(1)} %get-tuple-element.52.refs_2_), custom_call_target="tpu_custom_call" | custom-call | bytes 1024 | tf_op jit(solution)/shard_map/pallas_call | solution.py:393
  37.8 0.0 collective-permute-start.6
  37.8 0.7 %shard_map.73 = f32[2,2048]{1,0:T(2,128)S(1)} custom-call(f32[8,2,512]{2,1,0:T(2,128)S(1)} %all_to_all.5.parts_ref, bf16[512,4096]{1,0:T(8,128)(2,1)S(1)} %get-tuple-element.50.refs_0_, bf16[256,4096]{1,0:T(8,128)(2,1)S(1)} %get-tuple-element.51.refs_1_, bf16[256,4096]{1,0:T(8,128)(2,1)S(1)} %get-tuple-element.52.refs_2_), custom_call_target="tpu_custom_call" | custom-call | bytes 1024 | tf_op jit(solution)/shard_map/pallas_call | solution.py:393
  38.5 0.5 %collective-permute-done.6 = f32[2,2048]{1,0:T(2,128)S(1)} collective-permute-done((f32[2,2048]{1,0:T(2,128)S(1)}, f32[2,2048]{1,0:T(2,128)S(1)}, u32[]{:S(2)}, u32[]{:S(2)}) %collective-permute-start.6) | collective-permute-done | bytes 16416 | tf_op jit(solution)/shard_map/ppermute | solution.py:477
  39.0 0.6 %add.10 = f32[2,2048]{1,0:T(2,128)} add(f32[2,2048]{1,0:T(2,128)S(1)} %shard_map.73, f32[2,2048]{1,0:T(2,128)S(1)} %collective-permute-done.6) | non-fusion elementwise | flops 4096 | bytes 49152 | tf_op jit(solution)/shard_map/add | solution.py:478
  (6 shorter events, 0.1 us)
Async XLA Ops:
  1.0 7.4 %collective-permute-start = (bf16[2,192,128]{2,1,0:T(8,128)(2,1)S(1)}, bf16[2,192,128]{2,1,0:T(8,128)(2,1)S(1)}, u32[]{:S(2)}, u32[]{:S(2)}) collective-permute-start(bf16[2,192,128]{2,1,0:T(8,128)(2,1)S(1)} %get-tuple-element.61), channel_id=1, source_target_pairs={{0,2},{2,0},{4,6},{6,4},{8,10},{10,8},{12,14},{14,12},{1,3},{3,1},... | collective-permute-start | bytes 294920 | tf_op jit(solution)/shard_map/ppermute | solution.py:407
  4.0 12.7 %collective-permute-start.2 = (bf16[2,192,128]{2,1,0:T(8,128)(2,1)S(1)}, bf16[2,192,128]{2,1,0:T(8,128)(2,1)S(1)}, u32[]{:S(2)}, u32[]{:S(2)}) collective-permute-start(bf16[2,192,128]{2,1,0:T(8,128)(2,1)S(1)} %get-tuple-element.62.refs_0_), channel_id=1, source_target_pairs={{0,4},{2,6},{4,8},{6,10},{8,12},{10,14},{1,5},{3,7},{5,9},{7,11},{... | collective-permute-start | bytes 294920 | tf_op jit(solution)/shard_map/ppermute | solution.py:412
  8.4 8.3 %collective-permute-start.3 = (bf16[2,192,128]{2,1,0:T(8,128)(2,1)S(1)}, bf16[2,192,128]{2,1,0:T(8,128)(2,1)S(1)}, u32[]{:S(2)}, u32[]{:S(2)}) collective-permute-start(bf16[2,192,128]{2,1,0:T(8,128)(2,1)S(1)} %shard_map.68), channel_id=1, source_target_pairs={{0,4},{2,6},{4,8},{6,10},{8,12},{10,14},{1,5},{3,7},{5,9},{7,11},{... | collective-permute-start | bytes 294920 | tf_op jit(solution)/shard_map/ppermute | solution.py:412
  14.7 11.4 %collective-permute-start.5 = (bf16[4,192,128]{2,1,0:T(8,128)(2,1)S(1)}, bf16[4,192,128]{2,1,0:T(8,128)(2,1)S(1)}, u32[]{:S(2)}, u32[]{:S(2)}) collective-permute-start(bf16[4,192,128]{2,1,0:T(8,128)(2,1)S(1)} %shard_map.64.refs_2_), channel_id=1, source_target_pairs={{0,12},{2,14},{1,13},{3,15},{16,28},{18,30},{17,29},{19,31}} | collective-permute-start | bytes 589832 | tf_op jit(solution)/shard_map/ppermute | solution.py:412
  16.0 6.2 %collective-permute-start.1 = (bf16[208,512]{1,0:T(8,128)(2,1)S(1)}, bf16[208,512]{1,0:T(8,128)(2,1)S(1)}, u32[]{:S(2)}, u32[]{:S(2)}) collective-permute-start(bf16[208,512]{1,0:T(8,128)(2,1)S(1)} %pad_maximum_fusion), channel_id=1, source_target_pairs={{0,2},{2,0},{4,6},{6,4},{8,10},{10,8},{12,14},{14,12},{1,3},{3,1},... | collective-permute-start | bytes 638984 | tf_op jit(solution)/shard_map/ppermute | solution.py:407
  16.8 9.4 %collective-permute-start.4 = (bf16[4,192,128]{2,1,0:T(8,128)(2,1)S(1)}, bf16[4,192,128]{2,1,0:T(8,128)(2,1)S(1)}, u32[]{:S(2)}, u32[]{:S(2)}) collective-permute-start(bf16[4,192,128]{2,1,0:T(8,128)(2,1)S(1)} %shard_map.69.refs_0_), channel_id=1, source_target_pairs={{4,8},{6,10},{8,12},{10,14},{5,9},{7,11},{9,13},{11,15},{20,24},{2... | collective-permute-start | bytes 589832 | tf_op jit(solution)/shard_map/ppermute | solution.py:412
  37.8 1.2 %collective-permute-start.6 = (f32[2,2048]{1,0:T(2,128)S(1)}, f32[2,2048]{1,0:T(2,128)S(1)}, u32[]{:S(2)}, u32[]{:S(2)}) collective-permute-start(f32[2,2048]{1,0:T(2,128)S(1)} %shard_map.74), channel_id=1, source_target_pairs={{0,1},{1,0},{2,3},{3,2},{4,5},{5,4},{6,7},{7,6},{8,9},{9,8},{10,11... | collective-permute-start | bytes 49160 | tf_op jit(solution)/shard_map/ppermute | solution.py:477

commit v13 on v11

--- a/solution.py
+++ b/solution.py
@@ -442,7 +442,7 @@
     member, inverse = members(across, turns, meta, groups[0])
     inverse, flags = lax.optimization_barrier((inverse, flags))
     depth = out_weight.shape[0]
-    pieces = [4 * depth // 8, 3 * depth // 8, depth // 8]
+    pieces = [5 * depth // 8, 2 * depth // 8, depth // 8]
     turned, flags, weight, *state = attend_first(
         across, flags, [groups[0], *others], rows, out_weight, pieces[0]
     )

time: 39.6 us -> 39.6 us (level)
  no operation moved by 1% of the time
where the time goes in v13:
time: 39.6 us; the launch traced here: 39.2 us
  starting transfers between devices  13.1 us (33%)
  blocking collectives  10.3 us (26%)
  Pallas kernels  7.87 us (20%)
  waiting for transfers between devices  4.15 us (10%)
  other arithmetic  3.5 us (9%)
    all_to_all x1, blocking collectives, on_device(): lax.all_to_all(state[0], 'seq', split_axis=0, concat_axis=0, tiled=True)  10.3 us
    ppermute x4, starting transfers between devices, up(): return lax.ppermute(rows, 'seq', pairs)  8.93 us
    ppermute x2, starting transfers between devices, over(): return lax.ppermute(rows, 'seq', pairs)  4.12 us
    ppermute x2, waiting for transfers between devices, over(): return lax.ppermute(rows, 'seq', pairs)  3.62 us
    pallas_call x1, Pallas kernels, attend_first(): call(functools.partial(first_kernel, across), [jax.ShapeDtypeStruct((acro...  2.58 us
    select_n x2, other arithmetic, pick(): jnp.where(number == part, rows[:, part * width:(part + 1) * width], picked)  1.94 us
    pallas_call x3, Pallas kernels, attend_next(): call(functools.partial(next_kernel, across, distances, turns, last, at, e...  1.93 us
    pallas_call x2, Pallas kernels, project(): call(functools.partial(project_kernel, across, other), jax.ShapeDtypeStru...  1.34 us
  transfers between devices with their start and end apart: 7, of which 2 were waited for; matrix products, arithmetic and copies ran while one was open for 5% of the time, Pallas kernels for 18%

profile of v13, /device:TPU:0, one launch (start us, length us, event | category | flops | bytes accessed | tf_op | source)
XLA Modules:
  0.0 39.2 jit_solution(15602997291019058367)
XLA Ops:
  0.0 0.9 %broadcast_select_fusion.4 = (bf16[192,128]{1,0:T(8,128)(2,1)S(1)}, bf16[192,128]{1,0:T(8,128)(2,1)S(1)}, bf16[192,128]{1,0:T(8,128)(2,1)S(1)}, bf16[192,128]{1,0:T(8,128)(2,1)S(1)}) fusion(pred[]{:T(512)S(6)} %eq.19, bf16[192,256]{1,0:T(8,128)(2,1)} %param.8, pred[]{:T(512)S(6)} %eq.17, bf16[192,256]{1,0:T(8,128)(2,1)} %param.7), kind=kLoop, calls=%fused_computation.5 | loop fusion | flops 98304 | bytes 393218 | tf_op jit(solution)/shard_map/jit(_where)/select_n | solution.py:50
  0.9 0.1 broadcast_select_fusion.2
  1.0 3.0 %collective-permute-start = (bf16[2,192,128]{2,1,0:T(8,128)(2,1)S(1)}, bf16[2,192,128]{2,1,0:T(8,128)(2,1)S(1)}, u32[]{:S(2)}, u32[]{:S(2)}) collective-permute-start(bf16[2,192,128]{2,1,0:T(8,128)(2,1)S(1)} %get-tuple-element.61), channel_id=1, source_target_pairs={{0,2},{2,0},{4,6},{6,4},{8,10},{10,8},{12,14},{14,12},{1,3},{3,1},... | collective-permute-start | bytes 294920 | tf_op jit(solution)/shard_map/ppermute | solution.py:407
  4.0 3.5 %collective-permute-start.2 = (bf16[2,192,128]{2,1,0:T(8,128)(2,1)S(1)}, bf16[2,192,128]{2,1,0:T(8,128)(2,1)S(1)}, u32[]{:S(2)}, u32[]{:S(2)}) collective-permute-start(bf16[2,192,128]{2,1,0:T(8,128)(2,1)S(1)} %get-tuple-element.62.refs_0_), channel_id=1, source_target_pairs={{0,4},{2,6},{4,8},{6,10},{8,12},{10,14},{1,5},{3,7},{5,9},{7,11},{... | collective-permute-start | bytes 294920 | tf_op jit(solution)/shard_map/ppermute | solution.py:412
  7.5 0.7 %pad_add_fusion.meta_ref = s32[24]{0:T(128)S(1)} fusion(s32[8]{0:T(128)} %bitcast.1, s32[16]{0:T(128)} %param.10), kind=kLoop, calls=%fused_computation.9 | loop fusion | flops 24 | bytes 192 | tf_op jit(solution)/shard_map/concatenate | solution.py:424
  8.3 0.1 slice.33
  8.3 0.1 pad.6.clone
  8.4 0.0 collective-permute-done.refs_1_.refs_0_
  8.4 3.5 %collective-permute-start.3 = (bf16[2,192,128]{2,1,0:T(8,128)(2,1)S(1)}, bf16[2,192,128]{2,1,0:T(8,128)(2,1)S(1)}, u32[]{:S(2)}, u32[]{:S(2)}) collective-permute-start(bf16[2,192,128]{2,1,0:T(8,128)(2,1)S(1)} %shard_map.68), channel_id=1, source_target_pairs={{0,4},{2,6},{4,8},{6,10},{8,12},{10,14},{1,5},{3,7},{5,9},{7,11},{... | collective-permute-start | bytes 294920 | tf_op jit(solution)/shard_map/ppermute | solution.py:412
  11.9 1.1 %broadcast_select_fusion = (bf16[192,512]{1,0:T(8,128)(2,1)S(1)}, bf16[192,512]{1,0:T(8,128)(2,1)S(1)}) fusion(pred[]{:T(512)S(6)} %eq.19, bf16[192,1024]{1,0:T(8,128)(2,1)} %param.6, pred[]{:T(512)S(6)} %eq.17), kind=kLoop, calls=%fused_computation.1 | loop fusion | flops 196608 | bytes 786434 | tf_op jit(solution)/shard_map/jit(_where)/select_n | solution.py:50
  13.0 0.1 pad_maximum_fusion
  13.1 1.2 %shard_map.66.refs_4_ = bf16[128,4096]{1,0:T(8,128)(2,1)S(1)} custom-call(bf16[1024,4096]{1,0:T(8,128)(2,1)} %refs_5_.1, bf16[192,512]{1,0:T(8,128)(2,1)S(1)} %get-tuple-element.54.after_ref._.refs_0_), custom_call_target="tpu_custom_call" | custom-call | bytes 1024 | tf_op jit(solution)/shard_map/pallas_call | solution.py:199
  14.4 1.3 %collective-permute-start.5 = (bf16[4,192,128]{2,1,0:T(8,128)(2,1)S(1)}, bf16[4,192,128]{2,1,0:T(8,128)(2,1)S(1)}, u32[]{:S(2)}, u32[]{:S(2)}) collective-permute-start(bf16[4,192,128]{2,1,0:T(8,128)(2,1)S(1)} %shard_map.64.refs_2_), channel_id=1, source_target_pairs={{0,12},{2,14},{1,13},{3,15},{16,28},{18,30},{17,29},{19,31}} | collective-permute-start | bytes 589832 | tf_op jit(solution)/shard_map/ppermute | solution.py:412
  15.7 1.1 %collective-permute-start.1 = (bf16[208,512]{1,0:T(8,128)(2,1)S(1)}, bf16[208,512]{1,0:T(8,128)(2,1)S(1)}, u32[]{:S(2)}, u32[]{:S(2)}) collective-permute-start(bf16[208,512]{1,0:T(8,128)(2,1)S(1)} %pad_maximum_fusion), channel_id=1, source_target_pairs={{0,2},{2,0},{4,6},{6,4},{8,10},{10,8},{12,14},{14,12},{1,3},{3,1},... | collective-permute-start | bytes 638984 | tf_op jit(solution)/shard_map/ppermute | solution.py:407
  16.8 0.0 collective-permute-done.2.refs_0_
  16.8 0.0 collective-permute-done.3.refs_1_
  16.8 0.7 %collective-permute-start.4 = (bf16[4,192,128]{2,1,0:T(8,128)(2,1)S(1)}, bf16[4,192,128]{2,1,0:T(8,128)(2,1)S(1)}, u32[]{:S(2)}, u32[]{:S(2)}) collective-permute-start(bf16[4,192,128]{2,1,0:T(8,128)(2,1)S(1)} %shard_map.69.refs_0_), channel_id=1, source_target_pairs={{4,8},{6,10},{8,12},{10,14},{5,9},{7,11},{9,13},{11,15},{20,24},{2... | collective-permute-start | bytes 589832 | tf_op jit(solution)/shard_map/ppermute | solution.py:412
  17.5 0.7 %shard_map.65 = (bf16[2,64,768]{2,1,0:T(8,128)(2,1)S(1)}, f32[16,128]{1,0:T(8,128)S(1)}) custom-call(s32[24]{0:T(128)S(1)} %pad_add_fusion.meta_ref, bf16[192,512]{1,0:T(8,128)(2,1)S(1)} %get-tuple-element.54.after_ref._.refs_0_), custom_call_target="tpu_custom_call" | custom-call | flops 4000000000 | bytes 1024 | tf_op jit(solution)/shard_map/pallas_call | solution.py:172
  18.2 0.1 broadcast_in_dim.45.own_flags_ref
  18.3 3.6 %collective-permute-done.1.refs_1_ = bf16[208,512]{1,0:T(8,128)(2,1)S(1)} collective-permute-done((bf16[208,512]{1,0:T(8,128)(2,1)S(1)}, bf16[208,512]{1,0:T(8,128)(2,1)S(1)}, u32[]{:S(2)}, u32[]{:S(2)}) %collective-permute-start.1) | collective-permute-done | bytes 213024 | tf_op jit(solution)/shard_map/ppermute | solution.py:407
  21.9 2.6 %shard_map.67 = (bf16[2,128,768]{2,1,0:T(8,128)(2,1)S(1)}, f32[2,16,128]{2,1,0:T(8,128)S(1)}, bf16[640,4096]{1,0:T(8,128)(2,1)S(1)}, f32[2,1,768]{2,1,0:T(1,128)...) custom-call(f32[16,128]{1,0:T(8,128)S(1)} %broadcast_in_dim.45.own_flags_ref, ...), custom_call_target="tpu_custom_call" | custom-call | bytes 1024 | tf_op jit(solution)/shard_map/pallas_call | solution.py:244
  24.5 1.6 %shard_map.70 = (f32[2,1,768]{2,1,0:T(1,128)S(1)}, f32[2,1,768]{2,1,0:T(1,128)S(1)}, f32[2,128,768]{2,1,0:T(8,128)S(1)}, bf16[256,4096]{1,0:T(8,128)(2,1)S(1)}) custom-call(f32[2,16,128]{2,1,0:T(8,128)S(1)} %get-tuple-element.35.flags_ref, ...), custom_call_target="tpu_custom_call", output_to_operand_aliasing={{0}: (3, {}), {1}: (4, {}), {2}: (5, {})} | custom-call | bytes 1024 | tf_op jit(solution)/shard_map/pallas_call | solution.py:349
  26.1 0.0 collective-permute-done.5.refs_0_
  26.1 0.0 collective-permute-done.4.refs_0_
  26.2 0.3 shard_map.72
  26.4 10.3 %all_to_all.5.parts_ref = f32[8,2,512]{2,1,0:T(2,128)S(1)} all-to-all(f32[8,2,512]{2,1,0:T(2,128)S(1)} %shard_map.72), channel_id=1, replica_groups=mesh['conv'=2,'seq'=8,'head'=2] {'seq'}, dimensions={0} | all-to-all | bytes 65536 | tf_op jit(solution)/shard_map/all_to_all | solution.py:473
  36.8 0.7 %shard_map.74 = f32[2,2048]{1,0:T(2,128)S(1)} custom-call(f32[8,2,512]{2,1,0:T(2,128)S(1)} %all_to_all.5.parts_ref, bf16[640,4096]{1,0:T(8,128)(2,1)S(1)} %get-tuple-element.50.refs_0_, bf16[256,4096]{1,0:T(8,128)(2,1)S(1)} %get-tuple-element.51.refs_1_, bf16[128,4096]{1,0:T(8,128)(2,1)S(1)} %get-tuple-element.52.refs_2_), custom_call_target="tpu_custom_call" | custom-call | bytes 1024 | tf_op jit(solution)/shard_map/pallas_call | solution.py:393
  37.4 0.0 collective-permute-start.6
  37.4 0.7 %shard_map.73 = f32[2,2048]{1,0:T(2,128)S(1)} custom-call(f32[8,2,512]{2,1,0:T(2,128)S(1)} %all_to_all.5.parts_ref, bf16[640,4096]{1,0:T(8,128)(2,1)S(1)} %get-tuple-element.50.refs_0_, bf16[256,4096]{1,0:T(8,128)(2,1)S(1)} %get-tuple-element.51.refs_1_, bf16[128,4096]{1,0:T(8,128)(2,1)S(1)} %get-tuple-element.52.refs_2_), custom_call_target="tpu_custom_call" | custom-call | bytes 1024 | tf_op jit(solution)/shard_map/pallas_call | solution.py:393
  38.1 0.5 %collective-permute-done.6 = f32[2,2048]{1,0:T(2,128)S(1)} collective-permute-done((f32[2,2048]{1,0:T(2,128)S(1)}, f32[2,2048]{1,0:T(2,128)S(1)}, u32[]{:S(2)}, u32[]{:S(2)}) %collective-permute-start.6) | collective-permute-done | bytes 16416 | tf_op jit(solution)/shard_map/ppermute | solution.py:475
  38.6 0.6 %add.10 = f32[2,2048]{1,0:T(2,128)} add(f32[2,2048]{1,0:T(2,128)S(1)} %shard_map.73, f32[2,2048]{1,0:T(2,128)S(1)} %collective-permute-done.6) | non-fusion elementwise | flops 4096 | bytes 49152 | tf_op jit(solution)/shard_map/add | solution.py:476
  (6 shorter events, 0.1 us)
Async XLA Ops:
  1.0 7.4 %collective-permute-start = (bf16[2,192,128]{2,1,0:T(8,128)(2,1)S(1)}, bf16[2,192,128]{2,1,0:T(8,128)(2,1)S(1)}, u32[]{:S(2)}, u32[]{:S(2)}) collective-permute-start(bf16[2,192,128]{2,1,0:T(8,128)(2,1)S(1)} %get-tuple-element.61), channel_id=1, source_target_pairs={{0,2},{2,0},{4,6},{6,4},{8,10},{10,8},{12,14},{14,12},{1,3},{3,1},... | collective-permute-start | bytes 294920 | tf_op jit(solution)/shard_map/ppermute | solution.py:407
  4.0 12.7 %collective-permute-start.2 = (bf16[2,192,128]{2,1,0:T(8,128)(2,1)S(1)}, bf16[2,192,128]{2,1,0:T(8,128)(2,1)S(1)}, u32[]{:S(2)}, u32[]{:S(2)}) collective-permute-start(bf16[2,192,128]{2,1,0:T(8,128)(2,1)S(1)} %get-tuple-element.62.refs_0_), channel_id=1, source_target_pairs={{0,4},{2,6},{4,8},{6,10},{8,12},{10,14},{1,5},{3,7},{5,9},{7,11},{... | collective-permute-start | bytes 294920 | tf_op jit(solution)/shard_map/ppermute | solution.py:412
  8.4 8.3 %collective-permute-start.3 = (bf16[2,192,128]{2,1,0:T(8,128)(2,1)S(1)}, bf16[2,192,128]{2,1,0:T(8,128)(2,1)S(1)}, u32[]{:S(2)}, u32[]{:S(2)}) collective-permute-start(bf16[2,192,128]{2,1,0:T(8,128)(2,1)S(1)} %shard_map.68), channel_id=1, source_target_pairs={{0,4},{2,6},{4,8},{6,10},{8,12},{10,14},{1,5},{3,7},{5,9},{7,11},{... | collective-permute-start | bytes 294920 | tf_op jit(solution)/shard_map/ppermute | solution.py:412
  14.4 11.7 %collective-permute-start.5 = (bf16[4,192,128]{2,1,0:T(8,128)(2,1)S(1)}, bf16[4,192,128]{2,1,0:T(8,128)(2,1)S(1)}, u32[]{:S(2)}, u32[]{:S(2)}) collective-permute-start(bf16[4,192,128]{2,1,0:T(8,128)(2,1)S(1)} %shard_map.64.refs_2_), channel_id=1, source_target_pairs={{0,12},{2,14},{1,13},{3,15},{16,28},{18,30},{17,29},{19,31}} | collective-permute-start | bytes 589832 | tf_op jit(solution)/shard_map/ppermute | solution.py:412
  15.7 6.2 %collective-permute-start.1 = (bf16[208,512]{1,0:T(8,128)(2,1)S(1)}, bf16[208,512]{1,0:T(8,128)(2,1)S(1)}, u32[]{:S(2)}, u32[]{:S(2)}) collective-permute-start(bf16[208,512]{1,0:T(8,128)(2,1)S(1)} %pad_maximum_fusion), channel_id=1, source_target_pairs={{0,2},{2,0},{4,6},{6,4},{8,10},{10,8},{12,14},{14,12},{1,3},{3,1},... | collective-permute-start | bytes 638984 | tf_op jit(solution)/shard_map/ppermute | solution.py:407
  16.8 9.4 %collective-permute-start.4 = (bf16[4,192,128]{2,1,0:T(8,128)(2,1)S(1)}, bf16[4,192,128]{2,1,0:T(8,128)(2,1)S(1)}, u32[]{:S(2)}, u32[]{:S(2)}) collective-permute-start(bf16[4,192,128]{2,1,0:T(8,128)(2,1)S(1)} %shard_map.69.refs_0_), channel_id=1, source_target_pairs={{4,8},{6,10},{8,12},{10,14},{5,9},{7,11},{9,13},{11,15},{20,24},{2... | collective-permute-start | bytes 589832 | tf_op jit(solution)/shard_map/ppermute | solution.py:412
  37.4 1.2 %collective-permute-start.6 = (f32[2,2048]{1,0:T(2,128)S(1)}, f32[2,2048]{1,0:T(2,128)S(1)}, u32[]{:S(2)}, u32[]{:S(2)}) collective-permute-start(f32[2,2048]{1,0:T(2,128)S(1)} %shard_map.74), channel_id=1, source_target_pairs={{0,1},{1,0},{2,3},{3,2},{4,5},{5,4},{6,7},{7,6},{8,9},{9,8},{10,11... | collective-permute-start | bytes 49160 | tf_op jit(solution)/shard_map/ppermute | solution.py:475
